TPU v7x, 128 devices: a whole 4x4x4 slice. The times are simulated.
128 devices in a mesh: dp: 64 (over y_lo, x, z, core), tensor: 2 (over y_hi).
Axes of the slice: x: 4, y: 4 (y_hi: 2, y_lo: 2; y = y_hi * 2 + y_lo), z: 4, core: 2. Of those that a mesh axis runs over, the one named last changes fastest.
Arguments:
- hidden_in: bfloat16 [32768, 1024], P(('dp', 'tensor')), may hold values from -6 to 6
- lengths: int32 [64, 4], P('dp'), may hold values from 1 to 509, as said below
- cotangent: bfloat16 [32768, 1024], P(('dp', 'tensor')), may hold values from -6 to 6
- norm_in: float32 [2, 1024], replicated, may hold values from 0.5 to 1.5
- norm_mid: float32 [2, 1024], replicated, may hold values from 0.5 to 1.5
- query_w: bfloat16 [2, 1024, 512], P(None, 'dp', 'tensor'), may hold values from -0.1875 to 0.1875
- key_w: bfloat16 [2, 1024, 512], P(None, 'dp', 'tensor'), may hold values from -0.1875 to 0.1875
- value_w: bfloat16 [2, 1024, 1024], P(None, 'dp', 'tensor'), may hold values from -0.1875 to 0.1875
- gate_w: bfloat16 [2, 1024, 1024], P(None, 'dp', 'tensor'), may hold values from -0.1875 to 0.1875
- out_w: bfloat16 [2, 1024, 1024], P(None, 'dp', 'tensor'), may hold values from -0.1875 to 0.1875
- low_down: bfloat16 [2, 1024, 16], replicated, may hold values from -0.1875 to 0.1875
- low_up: float32 [2, 16, 512], replicated, may hold values from -1.5 to 1.5
- decay_bias: float32 [2, 512], replicated, may hold values from 0 to 4
- group_gain: float32 [2, 256], replicated, may hold values from 0.1 to 1.9
- ffn_gate: bfloat16 [2, 1024, 2816], P(None, 'dp', 'tensor'), may hold values from -0.1875 to 0.1875
- ffn_up: bfloat16 [2, 1024, 2816], P(None, 'dp', 'tensor'), may hold values from -0.1875 to 0.1875
- ffn_down: bfloat16 [2, 1024, 2816], P(None, 'dp', 'tensor'), may hold values from -0.109375 to 0.109375
Outputs:
- output: float32 [32768, 1024], P(('dp', 'tensor'))
- input_grad: float32 [32768, 1024], P(('dp', 'tensor'))
- grad_norm_in: float32 [2, 1024], replicated
- grad_norm_mid: float32 [2, 1024], replicated
- grad_query_w: float32 [2, 1024, 512], P(None, 'dp', 'tensor')
- grad_key_w: float32 [2, 1024, 512], P(None, 'dp', 'tensor')
- grad_value_w: float32 [2, 1024, 1024], P(None, 'dp', 'tensor')
- grad_gate_w: float32 [2, 1024, 1024], P(None, 'dp', 'tensor')
- grad_out_w: float32 [2, 1024, 1024], P(None, 'dp', 'tensor')
- grad_low_down: float32 [2, 1024, 16], replicated
- grad_low_up: float32 [2, 16, 512], replicated
- grad_decay_bias: float32 [2, 512], replicated
- grad_group_gain: float32 [2, 256], replicated
- grad_ffn_gate: float32 [2, 1024, 2816], P(None, 'dp', 'tensor')
- grad_ffn_up: float32 [2, 1024, 2816], P(None, 'dp', 'tensor')
- grad_ffn_down: float32 [2, 1024, 2816], P(None, 'dp', 'tensor')
Inputs may be any that keep to these rules, and one draw needn't show every extreme that they name: Each slot's lengths are at least 1 and sum to between 257 and 512; some slot sums to exactly 512, and in it the last document has 509 positions; no document of a slot ends exactly at position 256, so one document covers positions 255 and 256.
All inputs are finite; a program needn't handle non-finite values.
Results may differ from a plain program's by a relative error of at most 0.035.
Values may be sent and summed in bfloat16 or wider, within the bound.
No kernel may reach another device: no remote copies, remote signals or barrier semaphores. Data moves between devices by JAX's collectives and lax.ppermute only.
A program may use at most 320 MiB of HBM per device.

v0:
```python
from functools import partial

import jax
import jax.numpy as jnp
from jax import lax
from jax.sharding import PartitionSpec as P

HEADS = 4
SPAN = 64
LAYERS = 2


highest = lax.Precision.HIGHEST
norm_eps = 1e-06
group_eps = 1.0
decay_norm = 16.0


def in_order(blocks, dim):
    lengths = list(blocks.shape[1:])
    lengths[dim] *= blocks.shape[0]
    return jnp.moveaxis(blocks, 0, dim).reshape(lengths)


def sent_to_all(x, axis):
    devices = lax.axis_size(axis)
    return lax.all_to_all(jnp.broadcast_to(x[None], (devices, *x.shape)), axis, 0, 0, tiled=True)


def collect(x, axis, dim):
    return in_order(sent_to_all(x, axis), dim)


def cut_along(x, dim, devices):
    before, after = (x.shape[:dim], x.shape[dim + 1 :])
    return jnp.moveaxis(x.reshape(*before, devices, -1, *after), dim, 0)


def sum_at_owner(x, axis, dim):
    devices = lax.axis_size(axis)
    blocks = lax.all_to_all(cut_along(x, dim, devices), axis, 0, 0, tiled=True)
    return jnp.sum(blocks.astype(jnp.float32), axis=0)


def in_one_piece(arrays, axis, dim, along):
    widths = [a.shape[along] for a in arrays]
    both = jnp.concatenate(arrays, axis=along)
    result = lax.all_gather(both, axis, axis=dim, tiled=True)
    return tuple(jnp.split(result, [sum(widths[:k]) for k in range(1, len(widths))], axis=along))


def in_one_piece_2(arrays, axis, dim, along):
    widths = [a.shape[along] for a in arrays]
    both = jnp.concatenate(arrays, axis=along)
    result = lax.psum_scatter(both, axis, scatter_dimension=dim, tiled=True)
    return tuple(jnp.split(result, [sum(widths[:k]) for k in range(1, len(widths))], axis=along))


def rms_scale(rows_in, gain):
    return (
        rows_in * lax.rsqrt(jnp.mean(rows_in * rows_in, axis=-1, keepdims=True) + norm_eps) * gain
    )


def segment_ids(lengths_row, count):
    bounds = jnp.cumsum(lengths_row)
    places = jnp.arange(count, dtype=jnp.int32)
    return jnp.sum((places[:, None] >= bounds[None, :]).astype(jnp.int32), axis=1)


def linear_mix(queries, key_rows, value_rows, log_decay, seg_ids, span_len):
    row_count, head_count, key_width = queries.shape
    value_width = value_rows.shape[2]
    blocks = row_count // span_len
    shape_keys = (blocks, span_len, head_count, key_width)
    query_b = queries.reshape(shape_keys) * key_width ** (-0.5)
    key_b = key_rows.reshape(shape_keys)
    value_b = value_rows.reshape(blocks, span_len, head_count, value_width)
    places = jnp.arange(span_len)
    lower_mask = (places[:, None] >= places[None, :]).astype(jnp.float32)
    cum_decay = jnp.einsum(
        "ts,cshd->cthd", lower_mask, log_decay.reshape(shape_keys), precision=highest
    )
    query_e = query_b * jnp.exp(cum_decay)
    key_e = key_b * jnp.exp(-cum_decay)
    seg_b = seg_ids.reshape(blocks, span_len)
    same_doc = (seg_b[:, :, None] == seg_b[:, None, :]).astype(jnp.float32) * lower_mask
    scores = jnp.einsum("cthd,cshd->chts", query_e, key_e, precision=highest) * same_doc[:, None]
    inside_part = jnp.einsum("chts,cshe->cthe", scores, value_b, precision=highest)
    last_decay = cum_decay[:, -1]
    last_seg = seg_b[:, -1]
    tail_mask = (seg_b == last_seg[:, None]).astype(jnp.float32)
    key_tail = key_b * jnp.exp(last_decay[:, None] - cum_decay) * tail_mask[:, :, None, None]
    added_state = jnp.einsum("cshd,cshe->chde", key_tail, value_b, precision=highest)
    prev_seg = jnp.concatenate([jnp.full((1,), -1, seg_b.dtype), last_seg[:-1]])
    keep_state = (prev_seg == last_seg).astype(jnp.float32)
    start_mask = (seg_b == prev_seg[:, None]).astype(jnp.float32)

    def advance(carry_state, pieces):
        query_c, added_c, decay_c, keep_c, mask_c = pieces
        from_state = (
            jnp.einsum("thd,hde->the", query_c, carry_state, precision=highest)
            * mask_c[:, None, None]
        )
        carry_state = carry_state * (keep_c * jnp.exp(decay_c))[:, :, None] + added_c
        return (carry_state, from_state)

    start_state = jnp.zeros((head_count, key_width, value_width), jnp.float32)
    _, carried = lax.scan(
        advance, start_state, (query_e, added_state, last_decay, keep_state, start_mask)
    )
    return (inside_part + carried).reshape(row_count, head_count, value_width)


def mixer_core(
    queries, key_rows, value_rows, gates, logits, group_gain, seg_ids, head_count, span_len
):
    row_count = queries.shape[0]
    key_width = queries.shape[1] // head_count
    value_width = value_rows.shape[1] // head_count
    log_decay = jax.nn.log_sigmoid(logits) / decay_norm
    mixed = linear_mix(
        queries.reshape(row_count, head_count, key_width),
        key_rows.reshape(row_count, head_count, key_width),
        value_rows.reshape(row_count, head_count, value_width),
        log_decay.reshape(row_count, head_count, key_width),
        seg_ids,
        span_len,
    )
    normed = (
        mixed * lax.rsqrt(jnp.mean(mixed * mixed, axis=-1, keepdims=True) + group_eps) * group_gain
    )
    gated = normed * jax.nn.silu(gates.reshape(row_count, head_count, value_width))
    return gated.reshape(row_count, head_count * value_width)


def swiglu(gate_pre, up_pre):
    return jax.nn.silu(gate_pre) * up_pre


def dot_rows(left, right):
    return lax.dot_general(
        left, right, (((0,), (0,)), ((), ())), preferred_element_type=jnp.float32
    )


def dot_last(left, right):
    return lax.dot_general(
        left, right, (((1,), (1,)), ((), ())), preferred_element_type=jnp.float32
    )


def exact_rows(left, right):
    return lax.dot_general(
        left, right, (((0,), (0,)), ((), ())), precision=highest, preferred_element_type=jnp.float32
    )


def exact_last(left, right):
    return lax.dot_general(
        left, right, (((1,), (1,)), ((), ())), precision=highest, preferred_element_type=jnp.float32
    )


def gather_rows(values):
    return collect(values, "tensor", 0)


def scatter_rows(terms):
    return sum_at_owner(terms.astype(jnp.bfloat16), "tensor", 0)


def gather_grads(values):
    return collect(values, "tensor", 0)


def scatter_grads(terms):
    return sum_at_owner(terms.astype(jnp.bfloat16), "tensor", 0)


def fetch_layer(mats):
    return in_one_piece(
        (mats[0], mats[1], mats[2], mats[3], mats[4], mats[5], mats[6], mats[7]), "dp", 0, 1
    )


def local(
    hidden_in,
    lengths,
    cotangent,
    norm_in,
    norm_mid,
    query_w,
    key_w,
    value_w,
    gate_w,
    out_w,
    low_down,
    low_up,
    decay_bias,
    group_gain,
    ffn_gate,
    ffn_up,
    ffn_down,
):
    half_rows = hidden_in.shape[0]
    tensor_count = lax.axis_size("tensor")
    slot_rows = half_rows * tensor_count
    tensor_pos = lax.axis_index("tensor")
    head_local = HEADS // tensor_count
    key_cols = query_w.shape[2]
    col_start = tensor_pos * key_cols
    seg_ids = segment_ids(lengths[0], slot_rows)
    valid = (seg_ids < lengths.shape[1]).astype(jnp.float32)
    valid_rows = lax.dynamic_slice_in_dim(valid, tensor_pos * half_rows, half_rows)
    stacked = (query_w, key_w, value_w, gate_w, out_w, ffn_gate, ffn_up, ffn_down)
    core = partial(mixer_core, seg_ids=seg_ids, head_count=head_local, span_len=SPAN)
    resid = hidden_in.astype(jnp.float32)
    saved = []
    for layer_index in range(LAYERS):
        mats = fetch_layer(tuple((array[layer_index] for array in stacked)))
        w_query, w_key, w_value, w_gate, w_out, w_fgate, w_fup, w_fdown = mats
        up_cols = lax.dynamic_slice_in_dim(low_up[layer_index], col_start, key_cols, 1)
        bias_cols = lax.dynamic_slice_in_dim(decay_bias[layer_index], col_start, key_cols, 0)
        normed, in_back = jax.vjp(rms_scale, resid, norm_in[layer_index])
        whole_in = gather_rows(normed.astype(jnp.bfloat16))
        queries = jnp.dot(whole_in, w_query, preferred_element_type=jnp.float32).astype(
            jnp.bfloat16
        )
        key_rows = jnp.dot(whole_in, w_key, preferred_element_type=jnp.float32).astype(jnp.bfloat16)
        value_rows = jnp.dot(whole_in, w_value, preferred_element_type=jnp.float32).astype(
            jnp.bfloat16
        )
        gates = jnp.dot(whole_in, w_gate, preferred_element_type=jnp.float32)
        latent = jnp.dot(whole_in, low_down[layer_index], preferred_element_type=jnp.float32)
        logits = (
            jnp.dot(latent, up_cols, precision=highest, preferred_element_type=jnp.float32)
            + bias_cols
        )
        mixed_rows, mix_back = jax.vjp(
            core,
            queries.astype(jnp.float32),
            key_rows.astype(jnp.float32),
            value_rows.astype(jnp.float32),
            gates,
            logits,
            group_gain[layer_index],
        )
        out_rows = mixed_rows.astype(jnp.bfloat16)
        resid_mid = resid + scatter_rows(dot_last(out_rows, w_out))
        normed_mid, mid_back = jax.vjp(rms_scale, resid_mid, norm_mid[layer_index])
        whole_mid = gather_rows(normed_mid.astype(jnp.bfloat16))
        gate_pre = jnp.dot(whole_mid, w_fgate, preferred_element_type=jnp.float32)
        up_pre = jnp.dot(whole_mid, w_fup, preferred_element_type=jnp.float32)
        acted, act_back = jax.vjp(swiglu, gate_pre, up_pre)
        acted = acted.astype(jnp.bfloat16)
        resid = resid_mid + scatter_rows(dot_last(acted, w_fdown))
        saved.append(
            (
                mats,
                in_back,
                whole_in,
                latent,
                up_cols,
                mix_back,
                out_rows,
                mid_back,
                whole_mid,
                act_back,
                acted,
            )
        )
    grad_resid = cotangent.astype(jnp.float32) * valid_rows[:, None]
    big_grads = [None] * LAYERS
    small_parts = [None] * LAYERS
    for layer_index in reversed(range(LAYERS)):
        (
            mats,
            in_back,
            whole_in,
            latent,
            up_cols,
            mix_back,
            out_rows,
            mid_back,
            whole_mid,
            act_back,
            acted,
        ) = saved[layer_index]
        w_query, w_key, w_value, w_gate, w_out, w_fgate, w_fup, w_fdown = mats
        grad_branch = gather_grads(grad_resid.astype(jnp.bfloat16))
        grad_acted = jnp.dot(grad_branch, w_fdown, preferred_element_type=jnp.float32)
        grad_fdown = dot_rows(grad_branch, acted)
        grad_gate_pre, grad_up_pre = act_back(grad_acted)
        grad_gate_pre = grad_gate_pre.astype(jnp.bfloat16)
        grad_up_pre = grad_up_pre.astype(jnp.bfloat16)
        grad_mid = dot_last(grad_gate_pre, w_fgate) + dot_last(grad_up_pre, w_fup)
        grad_fgate = dot_rows(whole_mid, grad_gate_pre)
        grad_fup = dot_rows(whole_mid, grad_up_pre)
        part_resid, grad_gain_mid = mid_back(scatter_grads(grad_mid))
        grad_resid = grad_resid + part_resid
        grad_branch = gather_grads(grad_resid.astype(jnp.bfloat16))
        grad_out_rows = jnp.dot(grad_branch, w_out, preferred_element_type=jnp.float32)
        grad_wout = dot_rows(grad_branch, out_rows)
        grad_q, grad_k, grad_v, grad_gates, grad_logits, grad_group = mix_back(grad_out_rows)
        grad_q = grad_q.astype(jnp.bfloat16)
        grad_k = grad_k.astype(jnp.bfloat16)
        grad_v = grad_v.astype(jnp.bfloat16)
        grad_gates = grad_gates.astype(jnp.bfloat16)
        grad_bias_cols = jnp.sum(grad_logits, axis=0)
        grad_up_cols = exact_rows(latent, grad_logits)
        grad_latent = exact_last(grad_logits, up_cols)
        grad_in = (
            dot_last(grad_q, w_query)
            + dot_last(grad_k, w_key)
            + dot_last(grad_v, w_value)
            + dot_last(grad_gates, w_gate)
            + exact_last(grad_latent, low_down[layer_index].astype(jnp.float32))
        )
        grad_low_rows = exact_rows(whole_in.astype(jnp.float32), grad_latent)
        grad_wq = dot_rows(whole_in, grad_q)
        grad_wk = dot_rows(whole_in, grad_k)
        grad_wv = dot_rows(whole_in, grad_v)
        grad_wg = dot_rows(whole_in, grad_gates)
        part_resid, grad_gain_in = in_back(scatter_grads(grad_in))
        grad_resid = grad_resid + part_resid
        layer_terms = (
            grad_wq,
            grad_wk,
            grad_wv,
            grad_wg,
            grad_wout,
            grad_fgate,
            grad_fup,
            grad_fdown,
        )
        big_grads[layer_index] = layer_terms
        up_full = lax.dynamic_update_slice_in_dim(
            jnp.zeros(low_up.shape[1:], jnp.float32), grad_up_cols, col_start, 1
        )
        bias_full = lax.dynamic_update_slice_in_dim(
            jnp.zeros(decay_bias.shape[1:], jnp.float32), grad_bias_cols, col_start, 0
        )
        small_parts[layer_index] = (
            grad_gain_in,
            grad_gain_mid,
            grad_low_rows,
            up_full,
            bias_full,
            grad_group,
        )
    small_sums = lax.psum(
        (
            jnp.stack([part[0] for part in small_parts]),
            jnp.stack([part[1] for part in small_parts]),
            jnp.stack([part[2] for part in small_parts]),
            jnp.stack([part[3] for part in small_parts]),
            jnp.stack([part[4] for part in small_parts]),
            jnp.stack([part[5] for part in small_parts]),
        ),
        ("dp", "tensor"),
    )
    large = [
        jnp.stack([layer_grads[position] for layer_grads in big_grads]) for position in range(8)
    ]
    large = list(
        in_one_piece_2(
            (large[0], large[1], large[2], large[3], large[4], large[5], large[6], large[7]),
            "dp",
            1,
            2,
        )
    )
    return (
        resid,
        grad_resid,
        small_sums[0],
        small_sums[1],
        large[0],
        large[1],
        large[2],
        large[3],
        large[4],
        small_sums[2],
        small_sums[3],
        small_sums[4],
        small_sums[5],
        large[5],
        large[6],
        large[7],
    )


def solution(mesh):
    in_specs = (
        P(("dp", "tensor"), None),
        P("dp", None),
        P(("dp", "tensor"), None),
        P(),
        P(),
        P(None, "dp", "tensor"),
        P(None, "dp", "tensor"),
        P(None, "dp", "tensor"),
        P(None, "dp", "tensor"),
        P(None, "dp", "tensor"),
        P(),
        P(),
        P(),
        P(),
        P(None, "dp", "tensor"),
        P(None, "dp", "tensor"),
        P(None, "dp", "tensor"),
    )
    out_specs = (
        P(("dp", "tensor"), None),
        P(("dp", "tensor"), None),
        P(),
        P(),
        P(None, "dp", "tensor"),
        P(None, "dp", "tensor"),
        P(None, "dp", "tensor"),
        P(None, "dp", "tensor"),
        P(None, "dp", "tensor"),
        P(),
        P(),
        P(),
        P(),
        P(None, "dp", "tensor"),
        P(None, "dp", "tensor"),
        P(None, "dp", "tensor"),
    )
    return jax.shard_map(local, mesh=mesh, in_specs=in_specs, out_specs=out_specs, check_vma=False)
```

profile of v0, /device:TPU:0, one launch (start us, length us, event | category | flops | bytes accessed | tf_op | source)
XLA Modules:
  0.0 1448.6 jit_solution(13842633654529853438)
XLA Ops:
  28.0 11.5 all-to-all-done
  41.8 97.5 %all-gather.3.cloned.1.call-done = bf16[1024,6272]{1,0:T(8,128)(2,1)} async-done(((bf16[16,6272]{1,0:T(8,128)(2,1)}), bf16[1024,6272]{1,0:T(8,128)(2,1)}) %all-gather.3.cloned.1.call-update) | async-done | bytes 12845072 | tf_op jit(solution)/shard_map/all_gather | solution.py:48
  157.5 48.6 %while.84 = (s32[]{:T(128)}, f32[2,128,256]{2,1,0:T(8,128)S(1)}, f32[8,64,2,256]{3,1,2,0:T(8,128)}, f32[8,2,128,256]{3,2,1,0:T(8,128)}, f32[8,64,1,1]{1,3,2,0:T(...) while((s32[]{:T(128)}, f32[2,128,256]{2,1,0:T(8,128)S(1)}, ...), condition=%wide.region_4.6_spmd.clone, body=%wide.region_3.5_spmd.clone.sunk | while | flops 50692608 | bytes 1779140 | solution.py:109
  226.2 15.5 %all-to-all-done.1 = bf16[2,256,1024]{2,1,0:T(8,128)(2,1)S(1)} async-done(((bf16[2,256,1024]{2,1,0:T(8,128)(2,1)}), bf16[2,256,1024]{2,1,0:T(8,128)(2,1)S(1)}, u32[]{:S(2)}, u32[]{:S(2)}) %all-to-all-start.1) | async-done | bytes 1048608 | tf_op jit(solution)/shard_map/all_to_all | solution.py:41
  242.8 17.4 %all_to_all.80 = bf16[2,256,1024]{2,1,0:T(8,128)(2,1)S(1)} all-to-all(bf16[2,256,1024]{2,1,0:T(8,128)(2,1)S(1)} %broadcast_in_dim.166), channel_id=1, replica_groups=mesh['dp'=64,'tensor'=2] {'tensor'}, dimensions={0} | all-to-all | bytes 2097152 | tf_op jit(solution)/shard_map/all_to_all | solution.py:27
  264.3 6.3 multiply_convert_fusion.3
  274.8 16.2 %all_to_all.81 = bf16[2,256,1024]{2,1,0:T(8,128)(2,1)S(1)} all-to-all(bf16[2,256,1024]{2,1,0:T(8,128)(2,1)S(1)} %bitcast.630), channel_id=1, replica_groups=mesh['dp'=64,'tensor'=2] {'tensor'}, dimensions={0} | all-to-all | bytes 2097152 | tf_op jit(solution)/shard_map/all_to_all | solution.py:41
  302.2 6.9 all-to-all-done.4
  340.2 55.2 %while.85 = (s32[]{:T(128)}, f32[2,128,256]{2,1,0:T(8,128)S(1)}, f32[8,64,2,256]{3,1,2,0:T(8,128)}, f32[8,2,128,256]{3,2,1,0:T(8,128)}, f32[8,64,1,1]{1,3,2,0:T(...) while((s32[]{:T(128)}, f32[2,128,256]{2,1,0:T(8,128)S(1)}, ...), condition=%wide.region_11.13_spmd.clone, body=%wide.region_10.12_spmd.clone.sunk | while | flops 50692608 | bytes 1778884 | solution.py:109
  415.7 9.9 all-to-all-done.5
  435.1 8.2 all-to-all-done.8
  444.4 15.1 %all-to-all-start.6 = ((bf16[2,256,1024]{2,1,0:T(8,128)(2,1)}), bf16[2,256,1024]{2,1,0:T(8,128)(2,1)S(1)}, u32[]{:S(2)}, u32[]{:S(2)}) async-start(bf16[2,256,1024]{2,1,0:T(8,128)(2,1)} %broadcast_in_dim.168), calls=%async_computation.6 | async-start | bytes 2097152 | tf_op jit(solution)/shard_map/all_to_all | solution.py:27
  514.0 6.3 all-to-all-done.7
  530.8 6.1 convolution_bitcast_fusion.6
  552.7 68.8 %while.86 = (s32[]{:T(128)}, f32[2,128,256]{2,1,0:T(8,128)S(1)}, f32[8,64,2,128]{3,1,2,0:T(8,128)}, f32[8,2,128,256]{3,2,1,0:T(8,128)}, f32[8,2,128]{2,1,0:T(2,1...) while((s32[]{:T(128)}, f32[2,128,256]{2,1,0:T(8,128)S(1)}, ...), condition=%wide.region_21.23_spmd.clone, body=%wide.region_19.22_spmd.clone.sunk | while | flops 101187840 | bytes 2239696 | solution.py:109
  679.7 6.4 fusion.59
  739.3 67.2 %while.87 = (s32[]{:T(128)}, f32[2,128,256]{2,1,0:T(8,128)S(1)}, f32[8,64,2,128]{3,1,2,0:T(8,128)}, f32[8,2,128,256]{3,2,1,0:T(8,128)}, f32[8,2,128]{2,1,0:T(2,1...) while((s32[]{:T(128)}, f32[2,128,256]{2,1,0:T(8,128)S(1)}, ...), condition=%wide.region_30.32_spmd.clone, body=%wide.region_28.31_spmd.clone.sunk | while | flops 101187840 | bytes 2240208 | solution.py:109
  874.0 9.4 maximum_dynamic-update-slice_fusion.2
  883.4 8.3 maximum_dynamic-update-slice_fusion.1
  891.7 9.3 maximum_dynamic-update-slice_fusion
  927.4 8.0 all-to-all-done.15
  938.7 111.8 %all-reduce.2 = (f32[2,1024]{1,0:T(2,128)}, f32[2,1024]{1,0:T(2,128)}, f32[2,512]{1,0:T(2,128)}, f32[2,256]{1,0:T(2,128)}) all-reduce(f32[2,1024]{1,0:T(2,128)S(1)} %get-tuple-element.1160, f32[2,1024]{1,0:T(2,128)S(1)} %get-tuple-element.1161, ...), channel_id=1, replica_groups=mesh['dp'=64,'tensor'=2] {'dp','tensor'}, use_global_device_ids=true, to_apply=%region_36.38 | all-reduce | flops 5632 | bytes 45056 | tf_op jit(solution)/shard_map/psum | solution.py:352
  1050.5 241.7 %reduce-scatter.2.cloned.1.call-done = f32[2,16,6272]{2,1,0:T(8,128)} async-done(((f32[2,1024,6272]{2,1,0:T(8,128)}), f32[2,16,6272]{2,1,0:T(8,128)}) %reduce-scatter.2.cloned.1.call-update) | async-done | bytes 802832 | tf_op jit(solution)/shard_map/reduce_scatter | solution.py:55
  1297.1 141.7 %all-reduce.6.cloned.1.call-done = (f32[2,1024,16]{1,2,0:T(8,128)}, f32[2,16,512]{2,1,0:T(8,128)}) async-done(((f32[2,1024,16]{1,2,0:T(8,128)}, f32[2,16,512]{2,1,0:T(8,128)}), (f32[2,1024,16]{1,2,0:T(8,128)}, f32[2,16,512]{2,1,0:T(8,128)})) %all-reduce.6.cloned.1.call-update) | async-done | bytes 196624 | tf_op jit(solution)/shard_map/psum | solution.py:352
  (823 shorter events, 677.5 us)
Async XLA Ops:
  7.2 132.1 %all-gather.3.cloned.1.call-start = ((), (), s32[]{:S(2)}) async-start(), calls=%async_computation.17 | async-start | bytes 13045760 | tf_op jit(solution)/shard_map/all_gather | solution.py:48
  14.1 282.9 %all-gather.5.cloned.1.call-start = ((), (), s32[]{:S(2)}) async-start(), calls=%async_computation.18 | async-start | bytes 13045760 | tf_op jit(solution)/shard_map/all_gather | solution.py:48
  19.8 19.6 %all-to-all-start = ((bf16[2,256,1024]{2,1,0:T(8,128)(2,1)}), bf16[2,256,1024]{2,1,0:T(8,128)(2,1)S(1)}, u32[]{:S(2)}, u32[]{:S(2)}) async-start(bf16[2,256,1024]{2,1,0:T(8,128)(2,1)} %broadcast_in_dim.165), calls=%async_computation | async-start | bytes 2097152 | tf_op jit(solution)/shard_map/all_to_all | solution.py:27
  27.1 112.1 %copy-start.91 = (f32[1,16,512]{2,1,0:T(8,128)}, f32[1,16,512]{2,1,0:T(8,128)S(1)}, u32[]{:S(2)}) copy-start(f32[1,16,512]{2,1,0:T(8,128)S(1)} %get-tuple-element.1117) | copy-start | bytes 98308
  39.4 175.7 %copy-start = (bf16[2,256,1024]{2,1,0:T(8,128)(2,1)}, bf16[2,256,1024]{2,1,0:T(8,128)(2,1)S(1)}, u32[]{:S(2)}) copy-start(bf16[2,256,1024]{2,1,0:T(8,128)(2,1)S(1)} %all-to-all-done) | copy-start | bytes 3145732
  39.8 99.4 %copy-start.87 = (f32[512,16]{0,1:T(8,128)}, f32[512,16]{0,1:T(8,128)S(1)}, u32[]{:S(2)}) copy-start(f32[512,16]{0,1:T(8,128)S(1)} %fusion.247) | copy-start | bytes 98308
  222.0 19.7 %all-to-all-start.1 = ((bf16[2,256,1024]{2,1,0:T(8,128)(2,1)}), bf16[2,256,1024]{2,1,0:T(8,128)(2,1)S(1)}, u32[]{:S(2)}, u32[]{:S(2)}) async-start(bf16[2,256,1024]{2,1,0:T(8,128)(2,1)} %bitcast.25), calls=%async_computation.1 | async-start | bytes 2097152 | tf_op jit(solution)/shard_map/all_to_all | solution.py:41
  291.4 142.4 %copy-start.2 = (f32[256,1024]{1,0:T(8,128)}, f32[256,1024]{1,0:T(8,128)S(1)}, u32[]{:S(2)}) copy-start(f32[256,1024]{1,0:T(8,128)S(1)} %get-tuple-element.1075) | copy-start | bytes 3145732
  292.7 16.4 %all-to-all-start.4 = ((bf16[2,256,1024]{2,1,0:T(8,128)(2,1)}), bf16[2,256,1024]{2,1,0:T(8,128)(2,1)S(1)}, u32[]{:S(2)}, u32[]{:S(2)}) async-start(bf16[2,256,1024]{2,1,0:T(8,128)(2,1)} %broadcast_in_dim.167), calls=%async_computation.4 | async-start | bytes 2097152 | tf_op jit(solution)/shard_map/all_to_all | solution.py:27
  409.2 16.4 %all-to-all-start.5 = ((bf16[2,256,1024]{2,1,0:T(8,128)(2,1)}), bf16[2,256,1024]{2,1,0:T(8,128)(2,1)}, u32[]{:S(2)}, u32[]{:S(2)}) async-start(bf16[2,256,1024]{2,1,0:T(8,128)(2,1)} %bitcast.627), calls=%async_computation.5 | async-start | bytes 2097152 | tf_op jit(solution)/shard_map/all_to_all | solution.py:41
  427.8 15.5 %all-to-all-start.8 = ((bf16[2,256,1024]{2,1,0:T(8,128)(2,1)}), bf16[2,256,1024]{2,1,0:T(8,128)(2,1)}, u32[]{:S(2)}, u32[]{:S(2)}) async-start(bf16[2,256,1024]{2,1,0:T(8,128)(2,1)} %broadcast_in_dim.169), calls=%async_computation.8 | async-start | bytes 2097152 | tf_op jit(solution)/shard_map/all_to_all | solution.py:27
  444.4 25.8 %all-to-all-start.6 = ((bf16[2,256,1024]{2,1,0:T(8,128)(2,1)}), bf16[2,256,1024]{2,1,0:T(8,128)(2,1)S(1)}, u32[]{:S(2)}, u32[]{:S(2)}) async-start(bf16[2,256,1024]{2,1,0:T(8,128)(2,1)} %broadcast_in_dim.168), calls=%async_computation.6 | async-start | bytes 2097152 | tf_op jit(solution)/shard_map/all_to_all | solution.py:27
  489.5 15.4 %all-to-all-start.9 = ((bf16[2,256,1024]{2,1,0:T(8,128)(2,1)}), bf16[2,256,1024]{2,1,0:T(8,128)(2,1)}, u32[]{:S(2)}, u32[]{:S(2)}) async-start(bf16[2,256,1024]{2,1,0:T(8,128)(2,1)} %bitcast.57), calls=%async_computation.9 | async-start | bytes 2097152 | tf_op jit(solution)/shard_map/all_to_all | solution.py:41
  504.9 15.4 %all-to-all-start.7 = ((bf16[2,256,1024]{2,1,0:T(8,128)(2,1)}), bf16[2,256,1024]{2,1,0:T(8,128)(2,1)}, u32[]{:S(2)}, u32[]{:S(2)}) async-start(bf16[2,256,1024]{2,1,0:T(8,128)(2,1)} %bitcast.626), calls=%async_computation.7 | async-start | bytes 2097152 | tf_op jit(solution)/shard_map/all_to_all | solution.py:41
  526.3 15.4 %all-to-all-start.10 = ((bf16[2,256,1024]{2,1,0:T(8,128)(2,1)}), bf16[2,256,1024]{2,1,0:T(8,128)(2,1)}, u32[]{:S(2)}, u32[]{:S(2)}) async-start(bf16[2,256,1024]{2,1,0:T(8,128)(2,1)} %broadcast_in_dim.171), calls=%async_computation.10 | async-start | bytes 2097152 | tf_op jit(solution)/shard_map/all_to_all | solution.py:27
  552.7 68.8 %copy-start.7 = (f32[8,64,2,128]{3,1,2,0:T(8,128)S(1)}, f32[8,64,2,128]{3,1,2,0:T(8,128)}, u32[]{:S(2)}) copy-start(f32[8,64,2,128]{3,1,2,0:T(8,128)} %copy-done.6) | copy-start | bytes 1572868
  643.9 15.4 %all-to-all-start.11 = ((bf16[2,256,1024]{2,1,0:T(8,128)(2,1)}), bf16[2,256,1024]{2,1,0:T(8,128)(2,1)}, u32[]{:S(2)}, u32[]{:S(2)}) async-start(bf16[2,256,1024]{2,1,0:T(8,128)(2,1)} %bitcast.75), calls=%async_computation.11 | async-start | bytes 2097152 | tf_op jit(solution)/shard_map/all_to_all | solution.py:41
  664.3 15.4 %all-to-all-start.12 = ((bf16[2,256,1024]{2,1,0:T(8,128)(2,1)}), bf16[2,256,1024]{2,1,0:T(8,128)(2,1)}, u32[]{:S(2)}, u32[]{:S(2)}) async-start(bf16[2,256,1024]{2,1,0:T(8,128)(2,1)} %broadcast_in_dim.175), calls=%async_computation.12 | async-start | bytes 2097152 | tf_op jit(solution)/shard_map/all_to_all | solution.py:27
  695.4 15.7 %all-to-all-start.13 = ((bf16[2,256,1024]{2,1,0:T(8,128)(2,1)}), bf16[2,256,1024]{2,1,0:T(8,128)(2,1)}, u32[]{:S(2)}, u32[]{:S(2)}) async-start(bf16[2,256,1024]{2,1,0:T(8,128)(2,1)} %bitcast.628), calls=%async_computation.13 | async-start | bytes 2097152 | tf_op jit(solution)/shard_map/all_to_all | solution.py:41
  716.2 15.1 %all-to-all-start.14 = ((bf16[2,256,1024]{2,1,0:T(8,128)(2,1)}), bf16[2,256,1024]{2,1,0:T(8,128)(2,1)S(1)}, u32[]{:S(2)}, u32[]{:S(2)}) async-start(bf16[2,256,1024]{2,1,0:T(8,128)(2,1)} %broadcast_in_dim.177), calls=%async_computation.14 | async-start | bytes 2097152 | tf_op jit(solution)/shard_map/all_to_all | solution.py:27
  719.8 572.5 %reduce-scatter.2.cloned.1.call-start = ((), (), s32[]{:S(2)}) async-start(), calls=%async_computation.19 | async-start | bytes 52183040 | tf_op jit(solution)/shard_map/reduce_scatter | solution.py:55
  739.3 67.2 %copy-start.9 = (f32[8,64,2,128]{3,2,1,0:T(2,128)S(1)}, f32[8,64,2,128]{3,2,1,0:T(2,128)}, u32[]{:S(2)}) copy-start(f32[8,64,2,128]{3,2,1,0:T(2,128)} %copy-done.8) | copy-start | bytes 1572868
  919.5 15.9 %all-to-all-start.15 = ((bf16[2,256,1024]{2,1,0:T(8,128)(2,1)}), bf16[2,256,1024]{2,1,0:T(8,128)(2,1)}, u32[]{:S(2)}, u32[]{:S(2)}) async-start(bf16[2,256,1024]{2,1,0:T(8,128)(2,1)} %bitcast.608), calls=%async_computation.15 | async-start | bytes 2097152 | tf_op jit(solution)/shard_map/all_to_all | solution.py:41
  924.4 514.5 %all-reduce.6.cloned.1.call-start = ((), (), s32[]{:S(2)}) async-start(), calls=%async_computation.20 | async-start | bytes 393216 | tf_op jit(solution)/shard_map/psum | solution.py:352
  (139 other events, 1001.3 us)
Sparse Core Ops, SparseCore 0:
  14.2 125.0 all-gather.2
  140.9 122.1 all-gather.4
  901.2 391.0 reduce-scatter.1
  1298.2 140.6 all-reduce.5
where the time goes:
time: 1460 us; the launch traced here: 1450 us
  waiting for transfers between devices  565 us (39%)
  matrix products  290 us (20%)
  local copies, waits for them, and re-layouts  184 us (13%)
  other arithmetic  175 us (12%)
  blocking collectives  145 us (10%)
  starting transfers between devices  71.7 us (5%)
  between operations  15.9 us (1%)
    reduce_scatter x1, waiting for transfers between devices, in_one_piece_2(): result = lax.psum_scatter(both, axis, scatter_dimension=dim, tiled=True)  242 us
    psum x1, waiting for transfers between devices, local(): lax.psum((jnp.stack([part[0] for part in small_parts]), jnp.stack([part[1...  142 us
    psum x1, blocking collectives, local(): lax.psum((jnp.stack([part[0] for part in small_parts]), jnp.stack([part[1...  112 us
    all_gather x2, waiting for transfers between devices, in_one_piece(): result = lax.all_gather(both, axis, axis=dim, tiled=True)  97.5 us
    dot_general x48, matrix products, advance(): jnp.einsum('thd,hde->the', query_c, carry_state, precision=highest)  76 us
    dynamic_update_slice x80, other arithmetic, linear_mix(): lax.scan(advance, start_state, (query_e, added_state, last_decay, keep_st...  65.7 us
    dot_general x16, matrix products, dot_rows(): lax.dot_general(left, right, (((0,), (0,)), ((), ())), preferred_element_...  52.1 us
    dot_general x16, matrix products, dot_last(): lax.dot_general(left, right, (((1,), (1,)), ((), ())), preferred_element_...  47.9 us
  transfers between devices with their start and end apart: 18, of which 16 were waited for; matrix products, arithmetic and copies ran while one was open for 15% of the time, Pallas kernels for 0%

commit v1 on v0

v1 whole, which is shorter than its diff:
```python
from functools import partial

import jax
import jax.numpy as jnp
from jax import lax
from jax.experimental import pallas as pl
from jax.experimental.pallas import tpu as pltpu
from jax.sharding import Mesh, PartitionSpec as P

LAYERS = 2
HEADS = 4
SPAN = 64
ROWS = 256
D = 1024
KD = 128
VD = 256
FINE = ("yl", "x", "z", "c", "yh")
PLANE = {"x": ("yh", "yl", "z"), "y": ("x", "z"), "z": ("yh", "yl", "x")}
GROUPS = ("x", "z", "y")
bf = jnp.bfloat16
f32 = jnp.float32
highest = lax.Precision.HIGHEST
norm_eps = 1e-06
group_eps = 1.0
decay_norm = 16.0
scale = KD**-0.5
NN = (((1,), (0,)), ((), ()))
NT = (((1,), (1,)), ((), ()))
TN = (((0,), (0,)), ((), ()))


def dot(a, b, dims=NN, precision=None):
    return lax.dot_general(a, b, dims, precision=precision, preferred_element_type=f32)


def call(kernel, out_shape, *, flops=0, moved=0, vmem=48, **kw):
    return pl.pallas_call(
        kernel,
        out_shape=out_shape,
        compiler_params=pltpu.CompilerParams(vmem_limit_bytes=vmem << 20),
        cost_estimate=pl.CostEstimate(flops=flops, bytes_accessed=moved, transcendentals=0),
        **kw,
    )


def shape(*dims, dtype=f32):
    return jax.ShapeDtypeStruct(dims, dtype)


def swap(a):
    return lax.ppermute(a, "c", [(0, 1), (1, 0)])


def ring(a, axis):
    if axis == "y":
        names = ("yl", "c", "yh")
        place = lambda i, c: ((i % 2) * 2 + c) * 2 + i // 2
    else:
        names = (axis, "c")
        place = lambda i, c: i * 2 + c
    pairs = [
        (place(i, c), place((i + 1 - 2 * c) % 4, c)) for i in range(4) for c in range(2)
    ]
    return lax.ppermute(a, names, pairs)


def plane_gather(s, axis):
    b = jnp.broadcast_to(s[None], (16, *s.shape))
    return lax.all_to_all(b, PLANE[axis], 0, 0, tiled=True)


def plane_sum(t, axis):
    r = lax.all_to_all(t, PLANE[axis], 0, 0, tiled=True)
    return jnp.sum(r.astype(f32), axis=0)


def axis_gather(p, axis):
    b0 = jnp.stack([p, swap(p)])
    t1 = ring(b0, axis)
    t2 = ring(t1[0], axis)
    lead = (256,) if axis == "y" else (2, 128)
    pieces = (b0, t1, swap(t1), t2, swap(t2))
    return tuple(a.reshape(*((2,) if a.ndim == 4 else ()), *lead, a.shape[-1]) for a in pieces)


def axis_sum(parts, axis):
    u1, u2, u0 = (a.reshape(*a.shape[: a.ndim - (2 if axis == "y" else 3)], 16, 16, a.shape[-1]) for a in parts)
    r2 = ring(u2, axis)
    u1 = jnp.stack([(u1[0].astype(f32) + r2.astype(f32)).astype(bf), u1[1]])
    r1 = ring(u1, axis)
    far = swap(r1[1])
    return (u0.astype(f32) + r1[0].astype(f32) + far.astype(f32)).astype(bf)


def rows_of(refs, pick):
    b0, t1, t1p, t2, t2p = refs
    return jnp.concatenate(
        [pick(b0, 0), pick(b0, 1), pick(t1, 0), pick(t1, 1), pick(t1p, 0), pick(t1p, 1), pick(t2, None), pick(t2p, None)],
        axis=0,
    )


def half_of(ref, part):
    return ref[0] if part is None else ref[part, 0]


def half_specs(width):
    two = pl.BlockSpec((2, 1, 128, width), lambda h: (0, h, 0, 0))
    one = pl.BlockSpec((1, 128, width), lambda h: (h, 0, 0))
    return [two, two, two, one, one]


def whole(*dims):
    return pl.BlockSpec(dims, lambda h: (0,) * len(dims))


def per_half(*dims):
    return pl.BlockSpec((1, *dims), lambda h: (h,) + (0,) * len(dims))


def proj_kernel(x, *refs):
    out = refs[5]
    out[0] = dot(x[...], rows_of(refs[:5], half_of)).astype(out.dtype)


def proj(x, pieces):
    n = pieces[0].shape[-1]
    return call(
        proj_kernel,
        shape(2, ROWS, n, dtype=bf),
        grid=(2,),
        in_specs=[whole(ROWS, D)] + half_specs(n),
        out_specs=per_half(ROWS, n),
        flops=4 * ROWS * D * n,
        moved=4 * D * n,
    )(x, *pieces)


def ffn_kernel(hx, hz, *refs):
    gate = dot(hx[...], rows_of(refs[:5], half_of))
    up = dot(hz[...], rows_of(refs[5:10], half_of))
    gate_out, up_out, acted = refs[10:]
    gate_out[0] = gate.astype(bf)
    up_out[0] = up.astype(bf)
    acted[0] = (gate * jax.nn.sigmoid(gate) * up).astype(bf)


def ffn(hx, hz, px, pz):
    n = px[0].shape[-1]
    return call(
        ffn_kernel,
        (shape(2, ROWS, n, dtype=bf),) * 3,
        grid=(2,),
        in_specs=[whole(ROWS, D)] * 2 + half_specs(n) * 2,
        out_specs=[per_half(ROWS, n)] * 3,
        flops=8 * ROWS * D * n,
        moved=8 * D * n,
    )(hx, hz, *px, *pz)


def spread(value, perm):
    high = value.astype(bf)
    low = (value - high.astype(f32)).astype(bf)
    return dot(high, perm) + dot(low, perm)


def rms(v, gain):
    return v * lax.rsqrt(jnp.mean(v * v, axis=-1, keepdims=True) + norm_eps) * gain


def y_out_kernel(normed, where_, src, x, gain, py, px, pz, *refs):
    b0, t1, t1p, t2, t2p = refs[:5]
    outs = refs[5:]
    h, h1 = where_[0], where_[1]
    own, far = src[h], src[1 - h]
    one, two = src[h1], src[1 - h1]
    d0 = dot(own, b0[0], NT) + dot(far, t2[...], NT)
    d1 = dot(own, b0[1], NT) + dot(far, t2p[...], NT)
    d2 = dot(one, t1[0], NT) + dot(two, t1p[1], NT)
    d3 = dot(one, t1[1], NT) + dot(two, t1p[0], NT)
    total = x[...] + spread(jnp.concatenate([d0, d1, d2, d3], axis=1), py[...])
    outs[0][...] = total
    if normed:
        hn = rms(total, gain[...]).astype(bf)
        outs[1][...] = hn
        outs[2][...] = dot(hn, px[...], NT).astype(bf)
        outs[3][...] = dot(hn, pz[...], NT).astype(bf)


def y_out(where_, src, x, gain, perms, pieces, normed=True):
    n = pieces[0].shape[-1]
    vm = pl.BlockSpec(memory_space=pltpu.VMEM)
    outs = (shape(ROWS, D),) + ((shape(ROWS, D, dtype=bf),) * 3 if normed else ())
    return call(
        partial(y_out_kernel, normed),
        outs,
        in_specs=[pl.BlockSpec(memory_space=pltpu.SMEM)] + [vm] * (len(pieces) + 6),
        out_specs=tuple([vm] * len(outs)),
        flops=4 * ROWS * D * n + 8 * ROWS * D * D,
        moved=4 * D * n + 8 * D * D,
    )(where_, src, x, gain, perms["y"], perms["x"], perms["z"], *pieces)


def norm_kernel(x, gain, px, pz, hn_out, hx, hz):
    hn = rms(x[...], gain[...]).astype(bf)
    hn_out[...] = hn
    hx[...] = dot(hn, px[...], NT).astype(bf)
    hz[...] = dot(hn, pz[...], NT).astype(bf)


def norm_rows(x, gain, perms):
    return call(
        norm_kernel,
        (shape(ROWS, D, dtype=bf),) * 3,
        flops=4 * ROWS * D * D,
        moved=6 * D * D,
    )(x, gain, perms["x"], perms["z"])


def y_back_kernel(acting, where_, g, py, *refs):
    b0, t1, t1p, t2, t2p = refs[:5]
    h, h1 = where_[0], where_[1]
    same = h == h1
    gy = dot(g[...].astype(bf), py[...], NT).astype(bf)
    near, far = gy[:, :512], gy[:, 512:]
    joined = lambda a, b: jnp.concatenate([a, b], axis=0)
    part_a = dot(near, joined(b0[0], b0[1]))
    part_b = dot(near, joined(t2[...], t2p[...]))
    part_c = dot(far, joined(t1[0], t1[1]))
    part_d = dot(far, joined(t1p[1], t1p[0]))
    pick_c = jnp.where(same, 1.0, 0.0)
    pick_d = 1.0 - pick_c
    halves = (
        (h, part_a + pick_c * part_c + pick_d * part_d),
        (1 - h, part_b + pick_d * part_c + pick_c * part_d),
    )
    if acting:
        gate_in, up_in, gy_out, dgate, dup = refs[5:]
        gy_out[...] = gy
        for place, da in halves:
            gate = gate_in[place].astype(f32)
            up = up_in[place].astype(f32)
            sg = jax.nn.sigmoid(gate)
            dgate[place] = (da * up * sg * (1.0 + gate * (1.0 - sg))).astype(bf)
            dup[place] = (da * gate * sg).astype(bf)
    else:
        gy_out, out = refs[5:]
        gy_out[...] = gy
        for place, da in halves:
            out[place] = da


def y_back(where_, g, perms, pieces, saved=None):
    n = pieces[0].shape[-1]
    vm = pl.BlockSpec(memory_space=pltpu.VMEM)
    extra = () if saved is None else tuple(saved)
    outs = (shape(ROWS, D, dtype=bf),)
    outs += (shape(2, ROWS, n),) if saved is None else (shape(2, ROWS, n, dtype=bf),) * 2
    return call(
        partial(y_back_kernel, saved is not None),
        outs,
        in_specs=[pl.BlockSpec(memory_space=pltpu.SMEM)] + [vm] * (7 + len(extra)),
        out_specs=tuple([vm] * len(outs)),
        flops=4 * ROWS * D * n + 2 * ROWS * D * D,
        moved=4 * D * n + 2 * D * D,
    )(where_, g, perms["y"], *pieces, *extra)


def norm_back(v, gain, d_out):
    r = lax.rsqrt(jnp.mean(v * v, axis=-1, keepdims=True) + norm_eps)
    u = d_out * gain
    d_v = r * u - v * (r * r * r) * jnp.mean(u * v, axis=-1, keepdims=True)
    return d_v, jnp.sum(d_out * v * r, axis=0, keepdims=True)


def x_back_kernel(low, dx, dz, x, gain, g, px, pz, *refs):
    h = pl.program_id(0)
    rest = refs[10:]
    if low:
        d_logits, low_up, low_down = rest[:3]
        rest = rest[3:]
    g_out, gain_out = rest[:2]
    acc_x, acc_z = rest[-2:]
    part_x = dot(dx[0], rows_of(refs[:5], half_of), NT)
    part_z = dot(dz[0], rows_of(refs[5:10], half_of), NT)

    @pl.when(h == 0)
    def _():
        acc_x[...] = part_x
        acc_z[...] = part_z

    @pl.when(h == 1)
    def _():
        d_hn = spread(acc_x[...] + part_x, px[...]) + spread(acc_z[...] + part_z, pz[...])
        if low:
            d_latent = dot(d_logits[...], low_up[...], NT, highest)
            rest[2][...] = d_latent
            d_hn = d_hn + dot(d_latent, low_down[...], NT, highest)
        d_v, d_gain = norm_back(x[...], gain[...], d_hn)
        g_out[...] = g[...] + d_v
        gain_out[...] = d_gain


def x_back(dx, dz, x, gain, g, perms, px, pz, low=None):
    n = px[0].shape[-1]
    outs = (shape(ROWS, D), shape(1, D))
    out_specs = [whole(ROWS, D), whole(1, D)]
    extra, extra_specs = (), []
    if low is not None:
        extra = tuple(low)
        extra_specs = [whole(*a.shape) for a in low]
        outs += (shape(ROWS, 16),)
        out_specs.append(whole(ROWS, 16))
    return call(
        partial(x_back_kernel, low is not None),
        outs,
        grid=(2,),
        in_specs=[per_half(ROWS, n)] * 2
        + [whole(ROWS, D), whole(1, D), whole(ROWS, D), whole(D, D), whole(D, D)]
        + half_specs(n) * 2
        + extra_specs,
        out_specs=out_specs,
        scratch_shapes=[pltpu.VMEM((ROWS, D), f32)] * 2,
        flops=8 * ROWS * D * n + 8 * ROWS * D * D,
        moved=8 * D * n + 4 * D * D,
    )(dx, dz, x, gain, g, perms["x"], perms["z"], *px, *pz, *extra)


def x_weight_kernel(a, ar, d, dr, u1, u2, u0):
    r = (dot(a[...], d[0], TN) + dot(ar[...], dr[0], TN)).astype(bf)
    u1[0, 0] = r[:128]
    u1[1, 0] = r[128:256]
    u2[0] = r[256:384]
    u0[0] = r[384:]


def cols(a, *blocks, width=128):
    return jnp.concatenate([a[:, b * width : (b + 1) * width] for b in blocks], axis=1)


def x_weight(hx, hx_far, d, d_far):
    n = d.shape[-1]
    one = per_half(128, n)
    return call(
        x_weight_kernel,
        (shape(2, 2, 128, n, dtype=bf), shape(2, 128, n, dtype=bf), shape(2, 128, n, dtype=bf)),
        grid=(2,),
        in_specs=[whole(ROWS, 512)] * 2 + [per_half(ROWS, n)] * 2,
        out_specs=[pl.BlockSpec((2, 1, 128, n), lambda h: (0, h, 0, 0)), one, one],
        flops=4 * ROWS * D * n,
        moved=2 * D * n,
    )(hx, hx_far, d, d_far)


def y_weight_kernel(where_, a, ar, d, dr, u1, u2, u0):
    h, h2 = where_[0], 1 - where_[1]
    first = lambda place: dot(a[:, :256], d[place], TN) + dot(ar[:, :256], dr[place], TN)
    u0[...] = first(h).astype(bf)
    u2[...] = first(1 - h).astype(bf)
    r = dot(a[:, 256:], d[h2], TN) + dot(ar[:, 256:], dr[h2], TN)
    u1[0] = r[:256].astype(bf)
    u1[1] = r[256:].astype(bf)


def y_weight(where_, gy, gy_far, d, d_far):
    n = d.shape[-1]
    vm = pl.BlockSpec(memory_space=pltpu.VMEM)
    return call(
        y_weight_kernel,
        (shape(2, 256, n, dtype=bf), shape(256, n, dtype=bf), shape(256, n, dtype=bf)),
        in_specs=[pl.BlockSpec(memory_space=pltpu.SMEM)] + [vm] * 4,
        out_specs=(vm, vm, vm),
        flops=4 * ROWS * D * n,
        moved=2 * D * n,
    )(where_, gy, gy_far, d, d_far)


def log_sigmoid(v):
    return jnp.minimum(v, 0.0) - jnp.log1p(jnp.exp(-jnp.abs(v)))


def decays(logits):
    ld = log_sigmoid(logits) / decay_norm
    r = lax.broadcasted_iota(jnp.int32, (ROWS, ROWS), 0)
    c = lax.broadcasted_iota(jnp.int32, (ROWS, ROWS), 1)
    lower = ((r >= c) & (r // SPAN == c // SPAN)).astype(f32)
    cum = dot(lower, ld, NN, highest)
    blocks = [cum[i * SPAN : (i + 1) * SPAN] for i in range(4)]
    ends = [b[SPAN - 1 :] for b in blocks]
    return blocks, ends


def run_sum(ends, start, stop):
    total = jnp.zeros_like(ends[0])
    for i in range(start, stop):
        total = total + ends[i]
    return total


def key_factors(blocks, ends, i):
    parts = [jnp.exp((ends[j] - blocks[j]) + run_sum(ends, j + 1, i)) for j in range(i)]
    parts.append(jnp.exp(-blocks[i]))
    return jnp.concatenate(parts, axis=0)


def allowed(segr, segc, i):
    rows_i = segr[i * SPAN : (i + 1) * SPAN]
    count = (i + 1) * SPAN
    r = lax.broadcasted_iota(jnp.int32, (SPAN, count), 0) + i * SPAN
    c = lax.broadcasted_iota(jnp.int32, (SPAN, count), 1)
    return (r >= c) & (rows_i == segc[:, :count])


def start_factors(blocks, ends):
    return jnp.concatenate([jnp.exp(blocks[i] + run_sum(ends, 0, i)) for i in range(4)], axis=0)


def tail_factors(blocks, ends):
    return jnp.concatenate([jnp.exp((ends[i] - blocks[i]) + run_sum(ends, i + 1, 4)) for i in range(4)], axis=0)


def mix_kernel(q, k, v, logits, segr, segc, out, state, state_q):
    blocks, ends = decays(logits[...])
    kf = k[0].astype(f32)
    qf = q[0].astype(f32) * scale
    segr, segc = segr[...], segc[...]
    tail = tail_factors(blocks, ends)
    tail_k = jnp.where(segr == segr[ROWS - 1 :], kf * tail, 0.0).astype(bf)
    state[0] = dot(tail_k, v[0], TN).astype(bf)
    state_q[0] = jnp.where(segr == segr[:1], qf * start_factors(blocks, ends), 0.0).astype(bf)
    for i in range(4):
        count = (i + 1) * SPAN
        qe = (qf[i * SPAN : count] * jnp.exp(blocks[i])).astype(bf)
        ke = (kf[:count] * key_factors(blocks, ends, i)).astype(bf)
        p = jnp.where(allowed(segr, segc, i), dot(qe, ke, NT), 0.0).astype(bf)
        out[0, i * SPAN : count] = dot(p, v[0, :count])


def head_cols(width, first=0):
    return pl.BlockSpec((1, ROWS, width), lambda t: (t // 2, 0, first + t % 2))


def by_head(*dims):
    return pl.BlockSpec((1, *dims), lambda t: (t,) + (0,) * len(dims))


def mix(qv, kg, logits, segr, segc):
    return call(
        mix_kernel,
        (
            shape(2, ROWS, 2 * VD),
            shape(HEADS, KD, VD, dtype=bf),
            shape(HEADS, ROWS, KD, dtype=bf),
        ),
        grid=(HEADS,),
        in_specs=[
            head_cols(KD),
            head_cols(KD),
            head_cols(VD, 1),
            pl.BlockSpec((ROWS, KD), lambda t: (0, t)),
            whole(ROWS, 1),
            whole(1, ROWS),
        ],
        out_specs=[head_cols(VD), by_head(KD, VD), by_head(ROWS, KD)],
        flops=HEADS * 120_000_000,
        moved=4_000_000,
    )(qv, kg, qv, logits, segr, segc)


def gate_kernel(local, state_q, state, g, gain, mixed_out, rows):
    mixed = local[0] + dot(state_q[0], state[0])
    mixed_out[0] = mixed
    gate = g[0].astype(f32)
    on = mixed * lax.rsqrt(jnp.mean(mixed * mixed, axis=-1, keepdims=True) + group_eps) * gain[...]
    rows[0] = (on * gate * jax.nn.sigmoid(gate)).astype(bf)


def gate_rows(local, state_q, state, kg, gain):
    return call(
        gate_kernel,
        (shape(2, ROWS, 2 * VD), shape(2, ROWS, 2 * VD, dtype=bf)),
        grid=(HEADS,),
        in_specs=[head_cols(VD), by_head(ROWS, KD), by_head(KD, VD), head_cols(VD, 1), whole(1, VD)],
        out_specs=[head_cols(VD), head_cols(VD)],
        flops=HEADS * 20_000_000,
        moved=3_000_000,
    )(local, state_q, state, kg, gain)


def mix_back_kernel(
    d_rows, mixed_in, g, gain_in, q, k, v, logits, segr, segc, state_in, state_q_in,
    dg_out, dgain, d_state, dq_out, dk_out, dv_out, net_out,
):
    mixed = mixed_in[0]
    gate = g[0].astype(f32)
    gain = gain_in[...]
    rho = lax.rsqrt(jnp.mean(mixed * mixed, axis=-1, keepdims=True) + group_eps)
    ng = mixed * rho
    sg = jax.nn.sigmoid(gate)
    dr = d_rows[0]
    d_on = dr * gate * sg
    dg_out[0] = (dr * ng * gain * sg * (1.0 + gate * (1.0 - sg))).astype(bf)
    dgain[0] = jnp.sum(d_on * ng, axis=0, keepdims=True)
    w = d_on * gain
    do = (rho * (w - ng * jnp.mean(w * ng, axis=-1, keepdims=True))).astype(bf)

    blocks, ends = decays(logits[...])
    kf = k[0].astype(f32)
    qf = q[0].astype(f32) * scale
    segr, segc = segr[...], segc[...]
    sq = state_q_in[0]
    d_state[0] = dot(sq, do, TN).astype(bf)
    from_state = dot(do, state_in[0], NT)
    start = jnp.where(segr == segr[:1], start_factors(blocks, ends), 0.0) * scale
    dq_state = from_state * start
    net_state = from_state * sq.astype(f32)
    dk = jnp.zeros((ROWS, KD), f32)
    dv = jnp.zeros((ROWS, VD), f32)
    net_k = jnp.zeros((ROWS, KD), f32)
    nets = []
    grow = lambda a: a if a.shape[0] == ROWS else jnp.concatenate(
        [a, jnp.zeros((ROWS - a.shape[0], a.shape[1]), f32)], axis=0
    )
    for i in range(4):
        count = (i + 1) * SPAN
        here = slice(i * SPAN, count)
        eb = jnp.exp(blocks[i])
        qe = (qf[here] * eb).astype(bf)
        factors = key_factors(blocks, ends, i)
        ke = (kf[:count] * factors).astype(bf)
        keep = allowed(segr, segc, i)
        p = jnp.where(keep, dot(qe, ke, NT), 0.0).astype(bf)
        dp = jnp.where(keep, dot(do[here], v[0, :count], NT), 0.0).astype(bf)
        dv = dv + grow(dot(p, do[here], TN))
        dqe = dot(dp, ke)
        dq_out[0, here] = (dqe * eb * scale + dq_state[here]).astype(bf)
        nets.append(dqe * qe.astype(f32) + net_state[here])
        dke = dot(dp, qe, TN)
        dk = dk + grow(dke * factors)
        net_k = net_k + grow(dke * ke.astype(f32))
    dk_out[0] = dk
    dv_out[0] = dv
    net_out[0] = jnp.concatenate(nets, axis=0) - net_k


def mix_back(d_rows, mixed, qv, kg, gain, logits, segr, segc, state, state_q):
    return call(
        mix_back_kernel,
        (
            shape(2, ROWS, 2 * VD, dtype=bf),
            shape(HEADS, 1, VD),
            shape(HEADS, KD, VD, dtype=bf),
            shape(2, ROWS, 2 * KD, dtype=bf),
            shape(HEADS, ROWS, KD),
            shape(HEADS, ROWS, VD),
            shape(HEADS, ROWS, KD),
        ),
        grid=(HEADS,),
        in_specs=[
            head_cols(VD),
            head_cols(VD),
            head_cols(VD, 1),
            whole(1, VD),
            head_cols(KD),
            head_cols(KD),
            head_cols(VD, 1),
            pl.BlockSpec((ROWS, KD), lambda t: (0, t)),
            whole(ROWS, 1),
            whole(1, ROWS),
            by_head(KD, VD),
            by_head(ROWS, KD),
        ],
        out_specs=[
            head_cols(VD),
            by_head(1, VD),
            by_head(KD, VD),
            head_cols(KD),
            by_head(ROWS, KD),
            by_head(ROWS, VD),
            by_head(ROWS, KD),
        ],
        flops=HEADS * 300_000_000,
        moved=8_000_000,
    )(d_rows, mixed, kg, gain, qv, kg, qv, logits, segr, segc, state, state_q)


def decay_back_kernel(dk_in, dv_in, net, k, v, logits_in, segr, segc, d_state, dk_out, dv_out, d_logits):
    logits = logits_in[...]
    blocks, ends = decays(logits)
    segr, segc = segr[...], segc[...]
    kf = k[0].astype(f32)
    tail = jnp.where(segr == segr[ROWS - 1 :], tail_factors(blocks, ends), 0.0)
    tail_k = (kf * tail).astype(bf)
    ds = d_state[0]
    back = dot(v[0], ds, NT)
    dk_out[0] = (dk_in[0] + back * tail).astype(bf)
    dv_out[0] = (dv_in[0] + dot(tail_k, ds)).astype(bf)
    r = lax.broadcasted_iota(jnp.int32, (ROWS, ROWS), 0)
    c = lax.broadcasted_iota(jnp.int32, (ROWS, ROWS), 1)
    same = segr == segc
    after = jnp.where(same & (c >= r), 1.0, 0.0)
    before = jnp.where(same & (c < r), 1.0, 0.0)
    d_ld = dot(after, net[0], NN, highest) + dot(before, back * tail_k.astype(f32), NN, highest)
    d_logits[...] = d_ld * jax.nn.sigmoid(-logits) / decay_norm


def decay_back(dk, dv, net, qv, kg, logits, segr, segc, d_state):
    return call(
        decay_back_kernel,
        (
            shape(2, ROWS, 2 * KD, dtype=bf),
            shape(2, ROWS, 2 * VD, dtype=bf),
            shape(ROWS, HEADS * KD),
        ),
        grid=(HEADS,),
        in_specs=[
            by_head(ROWS, KD),
            by_head(ROWS, VD),
            by_head(ROWS, KD),
            head_cols(KD),
            head_cols(VD, 1),
            pl.BlockSpec((ROWS, KD), lambda t: (0, t)),
            whole(ROWS, 1),
            whole(1, ROWS),
            by_head(KD, VD),
        ],
        out_specs=[head_cols(KD), head_cols(VD), pl.BlockSpec((ROWS, KD), lambda t: (0, t))],
        flops=HEADS * 100_000_000,
        moved=4_000_000,
    )(dk, dv, net, kg, qv, logits, segr, segc, d_state)


def one_hot(places):
    return (places[:, None] == jnp.arange(D, dtype=jnp.int32)[None, :]).astype(bf)


def permutations():
    yl, x, z, c, yh = (lax.axis_index(a) for a in FINE)
    k = jnp.arange(D, dtype=jnp.int32)
    s = 1 - 2 * c
    step = lambda a: jnp.stack([a, a, a - s, a - s, a + s, a + s, a + 2, a + 2]) % 4
    core = jnp.stack([c, 1 - c, c, 1 - c, 1 - c, c, c, 1 - c])
    pick = lambda table, b: jnp.sum(jnp.where(b[:, None] == jnp.arange(table.shape[0])[None], table[None], 0), axis=1)
    block, r = k // 128, k % 128
    low_y, low_a, rr = r // 64, (r // 16) % 4, r % 16
    index = lambda yl, x, z, c: ((yl * 4 + x) * 4 + z) * 32 + c * 16 + rr
    perms = {
        "x": one_hot(index(low_y, pick(step(x), block), low_a, pick(core, block))),
        "z": one_hot(index(low_y, low_a, pick(step(z), block), pick(core, block))),
    }
    block, r = k // 256, k % 256
    perms["y"] = one_hot(
        index(
            pick(jnp.stack([yl, yl, 1 - yl, 1 - yl]), block),
            r // 64,
            (r // 16) % 4,
            pick(jnp.stack([c, 1 - c, c, 1 - c]), block),
        )
    )
    before = (yh * 2 + yl - s) % 4
    return perms, jnp.stack([yh, before // 2]).astype(jnp.int32)


def local(
    hidden_in, lengths, cotangent, norm_in, norm_mid, query_w, key_w, value_w, gate_w, out_w,
    low_down, low_up, decay_bias, group_gain, ffn_gate, ffn_up, ffn_down,
):
    yh = lax.axis_index("yh")
    perms, where_ = permutations()
    bounds = jnp.cumsum(lengths[0])
    places = jnp.arange(ROWS, dtype=jnp.int32) + yh * ROWS
    seg = jnp.sum((places[:, None] >= bounds[None, :]).astype(jnp.int32), axis=1)
    valid = (seg < lengths.shape[1]).astype(f32)
    segr, segc = seg[:, None], seg[None, :]

    shards = []
    for layer in range(LAYERS):
        shards.append(
            {
                "x": jnp.concatenate([query_w[layer], value_w[layer], ffn_gate[layer]], axis=1),
                "z": jnp.concatenate([key_w[layer], gate_w[layer], ffn_up[layer]], axis=1),
                "y": jnp.concatenate([out_w[layer], ffn_down[layer]], axis=1),
            }
        )
    attn_width = {"x": 768, "z": 768, "y": 512}
    weights = []
    for layer in range(LAYERS):
        planes = {a: plane_gather(shards[layer][a], a) for a in GROUPS}
        attn = {a: axis_gather(planes[a][..., : attn_width[a]], a) for a in GROUPS}
        feed = {a: axis_gather(planes[a][..., attn_width[a] :], a) for a in GROUPS}
        weights.append((attn, feed))

    x = hidden_in.astype(f32)
    hn, hnx, hnz = norm_rows(x, norm_in[:1], perms)
    saved = []
    for layer in range(LAYERS):
        attn, feed = weights[layer]
        qv = proj(hnx, attn["x"])
        kg = proj(hnz, attn["z"])
        latent = dot(hn, low_down[layer])
        logits = dot(latent, low_up[layer], NN, highest) + decay_bias[layer]
        local_mix, state, state_q = mix(qv, kg, logits, segr, segc)
        state = lax.ppermute(state, "yh", [(0, 1)])
        mixed, rows = gate_rows(local_mix, state_q, state, kg, group_gain[layer][None])
        x_mid, hm, hmx, hmz = y_out(where_, rows, x, norm_mid[layer : layer + 1], perms, attn["y"])
        gate_pre, up_pre, acted = ffn(hmx, hmz, feed["x"], feed["z"])
        saved.append((x, hn, hnx, hnz, qv, kg, latent, logits, state, state_q, mixed, rows, x_mid, hmx, hmz, gate_pre, up_pre, acted))
        if layer + 1 < LAYERS:
            x, hn, hnx, hnz = y_out(where_, acted, x_mid, norm_in[layer + 1 : layer + 2], perms, feed["y"])
        else:
            (x,) = y_out(where_, acted, x_mid, norm_in[:1], perms, feed["y"], normed=False)
    output = x

    g = cotangent.astype(f32) * valid[:, None]
    large = [None] * LAYERS
    small = [None] * LAYERS
    for layer in reversed(range(LAYERS)):
        attn, feed = weights[layer]
        x, hn, hnx, hnz, qv, kg, latent, logits, state, state_q, mixed, rows, x_mid, hmx, hmz, gate_pre, up_pre, acted = saved[layer]
        gb, d_gate, d_up = y_back(where_, g, perms, feed["y"], (gate_pre, up_pre))
        g_mid, grad_mid = x_back(d_gate, d_up, x_mid, norm_mid[layer : layer + 1], g, perms, feed["x"], feed["z"])
        mine, theirs = (5, 4, 6, 0), (3, 2, 7, 1)
        y_mine = lambda a: cols(a, 0, 2, 3, width=256)
        y_theirs = lambda a: swap(cols(a, 1, 3, 2, width=256))
        sums = {}
        u = y_weight(where_, y_mine(gb), y_theirs(gb), acted, swap(acted))
        sums["fd"] = axis_sum(u, "y")
        u = x_weight(cols(hmx, *mine), swap(cols(hmx, *theirs)), d_gate, swap(d_gate))
        sums["fg"] = axis_sum(u, "x")
        u = x_weight(cols(hmz, *mine), swap(cols(hmz, *theirs)), d_up, swap(d_up))
        sums["fu"] = axis_sum(u, "z")

        gm, d_rows = y_back(where_, g_mid, perms, attn["y"])
        u = y_weight(where_, y_mine(gm), y_theirs(gm), rows, swap(rows))
        sums["o"] = axis_sum(u, "y")
        d_g, d_gain, d_state, d_q, d_k, d_v, net = mix_back(
            d_rows, mixed, qv, kg, group_gain[layer][None], logits, segr, segc, state, state_q
        )
        d_state = lax.ppermute(d_state, "yh", [(1, 0)])
        d_k, d_v, d_logits = decay_back(d_k, d_v, net, qv, kg, logits, segr, segc, d_state)
        d_qv = jnp.concatenate([d_q, d_v], axis=2)
        d_kg = jnp.concatenate([d_k, d_g], axis=2)
        g, grad_in, d_latent = x_back(
            d_qv, d_kg, x, norm_in[layer : layer + 1], g_mid, perms, attn["x"], attn["z"],
            (d_logits, low_up[layer], low_down[layer].astype(f32)),
        )
        u = x_weight(cols(hnx, *mine), swap(cols(hnx, *theirs)), d_qv, swap(d_qv))
        sums["qv"] = axis_sum(u, "x")
        u = x_weight(cols(hnz, *mine), swap(cols(hnz, *theirs)), d_kg, swap(d_kg))
        sums["kg"] = axis_sum(u, "z")
        large[layer] = {
            "x": (plane_sum(sums["qv"], "x"), plane_sum(sums["fg"], "x")),
            "z": (plane_sum(sums["kg"], "z"), plane_sum(sums["fu"], "z")),
            "y": (plane_sum(sums["o"], "y"), plane_sum(sums["fd"], "y")),
        }
        small[layer] = (
            grad_in[0],
            grad_mid[0],
            dot(hn.astype(f32), d_latent, TN, highest),
            dot(latent, d_logits, TN, highest),
            jnp.sum(d_logits, axis=0),
            jnp.sum(d_gain[:, 0], axis=0),
        )
    input_grad = g

    stacked = [jnp.stack([part[i] for part in small]) for i in range(6)]
    flat = jnp.concatenate([a.reshape(-1) for a in stacked])
    flat = jnp.pad(flat, (0, 128 * 512 - flat.shape[0])).reshape(128, 4, 128)
    part = jnp.sum(lax.all_to_all(flat, FINE, 0, 0, tiled=True), axis=0)
    total = lax.all_to_all(jnp.broadcast_to(part[None], (128, 4, 128)), FINE, 0, 0, tiled=True).reshape(-1)
    small_sums, at = [], 0
    for a in stacked:
        small_sums.append(total[at : at + a.size].reshape(a.shape))
        at += a.size

    both = lambda group, i, lo, hi: jnp.stack([large[l][group][i][:, lo:hi] for l in range(LAYERS)])
    return (
        output,
        input_grad,
        small_sums[0],
        small_sums[1],
        both("x", 0, 0, 256),
        both("z", 0, 0, 256),
        both("x", 0, 256, 768),
        both("z", 0, 256, 768),
        both("y", 0, 0, 512),
        small_sums[2],
        small_sums[3],
        small_sums[4],
        small_sums[5],
        both("x", 1, 0, 1408),
        both("z", 1, 0, 1408),
        both("y", 1, 0, 1408),
    )


def solution(mesh):
    fine = Mesh(mesh.devices.reshape(2, 4, 4, 2, 2), FINE)
    dp = ("yl", "x", "z", "c")
    every = P(FINE, None)
    mat = P(None, dp, "yh")
    rep = P()
    in_specs = (every, P(dp, None), every, rep, rep) + (mat,) * 5 + (rep,) * 4 + (mat,) * 3
    out_specs = (every, every, rep, rep) + (mat,) * 5 + (rep,) * 4 + (mat,) * 3
    return jax.shard_map(local, mesh=fine, in_specs=in_specs, out_specs=out_specs, check_vma=False)
```

time: 1460 us -> 901 us (0.62)
  waiting for transfers between devices: 565 us -> 225 us
  matrix products: 290 us -> 6.54 us
  Pallas kernels: 0 us -> 201 us
  blocking collectives: 145 us -> 0 us
  starting transfers between devices: 71.7 us -> 180 us
  other arithmetic: 175 us -> 125 us
  local copies, waits for them, and re-layouts: 184 us -> 143 us
    dot_general x130 -> x8, matrix products: 290 us -> 6.54 us  [dot(): lax.dot_general(a, b, dims, precision=precision, preferred_element_type=f32)]
    reduce_scatter x1 -> x0, waiting for transfers between devices: 242 us -> none  [in_one_piece_2(): result = lax.psum_scatter(both, axis, scatter_dimension=dim, tiled=True)]
    pallas_call x0 -> x39, Pallas kernels: none -> 201 us  [the longest x4 43.8 us: x_back(): call(partial(x_back_kernel, low is not None), outs, grid=(2,), in_specs=[...]
    psum x1 -> x0, waiting for transfers between devices: 142 us -> none  [local(): lax.psum((jnp.stack([part[0] for part in small_parts]), jnp.stack([part[1...]
    psum x1 -> x0, blocking collectives: 112 us -> none  [local(): lax.psum((jnp.stack([part[0] for part in small_parts]), jnp.stack([part[1...]
    all_gather x2 -> x0, waiting for transfers between devices: 97.5 us -> none  [in_one_piece(): result = lax.all_gather(both, axis, axis=dim, tiled=True)]
    ppermute x0 -> x124, starting transfers between devices: none -> 82.2 us  [the longest x48 46.1 us: ring(): return lax.ppermute(a, names, pairs)]
    ppermute x0 -> x124, waiting for transfers between devices: none -> 74.7 us  [the longest x48 58.4 us: ring(): return lax.ppermute(a, names, pairs)]
  transfers between devices with their start and end apart: 18 -> 144, of which waited for: 16 -> 36; matrix products, arithmetic and copies ran while one was open for 15% -> 26% of each run, Pallas kernels for 0% -> 23%
where the time goes in v1:
time: 901 us; the launch traced here: 886 us
  waiting for transfers between devices  225 us (25%)
  Pallas kernels  201 us (22%)
  starting transfers between devices  180 us (20%)
  local copies, waits for them, and re-layouts  143 us (16%)
  other arithmetic  125 us (14%)
    all_to_all x12, waiting for transfers between devices, plane_sum(): r = lax.all_to_all(t, PLANE[axis], 0, 0, tiled=True)  88.5 us
    ppermute x48, waiting for transfers between devices, ring(): return lax.ppermute(a, names, pairs)  58.4 us
    all_to_all x6, waiting for transfers between devices, plane_gather(): return lax.all_to_all(b, PLANE[axis], 0, 0, tiled=True)  57.4 us
    all_to_all x12, starting transfers between devices, plane_sum(): r = lax.all_to_all(t, PLANE[axis], 0, 0, tiled=True)  52.4 us
    unnamed x599, local copies, waits for them, and re-layouts  46.5 us
    ppermute x48, starting transfers between devices, ring(): return lax.ppermute(a, names, pairs)  46.1 us
    pallas_call x4, Pallas kernels, x_back(): call(partial(x_back_kernel, low is not None), outs, grid=(2,), in_specs=[...  43.8 us
    all_to_all x6, starting transfers between devices, plane_gather(): return lax.all_to_all(b, PLANE[axis], 0, 0, tiled=True)  33.6 us
  transfers between devices with their start and end apart: 144, of which 36 were waited for; matrix products, arithmetic and copies ran while one was open for 26% of the time, Pallas kernels for 23%

profile of v1, /device:TPU:0, one launch (start us, length us, event | category | flops | bytes accessed | tf_op | source)
XLA Modules:
  0.0 886.3 jit_solution(5129261469917879147)
XLA Ops:
  4.4 8.0 all-to-all-start.2
  47.7 13.7 %all-to-all-done.5 = bf16[16,16,1920]{2,1,0:T(8,128)(2,1)S(1)} async-done(((bf16[16,16,1920]{2,1,0:T(8,128)(2,1)}), bf16[16,16,1920]{2,1,0:T(8,128)(2,1)S(1)}, u32[]{:S(2)}, u32[]{:S(2)}) %all-to-all-start.5) | async-done | bytes 983072 | tf_op jit(solution)/shard_map/all_to_all | solution.py:69
  68.8 15.6 %all-to-all-done.1 = bf16[16,16,2176]{2,1,0:T(8,128)(2,1)S(1)} async-done(((bf16[16,16,2176]{2,1,0:T(8,128)(2,1)}), bf16[16,16,2176]{2,1,0:T(8,128)(2,1)S(1)}, u32[]{:S(2)}, u32[]{:S(2)}) %all-to-all-start.1) | async-done | bytes 1114144 | tf_op jit(solution)/shard_map/all_to_all | solution.py:69
  96.3 9.1 %all-to-all-done = bf16[16,16,2176]{2,1,0:T(8,128)(2,1)} async-done(((bf16[16,16,2176]{2,1,0:T(8,128)(2,1)}), bf16[16,16,2176]{2,1,0:T(8,128)(2,1)}, u32[]{:S(2)}, u32[]{:S(2)}) %all-to-all-start) | async-done | bytes 1114144 | tf_op jit(solution)/shard_map/all_to_all | solution.py:69
  116.9 9.4 %all-to-all-done.3 = bf16[16,16,2176]{2,1,0:T(8,128)(2,1)} async-done(((bf16[16,16,2176]{2,1,0:T(8,128)(2,1)}), bf16[16,16,2176]{2,1,0:T(8,128)(2,1)}, u32[]{:S(2)}, u32[]{:S(2)}) %all-to-all-start.3) | async-done | bytes 1114144 | tf_op jit(solution)/shard_map/all_to_all | solution.py:69
  137.2 9.7 %all-to-all-done.4 = bf16[16,16,2176]{2,1,0:T(8,128)(2,1)} async-done(((bf16[16,16,2176]{2,1,0:T(8,128)(2,1)}), bf16[16,16,2176]{2,1,0:T(8,128)(2,1)}, u32[]{:S(2)}, u32[]{:S(2)}) %all-to-all-start.4) | async-done | bytes 1114144 | tf_op jit(solution)/shard_map/all_to_all | solution.py:69
  220.4 8.5 collective-permute-done.14
  239.8 19.5 %collective-permute-done.39 = bf16[16,16,768]{2,1,0:T(8,128)(2,1)S(1)} collective-permute-done((bf16[16,16,768]{2,1,0:T(8,128)(2,1)}, bf16[16,16,768]{2,1,0:T(8,128)(2,1)S(1)}, u32[]{:S(2)}, u32[]{:S(2)}) %collective-permute-start.39) | collective-permute-done | bytes 393248 | tf_op jit(solution)/shard_map/ppermute | solution.py:64
  307.6 9.1 %shard_map.295 = (f32[256,1024]{1,0:T(8,128)S(1)}, bf16[256,1024]{1,0:T(8,128)(2,1)S(1)}, bf16[256,1024]{1,0:T(8,128)(2,1)S(1)}, bf16[256,1024]{1,0:T(8,128)(2,1)S(1)}) custom-call(s32[2]{0:T(128)S(1)} %pad_add_fusion.where_, bf16[2,256,1408]{2,1,0:T(8,128)(2,1)} %get-tuple-element.130.src.d, f32[256,1024]{1,0:T(8,128)S(1)} %get-tuple-element.131.x, ...), custom_call_target="tpu_custom_call" | custom-call | flops 3623878656 | bytes 14155776 | tf_op jit(solution)/shard_map/pallas_call | solution.py:194
  363.3 7.6 shard_map.303
  373.7 10.6 %shard_map.304 = (f32[256,1024]{1,0:T(8,128)S(1)}, f32[1,1024]{1,0:T(1,128)S(1)}) custom-call(bf16[2,256,1408]{2,1,0:T(8,128)(2,1)} %copy-done.87, bf16[2,256,1408]{2,1,0:T(8,128)(2,1)} %copy-done.89, f32[256,1024]{1,0:T(8,128)S(1)} %get-tuple-element.143.x, f32[1,1024]{1,0:T(1,128)S(1)} %copy-done.174, f32[256,1024]{1,0:T(8,128)S(1)} %copy-done.3, ...), custom_call_target="tpu_custom_call" | custom-call | flops 5100273664 | bytes 15728640 | tf_op jit(solution)/shard_map/pallas_call | solution.py:314
  388.8 9.3 %shard_map.306 = (bf16[2,256,512]{2,1,0:T(8,128)(2,1)S(1)}, f32[4,1,256]{2,1,0:T(1,128)S(1)}, bf16[4,128,256]{2,1,0:T(8,128)(2,1)}, bf16[2,256,256]{2,1,0:T(8,12...) custom-call(f32[2,256,512]{2,1,0:T(8,128)} %copy-done.113, ...), custom_call_target="tpu_custom_call" | custom-call | flops 1200000000 | bytes 8000000 | tf_op jit(solution)/shard_map/pallas_call | solution.py:547
  417.5 7.8 shard_map.302
  435.4 11.3 %shard_map.308 = (f32[256,1024]{1,0:T(8,128)}, f32[1,1024]{1,0:T(1,128)S(1)}, f32[256,16]{1,0:T(8,128)S(1)}) custom-call(bf16[2,256,768]{2,1,0:T(8,128)(2,1)S(1)} %constant_dynamic-update-slice_fusion.dx.d, bf16[2,256,768]{2,1,0:T(8,128)(2,1)S(1)} %constant_dynamic-update-slice_fusion.2.dz.d, f32[256,1024]{1,0:T(8,128)} %copy-done.26, ...), custom_call_target="tpu_custom_call" | custom-call | flops 3758096384 | bytes 10485760 | tf_op jit(solution)/shard_map/pallas_call | solution.py:314
  449.3 7.7 shard_map.309
  460.1 10.6 %shard_map.310 = (f32[256,1024]{1,0:T(8,128)S(1)}, f32[1,1024]{1,0:T(1,128)S(1)}) custom-call(bf16[2,256,1408]{2,1,0:T(8,128)(2,1)} %copy-done.91, bf16[2,256,1408]{2,1,0:T(8,128)(2,1)} %copy-done.93, f32[256,1024]{1,0:T(8,128)S(1)} %copy-done.25, f32[1,1024]{1,0:T(1,128)S(1)} %get-tuple-element.430.gain, f32[256,1024]{1,0:T(8,128)S(1)} %copy-done.28, ...), custom_call_target="tpu_custom_call" | custom-call | flops 5100273664 | bytes 15728640 | tf_op jit(solution)/shard_map/pallas_call | solution.py:314
  475.8 8.7 shard_map.312
  506.2 8.4 collective-permute-done.63.d_state
  528.0 11.2 %shard_map.314 = (f32[256,1024]{1,0:T(8,128)}, f32[1,1024]{1,0:T(1,128)S(1)}, f32[256,16]{1,0:T(8,128)S(1)}) custom-call(bf16[2,256,768]{2,1,0:T(8,128)(2,1)S(1)} %constant_dynamic-update-slice_fusion.4.dx.d, bf16[2,256,768]{2,1,0:T(8,128)(2,1)S(1)} %constant_dynamic-update-slice_fusion.6.dz.d, f32[256,1024]{1,0:T(8,128)} %copy-done.1, ...), custom_call_target="tpu_custom_call" | custom-call | flops 3758096384 | bytes 10485760 | tf_op jit(solution)/shard_map/pallas_call | solution.py:314
  726.0 13.6 %all-to-all-done.11 = bf16[16,16,768]{2,1,0:T(8,128)(2,1)S(1)} async-done(((bf16[16,16,768]{2,1,0:T(8,128)(2,1)}), bf16[16,16,768]{2,1,0:T(8,128)(2,1)S(1)}, u32[]{:S(2)}, u32[]{:S(2)}) %all-to-all-start.11) | async-done | bytes 393248 | tf_op jit(solution)/shard_map/all_to_all | solution.py:73
  758.0 9.3 %all-to-all-done.10 = bf16[16,16,768]{2,1,0:T(8,128)(2,1)S(1)} async-done(((bf16[16,16,768]{2,1,0:T(8,128)(2,1)}), bf16[16,16,768]{2,1,0:T(8,128)(2,1)S(1)}, u32[]{:S(2)}, u32[]{:S(2)}) %all-to-all-start.10) | async-done | bytes 393248 | tf_op jit(solution)/shard_map/all_to_all | solution.py:73
  772.2 7.7 all-to-all-done.8
  797.9 11.2 %all-to-all-done.18 = bf16[16,16,1408]{2,1,0:T(8,128)(2,1)S(1)} async-done(((bf16[16,16,1408]{2,1,0:T(8,128)(2,1)}), bf16[16,16,1408]{2,1,0:T(8,128)(2,1)S(1)}, u32[]{:S(2)}, u32[]{:S(2)}) %all-to-all-start.18) | async-done | bytes 720928 | tf_op jit(solution)/shard_map/all_to_all | solution.py:73
  876.6 8.4 all-to-all-done.14
  (1165 shorter events, 635.4 us)
Async XLA Ops:
  91.6 58.7 %collective-permute-start.11 = (bf16[16,16,512]{2,1,0:T(8,128)(2,1)S(1)}, bf16[16,16,512]{2,1,0:T(8,128)(2,1)}, u32[]{:S(2)}, u32[]{:S(2)}) collective-permute-start(bf16[16,16,512]{2,1,0:T(8,128)(2,1)S(1)} %get-tuple-element.314), channel_id=1, source_target_pairs={{0,2},{2,0},{1,3},{3,1},{4,6},{6,4},{5,7},{7,5},{8,10},{10,8},{9,1... | collective-permute-start | bytes 786440 | tf_op jit(solution)/shard_map/ppermute | solution.py:51
  94.0 66.4 %collective-permute-start.26 = (bf16[16,16,1408]{2,1,0:T(8,128)(2,1)}, bf16[16,16,1408]{2,1,0:T(8,128)(2,1)}, u32[]{:S(2)}, u32[]{:S(2)}) collective-permute-start(bf16[16,16,1408]{2,1,0:T(8,128)(2,1)} %get-tuple-element.312), channel_id=1, source_target_pairs={{0,2},{2,0},{1,3},{3,1},{4,6},{6,4},{5,7},{7,5},{8,10},{10,8},{9,1... | collective-permute-start | bytes 2162696 | tf_op jit(solution)/shard_map/ppermute | solution.py:51
  96.3 56.2 %collective-permute-start.42 = (bf16[16,16,512]{2,1,0:T(8,128)(2,1)}, bf16[16,16,512]{2,1,0:T(8,128)(2,1)}, u32[]{:S(2)}, u32[]{:S(2)}) collective-permute-start(bf16[16,16,512]{2,1,0:T(8,128)(2,1)} %get-tuple-element.310), channel_id=1, source_target_pairs={{0,2},{2,0},{1,3},{3,1},{4,6},{6,4},{5,7},{7,5},{8,10},{10,8},{9,1... | collective-permute-start | bytes 786440 | tf_op jit(solution)/shard_map/ppermute | solution.py:51
  113.2 53.4 %collective-permute-start.57 = (bf16[16,16,1408]{2,1,0:T(8,128)(2,1)}, bf16[16,16,1408]{2,1,0:T(8,128)(2,1)}, u32[]{:S(2)}, u32[]{:S(2)}) collective-permute-start(bf16[16,16,1408]{2,1,0:T(8,128)(2,1)} %get-tuple-element.308), channel_id=1, source_target_pairs={{0,2},{2,0},{1,3},{3,1},{4,6},{6,4},{5,7},{7,5},{8,10},{10,8},{9,1... | collective-permute-start | bytes 2162696 | tf_op jit(solution)/shard_map/ppermute | solution.py:51
  114.0 41.2 %collective-permute-start.5 = (bf16[16,16,768]{2,1,0:T(8,128)(2,1)S(1)}, bf16[16,16,768]{2,1,0:T(8,128)(2,1)}, u32[]{:S(2)}, u32[]{:S(2)}) collective-permute-start(bf16[16,16,768]{2,1,0:T(8,128)(2,1)S(1)} %get-tuple-element.304), channel_id=1, source_target_pairs={{0,2},{2,0},{1,3},{3,1},{4,6},{6,4},{5,7},{7,5},{8,10},{10,8},{9,1... | collective-permute-start | bytes 1179656 | tf_op jit(solution)/shard_map/ppermute | solution.py:51
  219.1 40.3 %collective-permute-start.22 = (bf16[2,16,16,1408]{3,2,1,0:T(8,128)(2,1)}, bf16[2,16,16,1408]{3,2,1,0:T(8,128)(2,1)}, u32[]{:S(2)}, u32[]{:S(2)}) collective-permute-start(bf16[2,16,16,1408]{3,2,1,0:T(8,128)(2,1)} %pad_maximum_fusion.3), channel_id=1, source_target_pairs={{0,4},{2,14},{4,8},{6,2},{8,12},{10,6},{12,0},{14,10},{1,5},{3,15}... | collective-permute-start | bytes 4325384 | tf_op jit(solution)/shard_map/ppermute | solution.py:64
  231.7 35.6 %collective-permute-start.48 = (bf16[2,16,16,1408]{3,2,1,0:T(8,128)(2,1)}, bf16[2,16,16,1408]{3,2,1,0:T(8,128)(2,1)S(1)}, u32[]{:S(2)}, u32[]{:S(2)}) collective-permute-start(bf16[2,16,16,1408]{3,2,1,0:T(8,128)(2,1)} %pad_maximum_fusion.7), channel_id=1, source_target_pairs={{0,16},{2,50},{16,32},{18,2},{32,48},{34,18},{48,0},{50,34},{1,17}... | collective-permute-start | bytes 4325384 | tf_op jit(solution)/shard_map/ppermute | solution.py:64
  234.5 34.0 %collective-permute-start.53 = (bf16[2,16,16,1408]{3,2,1,0:T(8,128)(2,1)S(1)}, bf16[2,16,16,1408]{3,2,1,0:T(8,128)(2,1)}, u32[]{:S(2)}, u32[]{:S(2)}) collective-permute-start(bf16[2,16,16,1408]{3,2,1,0:T(8,128)(2,1)S(1)} %copy-done.229), channel_id=1, source_target_pairs={{0,4},{2,14},{4,8},{6,2},{8,12},{10,6},{12,0},{14,10},{1,5},{3,15}... | collective-permute-start | bytes 4325384 | tf_op jit(solution)/shard_map/ppermute | solution.py:64
  353.4 196.4 %collective-permute-start.85 = (bf16[2,256,512]{2,1,0:T(8,128)(2,1)}, bf16[2,256,512]{2,1,0:T(8,128)(2,1)}, u32[]{:S(2)}, u32[]{:S(2)}) collective-permute-start(bf16[2,256,512]{2,1,0:T(8,128)(2,1)} %get-tuple-element.127.src.d), channel_id=1, source_target_pairs={{0,2},{2,0},{1,3},{3,1},{4,6},{6,4},{5,7},{7,5},{8,10},{10,8},{9,1... | collective-permute-start | bytes 1572872 | tf_op jit(solution)/shard_map/ppermute | solution.py:51
  354.0 243.7 %collective-permute-start.115 = (bf16[2,256,1408]{2,1,0:T(8,128)(2,1)}, bf16[2,256,1408]{2,1,0:T(8,128)(2,1)}, u32[]{:S(2)}, u32[]{:S(2)}) collective-permute-start(bf16[2,256,1408]{2,1,0:T(8,128)(2,1)} %get-tuple-element.130.src.d), channel_id=1, source_target_pairs={{0,2},{2,0},{1,3},{3,1},{4,6},{6,4},{5,7},{7,5},{8,10},{10,8},{9,1... | collective-permute-start | bytes 4325384 | tf_op jit(solution)/shard_map/ppermute | solution.py:51
  354.5 234.0 %collective-permute-start.79 = (bf16[256,512]{1,0:T(8,128)(2,1)}, bf16[256,512]{1,0:T(8,128)(2,1)}, u32[]{:S(2)}, u32[]{:S(2)}) collective-permute-start(bf16[256,512]{1,0:T(8,128)(2,1)} %pad_maximum_fusion.51), channel_id=1, source_target_pairs={{0,2},{2,0},{1,3},{3,1},{4,6},{6,4},{5,7},{7,5},{8,10},{10,8},{9,1... | collective-permute-start | bytes 786440 | tf_op jit(solution)/shard_map/ppermute | solution.py:51
  388.5 113.3 %collective-permute-start.90 = (bf16[2,256,512]{2,1,0:T(8,128)(2,1)}, bf16[2,256,512]{2,1,0:T(8,128)(2,1)}, u32[]{:S(2)}, u32[]{:S(2)}) collective-permute-start(bf16[2,256,512]{2,1,0:T(8,128)(2,1)} %get-tuple-element.138.src.d), channel_id=1, source_target_pairs={{0,2},{2,0},{1,3},{3,1},{4,6},{6,4},{5,7},{7,5},{8,10},{10,8},{9,1... | collective-permute-start | bytes 1572872 | tf_op jit(solution)/shard_map/ppermute | solution.py:51
  425.3 76.2 %collective-permute-start.89 = (bf16[256,768]{1,0:T(8,128)(2,1)}, bf16[256,768]{1,0:T(8,128)(2,1)}, u32[]{:S(2)}, u32[]{:S(2)}) collective-permute-start(bf16[256,768]{1,0:T(8,128)(2,1)} %pad_maximum_fusion.39), channel_id=1, source_target_pairs={{0,2},{2,0},{1,3},{3,1},{4,6},{6,4},{5,7},{7,5},{8,10},{10,8},{9,1... | collective-permute-start | bytes 1179656 | tf_op jit(solution)/shard_map/ppermute | solution.py:51
  501.6 90.3 %collective-permute-start.69 = (bf16[256,512]{1,0:T(8,128)(2,1)}, bf16[256,512]{1,0:T(8,128)(2,1)}, u32[]{:S(2)}, u32[]{:S(2)}) collective-permute-start(bf16[256,512]{1,0:T(8,128)(2,1)} %pad_maximum_fusion.47), channel_id=1, source_target_pairs={{0,2},{2,0},{1,3},{3,1},{4,6},{6,4},{5,7},{7,5},{8,10},{10,8},{9,1... | collective-permute-start | bytes 786440 | tf_op jit(solution)/shard_map/ppermute | solution.py:51
  514.7 35.3 %collective-permute-start.84 = (bf16[256,768]{1,0:T(8,128)(2,1)}, bf16[256,768]{1,0:T(8,128)(2,1)}, u32[]{:S(2)}, u32[]{:S(2)}) collective-permute-start(bf16[256,768]{1,0:T(8,128)(2,1)} %pad_maximum_fusion.37), channel_id=1, source_target_pairs={{0,2},{2,0},{1,3},{3,1},{4,6},{6,4},{5,7},{7,5},{8,10},{10,8},{9,1... | collective-permute-start | bytes 1179656 | tf_op jit(solution)/shard_map/ppermute | solution.py:51
  549.9 39.0 %collective-permute-start.80 = (bf16[2,256,768]{2,1,0:T(8,128)(2,1)S(1)}, bf16[2,256,768]{2,1,0:T(8,128)(2,1)}, u32[]{:S(2)}, u32[]{:S(2)}) collective-permute-start(bf16[2,256,768]{2,1,0:T(8,128)(2,1)S(1)} %copy-done.104), channel_id=1, source_target_pairs={{0,2},{2,0},{1,3},{3,1},{4,6},{6,4},{5,7},{7,5},{8,10},{10,8},{9,1... | collective-permute-start | bytes 2359304 | tf_op jit(solution)/shard_map/ppermute | solution.py:51
  639.5 37.9 %collective-permute-start.116 = (bf16[16,16,1408]{2,1,0:T(8,128)(2,1)}, bf16[16,16,1408]{2,1,0:T(8,128)(2,1)}, u32[]{:S(2)}, u32[]{:S(2)}) collective-permute-start(bf16[16,16,1408]{2,1,0:T(8,128)(2,1)} %bitcast.243), channel_id=1, source_target_pairs={{0,64},{2,67},{64,1},{66,2},{1,65},{3,66},{65,0},{67,3},{4,68},{6,... | collective-permute-start | bytes 2162696 | tf_op jit(solution)/shard_map/ppermute | solution.py:64
  699.1 80.9 %collective-permute-start.117 = (bf16[2,16,16,1408]{3,2,1,0:T(8,128)(2,1)}, bf16[2,16,16,1408]{3,2,1,0:T(8,128)(2,1)}, u32[]{:S(2)}, u32[]{:S(2)}) collective-permute-start(bf16[2,16,16,1408]{3,2,1,0:T(8,128)(2,1)} %pad_maximum_fusion.16), channel_id=1, source_target_pairs={{0,64},{2,67},{64,1},{66,2},{1,65},{3,66},{65,0},{67,3},{4,68},{6,... | collective-permute-start | bytes 4325384 | tf_op jit(solution)/shard_map/ppermute | solution.py:64
  701.7 80.2 %collective-permute-start.122 = (bf16[2,16,16,1408]{3,2,1,0:T(8,128)(2,1)}, bf16[2,16,16,1408]{3,2,1,0:T(8,128)(2,1)}, u32[]{:S(2)}, u32[]{:S(2)}) collective-permute-start(bf16[2,16,16,1408]{3,2,1,0:T(8,128)(2,1)} %pad_maximum_fusion.17), channel_id=1, source_target_pairs={{0,64},{2,67},{64,1},{66,2},{1,65},{3,66},{65,0},{67,3},{4,68},{6,... | collective-permute-start | bytes 4325384 | tf_op jit(solution)/shard_map/ppermute | solution.py:64
  703.6 79.6 %collective-permute-start.112 = (bf16[2,16,16,1408]{3,2,1,0:T(8,128)(2,1)}, bf16[2,16,16,1408]{3,2,1,0:T(8,128)(2,1)}, u32[]{:S(2)}, u32[]{:S(2)}) collective-permute-start(bf16[2,16,16,1408]{3,2,1,0:T(8,128)(2,1)} %pad_maximum_fusion.15), channel_id=1, source_target_pairs={{0,4},{2,14},{4,8},{6,2},{8,12},{10,6},{12,0},{14,10},{1,5},{3,15}... | collective-permute-start | bytes 4325384 | tf_op jit(solution)/shard_map/ppermute | solution.py:64
  719.4 73.9 %collective-permute-start.102 = (bf16[2,16,16,1408]{3,2,1,0:T(8,128)(2,1)}, bf16[2,16,16,1408]{3,2,1,0:T(8,128)(2,1)}, u32[]{:S(2)}, u32[]{:S(2)}) collective-permute-start(bf16[2,16,16,1408]{3,2,1,0:T(8,128)(2,1)} %pad_maximum_fusion.13), channel_id=1, source_target_pairs={{0,16},{2,50},{16,32},{18,2},{32,48},{34,18},{48,0},{50,34},{1,17}... | collective-permute-start | bytes 4325384 | tf_op jit(solution)/shard_map/ppermute | solution.py:64
  723.9 88.9 %collective-permute-start.107 = (bf16[2,16,16,1408]{3,2,1,0:T(8,128)(2,1)}, bf16[2,16,16,1408]{3,2,1,0:T(8,128)(2,1)}, u32[]{:S(2)}, u32[]{:S(2)}) collective-permute-start(bf16[2,16,16,1408]{3,2,1,0:T(8,128)(2,1)} %pad_maximum_fusion.14), channel_id=1, source_target_pairs={{0,4},{2,14},{4,8},{6,2},{8,12},{10,6},{12,0},{14,10},{1,5},{3,15}... | collective-permute-start | bytes 4325384 | tf_op jit(solution)/shard_map/ppermute | solution.py:64
  780.0 48.9 %collective-permute-start.97 = (bf16[2,16,16,1408]{3,2,1,0:T(8,128)(2,1)}, bf16[2,16,16,1408]{3,2,1,0:T(8,128)(2,1)}, u32[]{:S(2)}, u32[]{:S(2)}) collective-permute-start(bf16[2,16,16,1408]{3,2,1,0:T(8,128)(2,1)} %pad_maximum_fusion.12), channel_id=1, source_target_pairs={{0,16},{2,50},{16,32},{18,2},{32,48},{34,18},{48,0},{50,34},{1,17}... | collective-permute-start | bytes 4325384 | tf_op jit(solution)/shard_map/ppermute | solution.py:64
  795.3 35.6 %collective-permute-start.103 = (bf16[16,16,1408]{2,1,0:T(8,128)(2,1)}, bf16[16,16,1408]{2,1,0:T(8,128)(2,1)}, u32[]{:S(2)}, u32[]{:S(2)}) collective-permute-start(bf16[16,16,1408]{2,1,0:T(8,128)(2,1)} %slice_bitcast_fusion.8), channel_id=1, source_target_pairs={{0,2},{2,0},{1,3},{3,1},{4,6},{6,4},{5,7},{7,5},{8,10},{10,8},{9,1... | collective-permute-start | bytes 2162696 | tf_op jit(solution)/shard_map/ppermute | solution.py:51
  (411 other events, 5309.4 us)

commit v2 on v1

v2 whole, which is shorter than its diff:
```python
from functools import partial

import jax
import jax.numpy as jnp
from jax import lax
from jax.experimental import pallas as pl
from jax.experimental.pallas import tpu as pltpu
from jax.sharding import Mesh, PartitionSpec as P

LAYERS = 2
HEADS = 4
SPAN = 64
ATT = 2048
FF = 1408
ROWS = 256
D = 1024
KD = 128
VD = 256
FINE = ("yl", "x", "z", "c", "yh")
CHIPS = ("yh", "yl", "x", "z")
bf = jnp.bfloat16
f32 = jnp.float32
highest = lax.Precision.HIGHEST
norm_eps = 1e-06
group_eps = 1.0
decay_norm = 16.0
scale = KD**-0.5
NN = (((1,), (0,)), ((), ()))
NT = (((1,), (1,)), ((), ()))
TN = (((0,), (0,)), ((), ()))


def dot(a, b, dims=NN, precision=None):
    return lax.dot_general(a, b, dims, precision=precision, preferred_element_type=f32)


def call(kernel, out_shape, *, flops=0, moved=0, vmem=48, **kw):
    return pl.pallas_call(
        kernel,
        out_shape=out_shape,
        compiler_params=pltpu.CompilerParams(vmem_limit_bytes=vmem << 20),
        cost_estimate=pl.CostEstimate(flops=0, bytes_accessed=0, transcendentals=0),
        **kw,
    )


def shape(*dims, dtype=f32):
    return jax.ShapeDtypeStruct(dims, dtype)


def swap(a):
    return lax.ppermute(a, "c", [(0, 1), (1, 0)])


def ring(a, axis):
    if axis == "y":
        names = ("yl", "c", "yh")
        place = lambda i, c: ((i % 2) * 2 + c) * 2 + i // 2
    else:
        names = (axis, "c")
        place = lambda i, c: i * 2 + c
    pairs = [
        (place(i, c), place((i + 1 - 2 * c) % 4, c)) for i in range(4) for c in range(2)
    ]
    return lax.ppermute(a, names, pairs)


def shift(a, axis, step):
    if axis == "y":
        place = lambda i: (i % 2) * 2 + i // 2
        return lax.ppermute(a, ("yl", "yh"), [(place(i), place((i + step) % 4)) for i in range(4)])
    return lax.ppermute(a, axis, [(i, (i + step) % 4) for i in range(4)])


def chip_gather(s):
    return lax.all_gather(s, CHIPS, axis=0, tiled=True).reshape(2, 512, s.shape[1])


def after(value, *others):
    return lax.optimization_barrier((value, others))[0]


def add_kernel(plan, *refs):
    at = sum(count for _, count, _, _ in plan)
    outs, place = refs[at:], 0
    for out, count, start, n in plan:
        value = sum(t[...].reshape(t.shape[-2:]).astype(f32) for t in refs[place : place + count])
        outs[out][:, start : start + n] = value.astype(bf)
        place += count


def add_each(*groups):
    args, specs, outs, out_specs, plan, moved = [], [], [], [], [], 0
    for group in groups:
        start = 0
        for terms in group:
            for term in terms:
                a, which = term if isinstance(term, tuple) else (term, None)
                n = a.shape[-1]
                if which is None:
                    args.append(a.reshape(256, n))
                    specs.append(pl.BlockSpec((64, n), lambda i: (i, 0)))
                else:
                    args.append(a.reshape(2, 256, n))
                    specs.append(pl.BlockSpec((1, 64, n), lambda i, which=which: (which, i, 0)))
            plan.append((len(outs), len(terms), start, n))
            start += n
            moved += 512 * n * (len(terms) + 1)
        outs.append(shape(256, start, dtype=bf))
        out_specs.append(pl.BlockSpec((64, start), lambda i: (i, 0)))
    return call(
        partial(add_kernel, plan), tuple(outs), grid=(4,), in_specs=specs, out_specs=out_specs, flops=moved, moved=moved
    )(*args)


def split_kernel(plan, rows, extra, me, *refs):
    i = pl.program_id(0)
    at = sum(count for _, count, _, _ in plan) + extra
    outs, place = refs[at:], extra
    added = sum(t[...].astype(f32) for t in refs[:extra]).astype(bf)
    for group, count, start, n in plan:
        value = sum(t[...].reshape(t.shape[-2:]).astype(f32) for t in refs[place : place + count]).astype(bf)
        place += count
        for j in range(4):

            @pl.when(i == j)
            def _(out=outs[4 * group + j], value=value, start=start, n=n, group=group):
                out[:rows, start : start + n] = value
                if group == 0:
                    out[rows:, start : start + n] = added[:, start : start + n]


def split_sums(me, rows, groups, extra, extra_place):
    args, specs, outs, out_specs, plan = [], [], [], [], []
    for a in extra:
        args.append(a)
        specs.append(pl.BlockSpec((32, a.shape[1]), lambda i, me: (extra_place, 0)))
    for g, group in enumerate(groups):
        start = 0
        for terms in group:
            for term in terms:
                a, which = term if isinstance(term, tuple) else (term, None)
                n = a.shape[-1]
                if which is None:
                    args.append(a.reshape(-1, n))
                    specs.append(pl.BlockSpec((rows, n), lambda i, me, g=g: ((me[g] + i) % 4, 0)))
                else:
                    args.append(a.reshape(2, 4 * rows, n))
                    specs.append(pl.BlockSpec((1, rows, n), lambda i, me, g=g, which=which: (which, (me[g] + i) % 4, 0)))
            plan.append((g, len(terms), start, n))
            start += n
        dims = (rows + (32 if g == 0 else 0), start)
        outs += [shape(*dims, dtype=bf)] * 4
        out_specs += [pl.BlockSpec(dims, lambda i, me: (0, 0))] * 4
    out = call(
        partial(split_kernel, plan, rows, len(extra)),
        tuple(outs),
        grid_spec=pltpu.PrefetchScalarGridSpec(num_scalar_prefetch=1, grid=(4,), in_specs=specs, out_specs=out_specs),
    )(me, *args)
    return [out[4 * g : 4 * g + 4] for g in range(len(groups))]


def sum_kernel(*refs):
    for g in range(len(refs) // 5):
        refs[4 * (len(refs) // 5) + g][...] = sum(t[...].astype(f32) for t in refs[4 * g : 4 * g + 4])


def sums_of(groups):
    return call(sum_kernel, tuple(shape(*g[0].shape) for g in groups))(*(a for g in groups for a in g))


def passed_on(blocks, axis):
    return [blocks[0]] + [shift(blocks[j], axis, j) for j in (1, 2, 3)]


class Order:
    def __init__(self):
        self.seen = ()

    def __call__(self, kernel, first, *rest):
        out = kernel(after(first, *self.seen), *rest)
        self.seen = (out,)
        return out


def sixteens(a):
    return a.reshape(16, 16, a.shape[-1])


def whole(*dims):
    return pl.BlockSpec(dims, lambda h: (0,) * len(dims))


def per_half(*dims):
    return pl.BlockSpec((1, *dims), lambda h: (h,) + (0,) * len(dims))


def weight(width, place):
    return [pl.BlockSpec((1, 512, width), lambda h: (h, 0, place))] * 2


def rms(v, gain):
    return v * lax.rsqrt(jnp.mean(v * v, axis=-1, keepdims=True) + norm_eps) * gain


def norm_back(v, gain, d_out):
    r = lax.rsqrt(jnp.mean(v * v, axis=-1, keepdims=True) + norm_eps)
    u = d_out * gain
    d_v = r * u - v * (r * r * r) * jnp.mean(u * v, axis=-1, keepdims=True)
    return d_v, jnp.sum(d_out * v * r, axis=0, keepdims=True)


def to_given_order(value, order):
    high = value.astype(bf)
    rest = value - high.astype(f32)
    mid = rest.astype(bf)
    low = (rest - mid.astype(f32)).astype(bf)
    return dot(high, order) + dot(mid, order) + dot(low, order)


def entry_kernel(hidden, cot, valid, order, gain, x_out, g_out, hn_out):
    x = dot(hidden[...], order[...], NT)
    x_out[...] = x
    g_out[...] = dot(cot[...], order[...], NT) * valid[...]
    hn_out[...] = rms(x, gain[...]).astype(bf)


def entry(hidden, cot, valid, order, gain):
    return call(
        entry_kernel,
        (shape(ROWS, D), shape(ROWS, D), shape(ROWS, D, dtype=bf)),
        flops=4 * ROWS * D * D,
        moved=8 * D * D,
    )(hidden, cot, valid, order, gain)


def proj_kernel(hn, low_down, low_up, bias, w, wt, out, latent_out, logits_out):
    out[0] = (dot(hn[:, :512], w[0]) + dot(hn[:, 512:], wt[0])).astype(bf)

    @pl.when(pl.program_id(0) == 0)
    def _():
        latent = dot(hn[...], low_down[...])
        latent_out[...] = latent
        logits_out[...] = dot(latent, low_up[...], NN, highest) + bias[...]


def proj(hn, low_down, low_up, bias, w, place):
    return call(
        proj_kernel,
        (shape(2, ROWS, 1536, dtype=bf), shape(ROWS, 16), shape(ROWS, 512)),
        grid=(2,),
        in_specs=[whole(ROWS, D), whole(D, 16), whole(16, 512), whole(1, 512)] + weight(1536, place),
        out_specs=[per_half(ROWS, 1536), whole(ROWS, 16), whole(ROWS, 512)],
        flops=4 * ROWS * D * 1536,
        moved=4 * D * 1536,
    )(hn, low_down, low_up, bias, *w)


def ffn_kernel(hm, x, gain, w, wt, pre_out, acted_out, x_out, hn_out, acc):
    h = pl.program_id(0)
    near, far = hm[:, :512], hm[:, 512:]
    gate = dot(near, w[0, :, :FF]) + dot(far, wt[0, :, :FF])
    up = dot(near, w[0, :, FF : 2 * FF]) + dot(far, wt[0, :, FF : 2 * FF])
    pre_out[0, :, :FF] = gate.astype(bf)
    pre_out[0, :, FF:] = up.astype(bf)
    acted = (gate * jax.nn.sigmoid(gate) * up).astype(bf)
    acted_out[0] = acted
    part = jnp.concatenate([dot(acted, w[0, :, 2 * FF :], NT), dot(acted, wt[0, :, 2 * FF :], NT)], axis=1)

    @pl.when(h == 0)
    def _():
        acc[...] = part

    @pl.when(h == 1)
    def _():
        total = x[...] + (acc[...] + part)
        x_out[...] = total
        hn_out[...] = rms(total, gain[...]).astype(bf)


def ffn(hm, x, gain, w, place):
    return call(
        ffn_kernel,
        (
            shape(2, ROWS, 2 * FF, dtype=bf),
            shape(2, ROWS, FF, dtype=bf),
            shape(ROWS, D),
            shape(ROWS, D, dtype=bf),
        ),
        grid=(2,),
        in_specs=[whole(ROWS, D), whole(ROWS, D), whole(1, D)] + weight(3 * FF, place),
        out_specs=[per_half(ROWS, 2 * FF), per_half(ROWS, FF), whole(ROWS, D), whole(ROWS, D)],
        scratch_shapes=[pltpu.VMEM((ROWS, D), f32)],
        flops=12 * ROWS * D * FF,
        moved=12 * D * FF,
    )(hm, x, gain, *w)


def ffn_both_kernel(
    hm, x, order, g, gain, w, wt, acted_out, d_out, x_out, gb_out, g_out, gm_out, gain_out, acc, acc_back
):
    h = pl.program_id(0)
    near, far = hm[:, :512], hm[:, 512:]
    gate = dot(near, w[0, :, :FF]) + dot(far, wt[0, :, :FF])
    up = dot(near, w[0, :, FF : 2 * FF]) + dot(far, wt[0, :, FF : 2 * FF])
    sg = jax.nn.sigmoid(gate)
    acted = (gate * sg * up).astype(bf)
    acted_out[0] = acted
    part = jnp.concatenate([dot(acted, w[0, :, 2 * FF :], NT), dot(acted, wt[0, :, 2 * FF :], NT)], axis=1)
    gb = g[...].astype(bf)
    da = dot(gb[:, :512], w[0, :, 2 * FF :]) + dot(gb[:, 512:], wt[0, :, 2 * FF :])
    d_gate = (da * up * sg * (1.0 + gate * (1.0 - sg))).astype(bf)
    d_up = (da * gate * sg).astype(bf)
    d_out[0, :, :FF] = d_gate
    d_out[0, :, FF:] = d_up
    back = jnp.concatenate(
        [dot(d_gate, v[0, :, :FF], NT) + dot(d_up, v[0, :, FF : 2 * FF], NT) for v in (w, wt)], axis=1
    )

    @pl.when(h == 0)
    def _():
        acc[...] = part
        acc_back[...] = back
        gb_out[...] = gb

    @pl.when(h == 1)
    def _():
        x_out[...] = to_given_order(x[...] + (acc[...] + part), order[...])
        d_v, d_gain = norm_back(x[...], gain[...], acc_back[...] + back)
        total = g[...] + d_v
        g_out[...] = total
        gm_out[...] = total.astype(bf)
        gain_out[...] = d_gain


def ffn_both(hm, x, order, g, gain, w, place):
    return call(
        ffn_both_kernel,
        (
            shape(2, ROWS, FF, dtype=bf),
            shape(2, ROWS, 2 * FF, dtype=bf),
            shape(ROWS, D),
            shape(ROWS, D, dtype=bf),
            shape(ROWS, D),
            shape(ROWS, D, dtype=bf),
            shape(1, D),
        ),
        grid=(2,),
        in_specs=[whole(ROWS, D), whole(ROWS, D), whole(D, D), whole(ROWS, D), whole(1, D)] + weight(3 * FF, place),
        out_specs=[
            per_half(ROWS, FF), per_half(ROWS, 2 * FF), whole(ROWS, D), whole(ROWS, D), whole(ROWS, D),
            whole(ROWS, D), whole(1, D),
        ],
        scratch_shapes=[pltpu.VMEM((ROWS, D), f32)] * 2,
        flops=24 * ROWS * D * FF,
        moved=12 * D * FF,
    )(hm, x, order, g, gain, *w)


def ffn_back_kernel(g, x, gain, pre, w, wt, d_out, gb_out, g_out, gm_out, gain_out, acc):
    h = pl.program_id(0)
    gb = g[...].astype(bf)
    da = dot(gb[:, :512], w[0, :, 2 * FF :]) + dot(gb[:, 512:], wt[0, :, 2 * FF :])
    gate = pre[0, :, :FF].astype(f32)
    up = pre[0, :, FF:].astype(f32)
    sg = jax.nn.sigmoid(gate)
    d_gate = (da * up * sg * (1.0 + gate * (1.0 - sg))).astype(bf)
    d_up = (da * gate * sg).astype(bf)
    d_out[0, :, :FF] = d_gate
    d_out[0, :, FF:] = d_up
    part = jnp.concatenate(
        [
            dot(d_gate, v[0, :, :FF], NT) + dot(d_up, v[0, :, FF : 2 * FF], NT)
            for v in (w, wt)
        ],
        axis=1,
    )

    @pl.when(h == 0)
    def _():
        acc[...] = part
        gb_out[...] = gb

    @pl.when(h == 1)
    def _():
        d_v, d_gain = norm_back(x[...], gain[...], acc[...] + part)
        total = g[...] + d_v
        g_out[...] = total
        gm_out[...] = total.astype(bf)
        gain_out[...] = d_gain


def ffn_back(g, x, gain, pre, w, place):
    return call(
        ffn_back_kernel,
        (
            shape(2, ROWS, 2 * FF, dtype=bf),
            shape(ROWS, D, dtype=bf),
            shape(ROWS, D),
            shape(ROWS, D, dtype=bf),
            shape(1, D),
        ),
        grid=(2,),
        in_specs=[whole(ROWS, D), whole(ROWS, D), whole(1, D), per_half(ROWS, 2 * FF)] + weight(3 * FF, place),
        out_specs=[per_half(ROWS, 2 * FF), whole(ROWS, D), whole(ROWS, D), whole(ROWS, D), whole(1, D)],
        scratch_shapes=[pltpu.VMEM((ROWS, D), f32)],
        flops=12 * ROWS * D * FF,
        moved=12 * D * FF,
    )(g, x, gain, pre, *w)


def attn_back_kernel(first, d, d_logits, x, gain, g, low_up, low_down, order, w, wt, g_out, gain_out, latent_out, acc):
    h = pl.program_id(0)
    part = jnp.concatenate([dot(d[0], w[0], NT), dot(d[0], wt[0], NT)], axis=1)

    @pl.when(h == 0)
    def _():
        acc[...] = part

    @pl.when(h == 1)
    def _():
        d_latent = dot(d_logits[...], low_up[...], NT, highest)
        latent_out[...] = d_latent
        d_hn = acc[...] + part + dot(d_latent, low_down[...], NT, highest)
        d_v, d_gain = norm_back(x[...], gain[...], d_hn)
        total = g[...] + d_v
        g_out[...] = to_given_order(total, order[...]) if first else total
        gain_out[...] = d_gain


def attn_back(d, d_logits, x, gain, g, low_up, low_down, order, w, place, first):
    return call(
        partial(attn_back_kernel, first),
        (shape(ROWS, D), shape(1, D), shape(ROWS, 16)),
        grid=(2,),
        in_specs=[
            per_half(ROWS, 1536), whole(ROWS, 512), whole(ROWS, D), whole(1, D), whole(ROWS, D),
            whole(16, 512), whole(D, 16), whole(*order.shape),
        ]
        + weight(1536, place),
        out_specs=[whole(ROWS, D), whole(1, D), whole(ROWS, 16)],
        scratch_shapes=[pltpu.VMEM((ROWS, D), f32)],
        flops=4 * ROWS * D * 1536,
        moved=4 * D * 1536,
    )(d, d_logits, x, gain, g, low_up, low_down, order, *w)


def select_kernel(a, sel, out):
    out[0] = dot(a[...], sel[0], NT).astype(bf)


def select(a, sel):
    n = sel.shape[1]
    both = call(
        select_kernel,
        shape(2, ROWS, n, dtype=bf),
        grid=(2,),
        in_specs=[whole(ROWS, D), per_half(n, D)],
        out_specs=per_half(ROWS, n),
        flops=4 * ROWS * D * n,
        moved=4 * D * n,
    )(a, sel)
    return both, swap(both)


def own_weight_kernel(a, ar, b, br, d, dr, e, er, out):
    n = d.shape[-1]
    out[0, :, :n] = (dot(a[...], d[0], TN) + dot(ar[...], dr[0], TN)).astype(bf)
    out[0, :, n:] = (dot(b[...], e[0], TN) + dot(br[...], er[0], TN)).astype(bf)


def own_weight(a, ar, d, dr, b, br, e, er):
    n, m = d.shape[-1], e.shape[-1]
    near, far = pl.BlockSpec((ROWS, 512), lambda h: (0, 0)), pl.BlockSpec((ROWS, 512), lambda h: (0, 1))
    return call(
        own_weight_kernel,
        shape(2, 512, n + m, dtype=bf),
        grid=(2,),
        in_specs=[near, far] * 2 + [per_half(ROWS, n)] * 2 + [per_half(ROWS, m)] * 2,
        out_specs=per_half(512, n + m),
    )(a, ar, b, br, d, dr, e, er)


def x_weight_kernel(sets, lead, *refs):
    u, u1, u0 = refs[-3:]
    at = 0
    for i in range(sets):
        a, ar, d, dr = refs[4 * i : 4 * i + 4]
        n = d.shape[-1]
        r = (dot(a[0], d[0], TN) + dot(ar[0], dr[0], TN)).astype(bf)
        to = slice(at, at + n)
        part = lambda i: r[i * 128 : (i + 1) * 128].reshape(lead, 128 // lead, n)
        u[0, :, 0, :, to] = part(0)
        u[1, :, 0, :, to] = part(1)
        u1[:, 0, :, to] = part(2)
        u0[:, 0, :, to] = part(3)
        at += n


def x_weight(group, *sets):
    lead = (4, 1)[group]
    total, args, specs = 0, [], []
    for (a, ar), d, dr in sets:
        n = d.shape[-1] // 2
        args += [a, ar, d, dr]
        specs += [
            pl.BlockSpec((1, ROWS, 512), lambda h: (0, 0, group)),
            pl.BlockSpec((1, ROWS, 512), lambda h: (1, 0, group)),
        ]
        specs += [pl.BlockSpec((1, ROWS, n), lambda h: (h, 0, group))] * 2
        total += n
    dims = (lead, 2, 128 // lead, total)
    return call(
        partial(x_weight_kernel, len(sets), lead),
        (shape(2, *dims, dtype=bf), shape(*dims, dtype=bf), shape(*dims, dtype=bf)),
        grid=(2,),
        in_specs=specs,
        out_specs=[pl.BlockSpec((2, lead, 1, 128 // lead, total), lambda h: (0, 0, h, 0, 0))]
        + [pl.BlockSpec((lead, 1, 128 // lead, total), lambda h: (0, h, 0, 0))] * 2,
        flops=4 * ROWS * D * total,
        moved=2 * D * total,
    )(*args)


def y_weight_kernel(sets, where_, *refs):
    u, u1, u0 = refs[-3:]
    h, h2 = where_[0], where_[1]
    at = 0
    for i in range(sets):
        a, ar, d, dr = refs[4 * i : 4 * i + 4]
        n = d.shape[-1]
        to = slice(at, at + n)
        near = lambda place: dot(a[0, :, :256], d[place], TN) + dot(ar[1, :, :256], dr[place], TN)
        u0[:, to] = near(h).astype(bf)
        u[0, :, to] = near(1 - h).astype(bf)
        r = (dot(a[0, :, 256:], d[h2], TN) + dot(ar[1, :, 256:], dr[h2], TN)).astype(bf)
        u1[:, to] = r[:256]
        u[1, :, to] = r[256:]
        at += n


def y_weight(where_, *sets):
    total = sum(d.shape[-1] for _, d, _ in sets)
    args = [v for (a, ar), d, dr in sets for v in (a, ar, d, dr)]
    vm = pl.BlockSpec(memory_space=pltpu.VMEM)
    return call(
        partial(y_weight_kernel, len(sets)),
        (shape(2, 256, total, dtype=bf), shape(256, total, dtype=bf), shape(256, total, dtype=bf)),
        in_specs=[pl.BlockSpec(memory_space=pltpu.SMEM)] + [vm] * len(args),
        out_specs=(vm,) * 3,
        flops=4 * ROWS * D * total,
        moved=2 * D * total,
    )(where_, *args)


def log_sigmoid(v):
    return jnp.minimum(v, 0.0) - jnp.log1p(jnp.exp(-jnp.abs(v)))


def decays(logits):
    ld = log_sigmoid(logits) / decay_norm
    r = lax.broadcasted_iota(jnp.int32, (ROWS, ROWS), 0)
    c = lax.broadcasted_iota(jnp.int32, (ROWS, ROWS), 1)
    lower = ((r >= c) & (r // SPAN == c // SPAN)).astype(f32)
    cum = dot(lower, ld, NN, highest)
    blocks = [cum[i * SPAN : (i + 1) * SPAN] for i in range(4)]
    ends = [b[SPAN - 1 :] for b in blocks]
    return blocks, ends


def run_sum(ends, start, stop):
    total = jnp.zeros_like(ends[0])
    for i in range(start, stop):
        total = total + ends[i]
    return total


def key_factors(blocks, ends, i):
    parts = [jnp.exp((ends[j] - blocks[j]) + run_sum(ends, j + 1, i)) for j in range(i)]
    parts.append(jnp.exp(-blocks[i]))
    return jnp.concatenate(parts, axis=0)


def allowed(segr, segc, i):
    rows_i = segr[i * SPAN : (i + 1) * SPAN]
    count = (i + 1) * SPAN
    r = lax.broadcasted_iota(jnp.int32, (SPAN, count), 0) + i * SPAN
    c = lax.broadcasted_iota(jnp.int32, (SPAN, count), 1)
    return (r >= c) & (rows_i == segc[:, :count])


def start_factors(blocks, ends):
    return jnp.concatenate([jnp.exp(blocks[i] + run_sum(ends, 0, i)) for i in range(4)], axis=0)


def tail_factors(blocks, ends):
    return jnp.concatenate([jnp.exp((ends[i] - blocks[i]) + run_sum(ends, i + 1, 4)) for i in range(4)], axis=0)


def state_kernel(k, v, logits, segr, state):
    blocks, ends = decays(logits[...])
    segr = segr[...]
    tail_k = jnp.where(segr == segr[ROWS - 1 :], k[0].astype(f32) * tail_factors(blocks, ends), 0.0).astype(bf)
    state[0] = dot(tail_k, v[0], TN).astype(bf)


def mix_kernel(q, k, v, logits, segr, segc, out, state_q):
    blocks, ends = decays(logits[...])
    kf = k[0].astype(f32)
    qf = q[0].astype(f32) * scale
    segr, segc = segr[...], segc[...]
    state_q[0] = jnp.where(segr == segr[:1], qf * start_factors(blocks, ends), 0.0).astype(bf)
    for i in range(4):
        count = (i + 1) * SPAN
        qe = (qf[i * SPAN : count] * jnp.exp(blocks[i])).astype(bf)
        ke = (kf[:count] * key_factors(blocks, ends, i)).astype(bf)
        p = jnp.where(allowed(segr, segc, i), dot(qe, ke, NT), 0.0).astype(bf)
        out[0, i * SPAN : count] = dot(p, v[0, :count])


def head_cols(width, first=0):
    return pl.BlockSpec((1, ROWS, width), lambda t: (t // 2, 0, first + t % 2))


def by_head(*dims):
    return pl.BlockSpec((1, *dims), lambda t: (t,) + (0,) * len(dims))


def end_state(qkvg, logits, segr):
    return call(
        state_kernel,
        shape(HEADS, KD, VD, dtype=bf),
        grid=(HEADS,),
        in_specs=[head_cols(KD, 6), head_cols(VD, 1), pl.BlockSpec((ROWS, KD), lambda t: (0, t)), whole(ROWS, 1)],
        out_specs=by_head(KD, VD),
        flops=HEADS * 20_000_000,
        moved=2_000_000,
    )(qkvg, qkvg, logits, segr)


def mix(qkvg, logits, segr, segc):
    return call(
        mix_kernel,
        (shape(2, ROWS, 2 * VD), shape(HEADS, ROWS, KD, dtype=bf)),
        grid=(HEADS,),
        in_specs=[
            head_cols(KD),
            head_cols(KD, 6),
            head_cols(VD, 1),
            pl.BlockSpec((ROWS, KD), lambda t: (0, t)),
            whole(ROWS, 1),
            whole(1, ROWS),
        ],
        out_specs=[head_cols(VD), by_head(ROWS, KD)],
        flops=HEADS * 120_000_000,
        moved=4_000_000,
    )(qkvg, qkvg, qkvg, logits, segr, segc)


def out_weight(place):
    return [pl.BlockSpec((1, 512, VD), lambda t: (t // 2, 0, place * 2 + t % 2))] * 2


def out_kernel(local, state_q, state, g, gain, x, norm_gain, w, wt, mixed_out, rows, x_out, hm_out, acc):
    t = pl.program_id(0)
    mixed = local[0] + dot(state_q[0], state[0])
    mixed_out[0] = mixed
    gate = g[0].astype(f32)
    on = mixed * lax.rsqrt(jnp.mean(mixed * mixed, axis=-1, keepdims=True) + group_eps) * gain[...]
    mine = (on * gate * jax.nn.sigmoid(gate)).astype(bf)
    rows[0] = mine
    part = jnp.concatenate([dot(mine, w[0], NT), dot(mine, wt[0], NT)], axis=1)

    @pl.when(t == 0)
    def _():
        acc[...] = x[...]

    acc[...] += part

    @pl.when(t == HEADS - 1)
    def _():
        total = acc[...]
        x_out[...] = total
        hm_out[...] = rms(total, norm_gain[...]).astype(bf)


def out_rows(local, state_q, state, qkvg, gain, x, norm_gain, w, place):
    return call(
        out_kernel,
        (
            shape(2, ROWS, 2 * VD),
            shape(2, ROWS, 2 * VD, dtype=bf),
            shape(ROWS, D),
            shape(ROWS, D, dtype=bf),
        ),
        grid=(HEADS,),
        in_specs=[
            head_cols(VD), by_head(ROWS, KD), by_head(KD, VD), head_cols(VD, 4), whole(1, VD),
            whole(ROWS, D), whole(1, D),
        ]
        + out_weight(place),
        out_specs=[head_cols(VD), head_cols(VD), whole(ROWS, D), whole(ROWS, D)],
        scratch_shapes=[pltpu.VMEM((ROWS, D), f32)],
        flops=2 * ROWS * D * D + HEADS * 20_000_000,
        moved=2 * D * D + 5_000_000,
    )(local, state_q, state, qkvg, gain, x, norm_gain, *w)


def out_back_kernel(gm, mixed_in, g, gain_in, state_q, w, wt, dg_out, dgain, do_out, d_state):
    dr = dot(gm[:, :512], w[0]) + dot(gm[:, 512:], wt[0])
    mixed = mixed_in[0]
    gate = g[0].astype(f32)
    gain = gain_in[...]
    rho = lax.rsqrt(jnp.mean(mixed * mixed, axis=-1, keepdims=True) + group_eps)
    ng = mixed * rho
    sg = jax.nn.sigmoid(gate)
    d_on = dr * gate * sg
    dg_out[0] = (dr * ng * gain * sg * (1.0 + gate * (1.0 - sg))).astype(bf)
    dgain[0] = jnp.sum(d_on * ng, axis=0, keepdims=True)
    w_ = d_on * gain
    do = (rho * (w_ - ng * jnp.mean(w_ * ng, axis=-1, keepdims=True))).astype(bf)
    do_out[0] = do
    d_state[0] = dot(state_q[0], do, TN).astype(bf)


def out_back(gm, mixed, qkvg, gain, state_q, w, place):
    return call(
        out_back_kernel,
        (
            shape(2, ROWS, 2 * VD, dtype=bf),
            shape(HEADS, 1, VD),
            shape(2, ROWS, 2 * VD, dtype=bf),
            shape(HEADS, KD, VD, dtype=bf),
        ),
        grid=(HEADS,),
        in_specs=[whole(ROWS, D), head_cols(VD), head_cols(VD, 4), whole(1, VD), by_head(ROWS, KD)] + out_weight(place),
        out_specs=[head_cols(VD), by_head(1, VD), head_cols(VD), by_head(KD, VD)],
        flops=2 * ROWS * D * D + HEADS * 20_000_000,
        moved=2 * D * D + 5_000_000,
    )(gm, mixed, qkvg, gain, state_q, *w)


def mix_back_kernel(
    do_in, q, k, v, logits, segr, segc, state_in, state_q_in, dq_out, dk_out, dv_out, net_out
):
    do = do_in[0]
    blocks, ends = decays(logits[...])
    kf = k[0].astype(f32)
    qf = q[0].astype(f32) * scale
    segr, segc = segr[...], segc[...]
    sq = state_q_in[0]
    from_state = dot(do, state_in[0], NT)
    start = jnp.where(segr == segr[:1], start_factors(blocks, ends), 0.0) * scale
    dq_state = from_state * start
    net_state = from_state * sq.astype(f32)
    dk = jnp.zeros((ROWS, KD), f32)
    dv = jnp.zeros((ROWS, VD), f32)
    net_k = jnp.zeros((ROWS, KD), f32)
    nets = []
    grow = lambda a: a if a.shape[0] == ROWS else jnp.concatenate(
        [a, jnp.zeros((ROWS - a.shape[0], a.shape[1]), f32)], axis=0
    )
    for i in range(4):
        count = (i + 1) * SPAN
        here = slice(i * SPAN, count)
        eb = jnp.exp(blocks[i])
        qe = (qf[here] * eb).astype(bf)
        factors = key_factors(blocks, ends, i)
        ke = (kf[:count] * factors).astype(bf)
        keep = allowed(segr, segc, i)
        p = jnp.where(keep, dot(qe, ke, NT), 0.0).astype(bf)
        dp = jnp.where(keep, dot(do[here], v[0, :count], NT), 0.0).astype(bf)
        dv = dv + grow(dot(p, do[here], TN))
        dqe = dot(dp, ke)
        dq_out[0, here] = (dqe * eb * scale + dq_state[here]).astype(bf)
        nets.append(dqe * qe.astype(f32) + net_state[here])
        dke = dot(dp, qe, TN)
        dk = dk + grow(dke * factors)
        net_k = net_k + grow(dke * ke.astype(f32))
    dk_out[0] = dk
    dv_out[0] = dv
    net_out[0] = jnp.concatenate(nets, axis=0) - net_k


def mix_back(do, qkvg, logits, segr, segc, state, state_q):
    return call(
        mix_back_kernel,
        (
            shape(2, ROWS, 2 * KD, dtype=bf),
            shape(HEADS, ROWS, KD),
            shape(HEADS, ROWS, VD),
            shape(HEADS, ROWS, KD),
        ),
        grid=(HEADS,),
        in_specs=[
            head_cols(VD),
            head_cols(KD),
            head_cols(KD, 6),
            head_cols(VD, 1),
            pl.BlockSpec((ROWS, KD), lambda t: (0, t)),
            whole(ROWS, 1),
            whole(1, ROWS),
            by_head(KD, VD),
            by_head(ROWS, KD),
        ],
        out_specs=[head_cols(KD), by_head(ROWS, KD), by_head(ROWS, VD), by_head(ROWS, KD)],
        flops=HEADS * 300_000_000,
        moved=8_000_000,
    )(do, qkvg, qkvg, qkvg, logits, segr, segc, state, state_q)


def decay_back_kernel(dk_in, dv_in, net, k, v, logits_in, segr, segc, d_state, dk_out, dv_out, d_logits):
    logits = logits_in[...]
    blocks, ends = decays(logits)
    segr, segc = segr[...], segc[...]
    kf = k[0].astype(f32)
    tail = jnp.where(segr == segr[ROWS - 1 :], tail_factors(blocks, ends), 0.0)
    tail_k = (kf * tail).astype(bf)
    ds = d_state[0]
    back = dot(v[0], ds, NT)
    dk_out[0] = (dk_in[0] + back * tail).astype(bf)
    dv_out[0] = (dv_in[0] + dot(tail_k, ds)).astype(bf)
    r = lax.broadcasted_iota(jnp.int32, (ROWS, ROWS), 0)
    c = lax.broadcasted_iota(jnp.int32, (ROWS, ROWS), 1)
    same = segr == segc
    after = jnp.where(same & (c >= r), 1.0, 0.0)
    before = jnp.where(same & (c < r), 1.0, 0.0)
    d_ld = dot(after, net[0], NN, highest) + dot(before, back * tail_k.astype(f32), NN, highest)
    d_logits[...] = d_ld * jax.nn.sigmoid(-logits) / decay_norm


def decay_back(dk, dv, net, qkvg, logits, segr, segc, d_state):
    return call(
        decay_back_kernel,
        (
            shape(2, ROWS, 2 * KD, dtype=bf),
            shape(2, ROWS, 2 * VD, dtype=bf),
            shape(ROWS, HEADS * KD),
        ),
        grid=(HEADS,),
        in_specs=[
            by_head(ROWS, KD),
            by_head(ROWS, VD),
            by_head(ROWS, KD),
            head_cols(KD, 6),
            head_cols(VD, 1),
            pl.BlockSpec((ROWS, KD), lambda t: (0, t)),
            whole(ROWS, 1),
            whole(1, ROWS),
            by_head(KD, VD),
        ],
        out_specs=[head_cols(KD), head_cols(VD), pl.BlockSpec((ROWS, KD), lambda t: (0, t))],
        flops=HEADS * 100_000_000,
        moved=4_000_000,
    )(dk, dv, net, qkvg, qkvg, logits, segr, segc, d_state)


def one_hot(places):
    return (places[:, None] == jnp.arange(D, dtype=jnp.int32)[None, :]).astype(bf)


def orders():
    yl, x, z, c, yh = (lax.axis_index(a) for a in FINE)
    k = jnp.arange(D, dtype=jnp.int32)
    base = one_hot((k % 512) // 16 * 32 + jnp.where(k < 512, c, 1 - c) * 16 + k % 16)
    s = 1 - 2 * c
    pick = lambda table, b: jnp.sum(jnp.where(b[:, None] == jnp.arange(table.shape[0])[None], table[None], 0), axis=1)
    far = jnp.array([0, 1, 0, 0, 1, 0, 1, 1], jnp.int32)
    steps = lambda a: jnp.stack([a + 2, a + s, a + s, a, a + 2, a - s, a - s, a]) % 4
    block, r = k // 128, k % 128
    rr = r % 16
    index = lambda far, yl, x, z: far * 512 + ((yl * 4 + x) * 4 + z) * 16 + rr
    along_x = index(pick(far, block), (r // 16) % 2, pick(steps(x), block), r // 32)
    along_z = index(pick(far, block), r // 64, (r // 16) % 4, pick(steps(z), block))
    k = jnp.arange(1536, dtype=jnp.int32)
    block, r = k // 256, k % 256
    rr = r % 16
    along_y = index(
        pick(jnp.array([0, 0, 1, 1, 1, 0], jnp.int32), block),
        pick(jnp.stack([yl, 1 - yl, 1 - yl, yl, 1 - yl, 1 - yl]), block),
        r // 64,
        (r // 16) % 4,
    )
    next_half = ((yh * 2 + yl + s) % 4) // 2
    along_x, along_z, along_y = (a.reshape(2, -1) for a in (along_x, along_z, along_y))
    sel_xz = one_hot(jnp.concatenate([along_x, along_z], axis=1).reshape(-1)).reshape(2, D, D)
    sel_y = one_hot(along_y.reshape(-1)).reshape(2, 768, D)
    return base, sel_xz, sel_y, jnp.stack([yh, next_half]).astype(jnp.int32), jnp.stack([z, yh * 2 + yl, x, yh * 2 + yl, x, z]).astype(jnp.int32)


def own_first(a, axis):
    shape_ = a.shape
    a = a.reshape(*shape_[:axis], 32, 2, 16, *shape_[axis + 1 :])
    zero, one = (lax.index_in_dim(a, i, axis + 1, keepdims=False).reshape(*shape_[:axis], 512, *shape_[axis + 1 :]) for i in (0, 1))
    first = lax.axis_index("c") == 0
    return jnp.concatenate([jnp.where(first, zero, one), jnp.where(first, one, zero)], axis=axis)


def given_order(a, axis):
    shape_ = a.shape
    near, far = lax.slice_in_dim(a, 0, 512, axis=axis), lax.slice_in_dim(a, 512, 1024, axis=axis)
    first = lax.axis_index("c") == 0
    blocks = [b.reshape(*shape_[:axis], 32, 16, *shape_[axis + 1 :]) for b in (jnp.where(first, near, far), jnp.where(first, far, near))]
    return jnp.stack(blocks, axis=axis + 1).reshape(shape_)


def local(
    hidden_in, lengths, cotangent, norm_in, norm_mid, query_w, key_w, value_w, gate_w, out_w,
    low_down, low_up, decay_bias, group_gain, ffn_gate, ffn_up, ffn_down,
):
    yh = lax.axis_index("yh")
    qkvg = [(query_w[l], value_w[l], key_w[l], gate_w[l]) for l in range(LAYERS)]
    feeds = [(ffn_gate[l], ffn_up[l], ffn_down[l]) for l in range(LAYERS)]
    pad = jnp.zeros((16, 128), bf)
    gathered = chip_gather(jnp.concatenate([*qkvg[0], *qkvg[1], out_w[0], out_w[1], pad, *feeds[0]], axis=1))
    gathered_late = chip_gather(jnp.concatenate(feeds[1], axis=1))
    gathered = (gathered, swap(gathered))
    attn_w = [(gathered, 0, 6), (gathered, 1, 7)]
    feed_w = [(gathered, 1), None]

    order, sel_xz, sel_y, where_, me = orders()
    bounds = jnp.cumsum(lengths[0])
    places = jnp.arange(ROWS, dtype=jnp.int32) + yh * ROWS
    seg = jnp.sum((places[:, None] >= bounds[None, :]).astype(jnp.int32), axis=1)
    valid = (seg < lengths.shape[1]).astype(f32)
    segr, segc = seg[:, None], seg[None, :]
    gains_in, gains_mid = own_first(norm_in, 1), own_first(norm_mid, 1)
    downs = own_first(low_down, 1)

    order = after(order, sel_xz, sel_y, segr, segc)
    x, g, hn = entry(hidden_in, cotangent, valid[:, None], order, gains_in[:1])
    saved = []
    for layer in range(LAYERS):
        w, at_qkvg, at_out = attn_w[layer]
        qkvg, latent, logits = proj(hn, downs[layer], low_up[layer], decay_bias[layer][None], w, at_qkvg)
        state = lax.ppermute(end_state(qkvg, logits, segr), "yh", [(0, 1)])
        local_mix, state_q = mix(qkvg, logits, segr, segc)
        mixed, rows, x_mid, hm = out_rows(
            local_mix, state_q, state, qkvg, group_gain[layer][None], x, gains_mid[layer : layer + 1], w, at_out
        )
        last = layer + 1 == LAYERS
        if last:
            gathered_late = after(gathered_late, local_mix)
            feed_w[1] = ((gathered_late, swap(gathered_late)), 0)
        if last:
            acted, d_pre, output, *back = ffn_both(hm, x_mid, order, g, gains_mid[layer : layer + 1], *feed_w[layer])
            saved.append((x, hn, qkvg, latent, logits, state, state_q, mixed, rows, x_mid, hm, None, acted))
        else:
            pre, acted, x_next, hn_next = ffn(hm, x_mid, gains_in[layer + 1 : layer + 2], *feed_w[layer])
            saved.append((x, hn, qkvg, latent, logits, state, state_q, mixed, rows, x_mid, hm, pre, acted))
            x, hn = x_next, hn_next

    def rings(u):
        return [ring(v[0].reshape(2, 16, 16, -1), a) for v, a in zip(u, "xzy")]

    def second_terms(u, r):
        return add_each(*([(v[1], (w, 0))] for v, w in zip(u, r)))

    def second_rings(t):
        return [ring(sixteens(v), a) for v, a in zip(t, "xzy")]

    def last_terms(*parts):
        return [[(u[i][2], r1[i], (swap(r[i]), 1)) for u, r, r1 in parts] for i in range(3)]

    def weights(sets):
        return [x_weight(0, *sets[0]), x_weight(1, *sets[1]), y_weight(where_, *sets[2])]

    def flatten(small):
        stacked = [jnp.stack([part[i] for part in small]) for i in range(6)]
        for i in range(3):
            stacked[i] = given_order(stacked[i], 1)
        flat = jnp.concatenate([a.reshape(-1) for a in stacked])
        return stacked, jnp.pad(flat, (0, 32 * 2944 - flat.shape[0])).reshape(32, 2944)

    then = Order()
    small = [None] * LAYERS
    for layer in reversed(range(LAYERS)):
        x, hn, qkvg, latent, logits, state, state_q, mixed, rows, x_mid, hm, pre, acted = saved[layer]
        bottom = layer == 0
        w, at_qkvg, at_out = attn_w[layer]
        if bottom:
            d_pre, *back = then(ffn_back, g, x_mid, gains_mid[layer : layer + 1], pre, *feed_w[layer])
        gb, g_mid, gm, grad_mid = back
        d_pre_far, acted_far = swap(d_pre), swap(acted)
        d_g, d_gain, do, d_state = then(out_back, gm, mixed, qkvg, group_gain[layer][None], state_q, w, at_out)
        d_state = lax.ppermute(d_state, "yh", [(1, 0)])
        if bottom:
            hm_s, gb_s = then(select, hm, sel_xz), then(select, gb, sel_y)
            sets = (
                ((hm_s, d_pre, d_pre_far),),
                ((hm_s, d_pre, d_pre_far),),
                ((gb_s, acted, acted_far),),
            )
            sets = tuple(p + q for p, q in zip(attn_sets, sets))
            u = then(weights, sets)
            r = rings(u)
        else:
            t = then(own_weight, hm, swap(hm), d_pre, d_pre_far, gb, swap(gb), acted, acted_far)
            top = lax.psum_scatter(t.reshape(64, 16, 3 * FF), CHIPS, scatter_dimension=0, tiled=False)
        d_q, d_k, d_v, net = then(mix_back, do, qkvg, logits, segr, segc, state, state_q)
        d_k, d_v, d_logits = then(decay_back, d_k, d_v, net, qkvg, logits, segr, segc, d_state)
        d = jnp.concatenate([d_q, d_v, d_k, d_g], axis=2)
        d_far = swap(d)
        hn_s, gm_s = then(select, hn, sel_xz), then(select, gm, sel_y)
        attn_sets = (
            ((hn_s, d, d_far),),
            ((hn_s, d, d_far),),
            ((gm_s, rows, swap(rows)),),
        )
        if bottom:
            u_last = then(weights, attn_sets)
            r_last = rings(u_last)
            t1 = then(second_terms, u, r)
            r1 = second_rings(t1)
        g, grad_in, d_latent = then(
            attn_back,
            d, d_logits, x, gains_in[layer : layer + 1], g_mid, low_up[layer], downs[layer].astype(f32), order, w, at_qkvg, bottom
        )
        small[layer] = (
            grad_in[0],
            grad_mid[0],
            dot(hn.astype(f32), d_latent, TN, highest),
            dot(latent, d_logits, TN, highest),
            jnp.sum(d_logits, axis=0),
            jnp.sum(d_gain[:, 0], axis=0),
        )
        if bottom:
            stacked, flat = flatten(small)
            flat = flat + swap(flat)
            flat = flat.astype(bf)
            flat = [flat] + [shift(flat, "x", j) for j in (1, 2, 3)]
            t1_last = then(second_terms, u_last, after(r_last, flat[0]))
            r1_last = second_rings(t1_last)
    input_grad = g

    parts = last_terms((u, r, r1), (u_last, r_last, r1_last))
    parts = split_sums(me[:3], 64, parts, flat, 0)
    parts = [passed_on(p, a) for p, a in zip(parts, "zyx")]
    parts = split_sums(me[3:], 16, [[p] for p in parts], parts[0], 2)
    parts = [passed_on(p, a) for p, a in zip(parts, "yxz")]
    sums = dict(zip("xzy", sums_of(parts)))
    total = sums["x"][16:].reshape(-1)
    width = {"x": 768, "z": 768, "y": 512}
    small_sums, at = [], 0
    for a in stacked:
        small_sums.append(total[at : at + a.size].reshape(a.shape))
        at += a.size

    width = {"x": 768, "z": 768, "y": 512}

    def attn_part(group, lo, hi):
        at = FF + width[group]
        return jnp.stack([sums[group][:16, at + lo : at + hi], sums[group][:16, lo:hi]])

    def feed_part(group):
        at = width[group]
        place = "xzy".index(group) * FF
        return jnp.stack([sums[group][:16, at : at + FF], top[:, place : place + FF].astype(f32)])

    return (
        output,
        input_grad,
        small_sums[0],
        small_sums[1],
        attn_part("x", 0, 256),
        attn_part("z", 0, 256),
        attn_part("x", 256, 768),
        attn_part("z", 256, 768),
        attn_part("y", 0, 512),
        small_sums[2],
        small_sums[3],
        small_sums[4],
        small_sums[5],
        feed_part("x"),
        feed_part("z"),
        feed_part("y"),
    )


def solution(mesh):
    fine = Mesh(mesh.devices.reshape(2, 4, 4, 2, 2), FINE)
    dp = ("yl", "x", "z", "c")
    every = P(FINE, None)
    mat = P(None, dp, "yh")
    rep = P()
    in_specs = (every, P(dp, None), every, rep, rep) + (mat,) * 5 + (rep,) * 4 + (mat,) * 3
    out_specs = (every, every, rep, rep) + (mat,) * 5 + (rep,) * 4 + (mat,) * 3
    return jax.shard_map(local, mesh=fine, in_specs=in_specs, out_specs=out_specs, check_vma=False)
```

time: 901 us -> 611 us (0.68)
  starting transfers between devices: 180 us -> 73.7 us
  other arithmetic: 125 us -> 22.3 us
  local copies, waits for them, and re-layouts: 143 us -> 71.2 us
  waiting for transfers between devices: 225 us -> 213 us
  between operations: 4.74 us -> 15.7 us
    all_to_all x20 -> x0, waiting for transfers between devices: 151 us -> none  [the longest x12 88.5 us: plane_sum(): r = lax.all_to_all(t, PLANE[axis], 0, 0, tiled=True)]
    all_gather x0 -> x2, waiting for transfers between devices: none -> 112 us  [chip_gather(): lax.all_gather(s, CHIPS, axis=0, tiled=True).reshape(2, 512, s.shape[1])]
    all_to_all x20 -> x0, starting transfers between devices: 98.3 us -> none  [the longest x12 52.4 us: plane_sum(): r = lax.all_to_all(t, PLANE[axis], 0, 0, tiled=True)]
    another operation x61 -> x17, other arithmetic: 56 us -> 8.64 us  [the longest x5 3.14 us: attn_part(): jnp.stack([sums[group][:16, at + lo:at + hi], sums[group][:16, lo:hi]])]
    ppermute x2 -> x23, waiting for transfers between devices: 7.42 us -> 48.6 us  [the longest x15 28.8 us: shift(): return lax.ppermute(a, axis, [(i, (i + step) % 4) for i in range(4)])]
    ppermute x2 -> x23, starting transfers between devices: 7.72 us -> 45.6 us  [the longest x15 22.7 us: shift(): return lax.ppermute(a, axis, [(i, (i + step) % 4) for i in range(4)])]
    ppermute x48 -> x12, starting transfers between devices: 46.1 us -> 8.72 us  [ring(): return lax.ppermute(a, names, pairs)]
    squeeze x33 -> x3, local copies, waits for them, and re-layouts: 35.2 us -> 2.23 us  [the longest x2 1.61 us: local(): feeds = [(ffn_gate[l], ffn_up[l], ffn_down[l]) for l in range(LAYERS)]]
  transfers between devices with their start and end apart: 144 -> 65, of which waited for: 36 -> 31; matrix products, arithmetic and copies ran while one was open for 26% -> 8% of each run, Pallas kernels for 23% -> 30%
where the time goes in v2:
time: 611 us; the launch traced here: 601 us
  waiting for transfers between devices  213 us (35%)
  Pallas kernels  201 us (33%)
  starting transfers between devices  73.7 us (12%)
  local copies, waits for them, and re-layouts  71.2 us (12%)
  other arithmetic  22.3 us (4%)
  between operations  15.7 us (3%)
    all_gather x2, waiting for transfers between devices, chip_gather(): lax.all_gather(s, CHIPS, axis=0, tiled=True).reshape(2, 512, s.shape[1])  112 us
    unnamed x309, local copies, waits for them, and re-layouts  49.9 us
    ppermute x12, waiting for transfers between devices, ring(): return lax.ppermute(a, names, pairs)  37.7 us
    ppermute x15, waiting for transfers between devices, shift(): return lax.ppermute(a, axis, [(i, (i + step) % 4) for i in range(4)])  28.8 us
    ppermute x15, starting transfers between devices, shift(): return lax.ppermute(a, axis, [(i, (i + step) % 4) for i in range(4)])  22.7 us
    pallas_call x1, Pallas kernels, ffn_both(): call(ffn_both_kernel, (shape(2, ROWS, FF, dtype=bf), shape(2, ROWS, 2 * F...  19.1 us
    pallas_call x2, Pallas kernels, attn_back(): call(partial(attn_back_kernel, first), (shape(ROWS, D), shape(1, D), shap...  18.4 us
    pallas_call x4, Pallas kernels, x_weight(): call(partial(x_weight_kernel, len(sets), lead), (shape(2, *dims, dtype=bf...  16.9 us
  transfers between devices with their start and end apart: 65, of which 31 were waited for; matrix products, arithmetic and copies ran while one was open for 8% of the time, Pallas kernels for 30%

profile of v2, /device:TPU:0, one launch (start us, length us, event | category | flops | bytes accessed | tf_op | source)
XLA Modules:
  0.0 600.9 jit_solution(10681300016065366811)
XLA Ops:
  18.4 107.3 %all-gather.3.cloned.1.call-done = bf16[1024,8448]{1,0:T(8,128)(2,1)} async-done(((bf16[16,8448]{1,0:T(8,128)(2,1)}), bf16[1024,8448]{1,0:T(8,128)(2,1)}) %all-gather.3.cloned.1.call-update) | async-done | bytes 17301520 | tf_op jit(solution)/shard_map/all_gather | solution.py:76
  160.4 6.0 %collective-permute-start.1 = (bf16[4,128,256]{2,1,0:T(8,128)(2,1)}, bf16[4,128,256]{2,1,0:T(8,128)(2,1)}, u32[]{:S(2)}, u32[]{:S(2)}) collective-permute-start(bf16[4,128,256]{2,1,0:T(8,128)(2,1)} %shard_map.309), channel_id=1, source_target_pairs={{0,1},{2,3},{4,5},{6,7},{8,9},{10,11},{12,13},{14,15},{16,17},{18,... | collective-permute-start | bytes 786440 | tf_op jit(solution)/shard_map/ppermute | solution.py:936
  181.2 11.8 %shard_map.311 = (bf16[2,256,2816]{2,1,0:T(8,128)(2,1)}, bf16[2,256,1408]{2,1,0:T(8,128)(2,1)}, f32[256,1024]{1,0:T(8,128)S(1)}, bf16[256,1024]{1,0:T(8,128)(2,1)S(1)}) custom-call(bf16[256,1024]{1,0:T(8,128)(2,1)S(1)} %get-tuple-element.250.hm.a, f32[256,1024]{1,0:T(8,128)S(1)} %get-tuple-element.202.x, f32[1,1024]{1,0:T(1,128)S(1)} %get-tuple-element.489.gain, ...), custom_call_target="tpu_custom_call" | custom-call | tf_op jit(solution)/shard_map/pallas_call | solution.py:282
  219.5 6.0 collective-permute-done.2.state.state_in
  231.2 19.1 %shard_map.316 = (bf16[2,256,1408]{2,1,0:T(8,128)(2,1)S(1)}, bf16[2,256,2816]{2,1,0:T(8,128)(2,1)}, f32[256,1024]{1,0:T(8,128)}, bf16[256,1024]{1,0:T(8,128)(2,1...) custom-call(bf16[256,1024]{1,0:T(8,128)(2,1)S(1)} %get-tuple-element.220.hm.a, ...), custom_call_target="tpu_custom_call" | custom-call | tf_op jit(solution)/shard_map/pallas_call | solution.py:337
  260.5 8.9 %shard_map.318 = bf16[2,512,4224]{2,1,0:T(8,128)(2,1)} custom-call(bf16[256,1024]{1,0:T(8,128)(2,1)S(1)} %get-tuple-element.220.hm.a, bf16[256,1024]{1,0:T(8,128)(2,1)S(1)} %collective-permute-done.4.ar, bf16[256,1024]{1,0:T(8,128)(2,1)S(1)} %get-tuple-element.221.b, bf16[256,1024]{1,0:T(8,128)(2,1)S(1)} %collective-permute-done.5.br, ...), custom_call_target="tpu_custom_call" | custom-call | tf_op jit(solution)/shard_map/pallas_call | solution.py:475
  271.4 7.5 %shard_map.319 = (bf16[2,256,256]{2,1,0:T(8,128)(2,1)S(1)}, f32[4,256,128]{2,1,0:T(8,128)S(1)}, f32[4,256,256]{2,1,0:T(8,128)S(1)}, f32[4,256,128]{2,1,0:T(8,128)S(1)}) custom-call(bf16[2,256,512]{2,1,0:T(8,128)(2,1)S(1)} %copy-done.86, bf16[2,256,1536]{2,1,0:T(8,128)(2,1)S(1)} %copy-done.3, bf16[2,256,1536]{2,1,0:T(8,128)(2,1)S(1)} %copy-done.3, ...), custom_call_target="tpu_custom_call" | custom-call | tf_op jit(solution)/shard_map/pallas_call | solution.py:786
  278.9 7.4 %shard_map.320 = (bf16[2,256,256]{2,1,0:T(8,128)(2,1)S(1)}, bf16[2,256,512]{2,1,0:T(8,128)(2,1)S(1)}, f32[256,512]{1,0:T(8,128)S(1)}) custom-call(f32[4,256,128]{2,1,0:T(8,128)S(1)} %get-tuple-element.229.dk_in, f32[4,256,256]{2,1,0:T(8,128)S(1)} %get-tuple-element.227.dv_in, f32[4,256,128]{2,1,0:T(8,128)S(1)} %get-tuple-element.228.net, ...), custom_call_target="tpu_custom_call" | custom-call | tf_op jit(solution)/shard_map/pallas_call | solution.py:833
  296.5 7.3 %shard_map.323 = (f32[256,1024]{1,0:T(8,128)S(1)}, f32[1,1024]{1,0:T(1,128)S(1)}, f32[256,16]{1,0:T(8,128)S(1)}) custom-call(bf16[2,256,1536]{2,1,0:T(8,128)(2,1)S(1)} %constant_dynamic-update-slice_fusion.20.d.refs_2_, f32[256,512]{1,0:T(8,128)S(1)} %get-tuple-element.232.d_logits, f32[256,1024]{1,0:T(8,128)S(1)} %copy-done.34, ...), custom_call_target="tpu_custom_call" | custom-call | tf_op jit(solution)/shard_map/pallas_call | solution.py:432
  303.9 11.7 %shard_map.324 = (bf16[2,256,2816]{2,1,0:T(8,128)(2,1)}, bf16[256,1024]{1,0:T(8,128)(2,1)S(1)}, f32[256,1024]{1,0:T(8,128)S(1)}, bf16[256,1024]{1,0:T(8,128)(2,1)S(1)}, f32[1,1024]{1,0:T(1,128)S(1)}) custom-call(f32[256,1024]{1,0:T(8,128)S(1)} %get-tuple-element.237.g, f32[256,1024]{1,0:T(8,128)S(1)} %copy-done.29, ...), custom_call_target="tpu_custom_call" | custom-call | tf_op jit(solution)/shard_map/pallas_call | solution.py:394
  340.8 5.7 shard_map.329
  347.5 6.0 shard_map.328
  354.5 6.1 %shard_map.330 = (bf16[2,256,1920]{2,1,0:T(8,128)(2,1)}, bf16[256,1920]{1,0:T(8,128)(2,1)S(1)}, bf16[256,1920]{1,0:T(8,128)(2,1)S(1)}) custom-call(s32[2]{0:T(128)S(1)} %pad_add_fusion.1.where_, bf16[2,256,768]{2,1,0:T(8,128)(2,1)S(1)} %copy-done.40, bf16[2,256,768]{2,1,0:T(8,128)(2,1)S(1)} %copy-done.71, bf16[2,256,512]{2,1,0:T(8,128)(2,1)S(1)} %copy-done.74, ...), custom_call_target="tpu_custom_call" | custom-call | tf_op jit(solution)/shard_map/pallas_call | solution.py:546
  360.6 8.3 %shard_map.331 = (bf16[2,256,256]{2,1,0:T(8,128)(2,1)S(1)}, f32[4,256,128]{2,1,0:T(8,128)S(1)}, f32[4,256,256]{2,1,0:T(8,128)S(1)}, f32[4,256,128]{2,1,0:T(8,128)S(1)}) custom-call(bf16[2,256,512]{2,1,0:T(8,128)(2,1)S(1)} %copy-done.84, bf16[2,256,1536]{2,1,0:T(8,128)(2,1)S(1)} %copy-done.1, bf16[2,256,1536]{2,1,0:T(8,128)(2,1)S(1)} %copy-done.1, ...), custom_call_target="tpu_custom_call" | custom-call | tf_op jit(solution)/shard_map/pallas_call | solution.py:786
  369.0 7.3 %shard_map.332 = (bf16[2,256,256]{2,1,0:T(8,128)(2,1)S(1)}, bf16[2,256,512]{2,1,0:T(8,128)(2,1)S(1)}, f32[256,512]{1,0:T(8,128)S(1)}) custom-call(f32[4,256,128]{2,1,0:T(8,128)S(1)} %get-tuple-element.292.dk_in, f32[4,256,256]{2,1,0:T(8,128)S(1)} %get-tuple-element.290.dv_in, f32[4,256,128]{2,1,0:T(8,128)S(1)} %get-tuple-element.291.net, ...), custom_call_target="tpu_custom_call" | custom-call | tf_op jit(solution)/shard_map/pallas_call | solution.py:833
  418.5 11.1 %shard_map.339 = (f32[256,1024]{1,0:T(8,128)}, f32[1,1024]{1,0:T(1,128)S(1)}, f32[256,16]{1,0:T(8,128)S(1)}) custom-call(bf16[2,256,1536]{2,1,0:T(8,128)(2,1)} %constant_dynamic-update-slice_fusion.24.refs_2_.d, f32[256,512]{1,0:T(8,128)S(1)} %copy-done.21, f32[256,1024]{1,0:T(8,128)S(1)} %copy-done.27, f32[1,1024]{1,0:T(1,128)S(1)} %get-tuple-element.490.gain, ...), custom_call_target="tpu_custom_call" | custom-call | tf_op jit(solution)/shard_map/pallas_call | solution.py:432
  446.3 6.0 %collective-permute-done.32 = bf16[2,16,16,768]{3,2,1,0:T(8,128)(2,1)S(1)} collective-permute-done((bf16[2,16,16,768]{3,2,1,0:T(8,128)(2,1)}, bf16[2,16,16,768]{3,2,1,0:T(8,128)(2,1)S(1)}, u32[]{:S(2)}, u32[]{:S(2)}) %collective-permute-start.32) | collective-permute-done | bytes 786464 | tf_op jit(solution)/shard_map/ppermute | solution.py:65
  464.1 7.4 %collective-permute-done.28.refs_3_ = bf16[32,2944]{1,0:T(8,128)(2,1)S(1)} collective-permute-done((bf16[32,2944]{1,0:T(8,128)(2,1)S(1)}, bf16[32,2944]{1,0:T(8,128)(2,1)S(1)}, u32[]{:S(2)}, u32[]{:S(2)}) %collective-permute-start.28) | collective-permute-done | bytes 188448 | tf_op jit(solution)/shard_map/ppermute | solution.py:72
  473.5 7.8 %collective-permute-done.38 = bf16[16,16,768]{2,1,0:T(8,128)(2,1)S(1)} collective-permute-done((bf16[16,16,768]{2,1,0:T(8,128)(2,1)S(1)}, bf16[16,16,768]{2,1,0:T(8,128)(2,1)S(1)}, u32[]{:S(2)}, u32[]{:S(2)}) %collective-permute-start.38) | collective-permute-done | bytes 393248 | tf_op jit(solution)/shard_map/ppermute | solution.py:65
  481.5 18.0 %collective-permute-done.29 = bf16[16,16,2176]{2,1,0:T(8,128)(2,1)S(1)} collective-permute-done((bf16[16,16,2176]{2,1,0:T(8,128)(2,1)S(1)}, bf16[16,16,2176]{2,1,0:T(8,128)(2,1)S(1)}, u32[]{:S(2)}, u32[]{:S(2)}) %collective-permute-start.29) | collective-permute-done | bytes 1114144 | tf_op jit(solution)/shard_map/ppermute | solution.py:65
  506.0 8.3 %shard_map.341 = (bf16[96,2944]{1,0:T(8,128)(2,1)}, bf16[96,2944]{1,0:T(8,128)(2,1)}, bf16[96,2944]{1,0:T(8,128)(2,1)}, bf16[96,2944]{1,0:T(8,128)(2,1)}, bf16[6...) custom-call(s32[3]{0:T(128)S(1)} %pad_add_fusion.3.me, ...), custom_call_target="tpu_custom_call" | custom-call | tf_op jit(solution)/shard_map/pallas_call | solution.py:155
  519.2 6.2 %collective-permute-done.50.refs_13_ = bf16[64,2432]{1,0:T(8,128)(2,1)S(1)} collective-permute-done((bf16[64,2432]{1,0:T(8,128)(2,1)S(1)}, bf16[64,2432]{1,0:T(8,128)(2,1)S(1)}, u32[]{:S(2)}, u32[]{:S(2)}) %collective-permute-start.50) | collective-permute-done | bytes 311328 | tf_op jit(solution)/shard_map/ppermute | solution.py:72
  525.4 7.3 %collective-permute-start.45 = (bf16[96,2944]{1,0:T(8,128)(2,1)}, bf16[96,2944]{1,0:T(8,128)(2,1)S(1)}, u32[]{:S(2)}, u32[]{:S(2)}) collective-permute-start(bf16[96,2944]{1,0:T(8,128)(2,1)} %get-tuple-element.346), channel_id=1, source_target_pairs={{0,8},{4,12},{8,0},{12,4},{1,9},{5,13},{9,1},{13,5},{2,10},{6,14},... | collective-permute-start | bytes 1695752 | tf_op jit(solution)/shard_map/ppermute | solution.py:72
  544.6 8.3 %collective-permute-done.49.refs_11_ = bf16[64,2944]{1,0:T(8,128)(2,1)S(1)} collective-permute-done((bf16[64,2944]{1,0:T(8,128)(2,1)S(1)}, bf16[64,2944]{1,0:T(8,128)(2,1)S(1)}, u32[]{:S(2)}, u32[]{:S(2)}) %collective-permute-start.49) | collective-permute-done | bytes 376864 | tf_op jit(solution)/shard_map/ppermute | solution.py:71
  (576 shorter events, 278.4 us)
Async XLA Ops:
  7.2 118.5 %all-gather.3.cloned.1.call-start = ((), (), s32[]{:S(2)}) async-start(), calls=%async_computation.1 | async-start | bytes 17571840 | tf_op jit(solution)/shard_map/all_gather | solution.py:76
  17.5 193.7 %all-gather.5.cloned.1.call-start = ((), (), s32[]{:S(2)}) async-start(), calls=%async_computation.2 | async-start | bytes 8785920 | tf_op jit(solution)/shard_map/all_gather | solution.py:76
  125.7 26.2 %collective-permute-start = (bf16[2,512,8448]{2,1,0:T(8,128)(2,1)}, bf16[2,512,8448]{2,1,0:T(8,128)(2,1)}, u32[]{:S(2)}, u32[]{:S(2)}) collective-permute-start(bf16[2,512,8448]{2,1,0:T(8,128)(2,1)} %bitcast.214), channel_id=1, source_target_pairs={{0,2},{2,0},{1,3},{3,1},{4,6},{6,4},{5,7},{7,5},{8,10},{10,8},{9,1... | collective-permute-start | bytes 51904520 | tf_op jit(solution)/shard_map/ppermute | solution.py:52
  127.2 464.1 %reduce-scatter.2.cloned.1.call-start = ((), (), s32[]{:S(2)}) async-start(), calls=%async_computation.3 | async-start | bytes 8785920 | tf_op jit(solution)/shard_map/reduce_scatter | solution.py:999
  211.2 20.0 %collective-permute-start.3 = (bf16[2,512,4224]{2,1,0:T(8,128)(2,1)}, bf16[2,512,4224]{2,1,0:T(8,128)(2,1)}, u32[]{:S(2)}, u32[]{:S(2)}) collective-permute-start(bf16[2,512,4224]{2,1,0:T(8,128)(2,1)} %bitcast.226), channel_id=1, source_target_pairs={{0,2},{2,0},{1,3},{3,1},{4,6},{6,4},{5,7},{7,5},{8,10},{10,8},{9,1... | collective-permute-start | bytes 25952264 | tf_op jit(solution)/shard_map/ppermute | solution.py:52
  257.4 21.6 %collective-permute-start.8 = (bf16[4,128,256]{2,1,0:T(8,128)(2,1)}, bf16[4,128,256]{2,1,0:T(8,128)(2,1)}, u32[]{:S(2)}, u32[]{:S(2)}) collective-permute-start(bf16[4,128,256]{2,1,0:T(8,128)(2,1)} %get-tuple-element.219), channel_id=1, source_target_pairs={{1,0},{3,2},{5,4},{7,6},{9,8},{11,10},{13,12},{15,14},{17,16},{19,... | collective-permute-start | bytes 786440 | tf_op jit(solution)/shard_map/ppermute | solution.py:986
  317.2 18.6 %collective-permute-start.13 = (bf16[2,256,2816]{2,1,0:T(8,128)(2,1)}, bf16[2,256,2816]{2,1,0:T(8,128)(2,1)}, u32[]{:S(2)}, u32[]{:S(2)}) collective-permute-start(bf16[2,256,2816]{2,1,0:T(8,128)(2,1)} %get-tuple-element.271.refs_6_), channel_id=1, source_target_pairs={{0,2},{2,0},{1,3},{3,1},{4,6},{6,4},{5,7},{7,5},{8,10},{10,8},{9,1... | collective-permute-start | bytes 8650760 | tf_op jit(solution)/shard_map/ppermute | solution.py:52
  334.2 34.8 %collective-permute-start.17 = (bf16[4,128,256]{2,1,0:T(8,128)(2,1)}, bf16[4,128,256]{2,1,0:T(8,128)(2,1)}, u32[]{:S(2)}, u32[]{:S(2)}) collective-permute-start(bf16[4,128,256]{2,1,0:T(8,128)(2,1)} %get-tuple-element.249), channel_id=1, source_target_pairs={{1,0},{3,2},{5,4},{7,6},{9,8},{11,10},{13,12},{15,14},{17,16},{19,... | collective-permute-start | bytes 786440 | tf_op jit(solution)/shard_map/ppermute | solution.py:986
  378.3 33.3 %collective-permute-start.23 = (bf16[2,16,16,2176]{3,2,1,0:T(8,128)(2,1)}, bf16[2,16,16,2176]{3,2,1,0:T(8,128)(2,1)}, u32[]{:S(2)}, u32[]{:S(2)}) collective-permute-start(bf16[2,16,16,2176]{3,2,1,0:T(8,128)(2,1)} %bitcast.42), channel_id=1, source_target_pairs={{0,4},{2,14},{4,8},{6,2},{8,12},{10,6},{12,0},{14,10},{1,5},{3,15}... | collective-permute-start | bytes 6684680 | tf_op jit(solution)/shard_map/ppermute | solution.py:65
  379.7 33.3 %collective-permute-start.22 = (bf16[2,16,16,2176]{3,2,1,0:T(8,128)(2,1)}, bf16[2,16,16,2176]{3,2,1,0:T(8,128)(2,1)}, u32[]{:S(2)}, u32[]{:S(2)}) collective-permute-start(bf16[2,16,16,2176]{3,2,1,0:T(8,128)(2,1)} %bitcast.39), channel_id=1, source_target_pairs={{0,16},{2,50},{16,32},{18,2},{32,48},{34,18},{48,0},{50,34},{1,17}... | collective-permute-start | bytes 6684680 | tf_op jit(solution)/shard_map/ppermute | solution.py:65
  380.0 31.1 %collective-permute-start.24 = (bf16[2,16,16,1920]{3,2,1,0:T(8,128)(2,1)}, bf16[2,16,16,1920]{3,2,1,0:T(8,128)(2,1)}, u32[]{:S(2)}, u32[]{:S(2)}) collective-permute-start(bf16[2,16,16,1920]{3,2,1,0:T(8,128)(2,1)} %bitcast.44), channel_id=1, source_target_pairs={{0,64},{2,67},{64,1},{66,2},{1,65},{3,66},{65,0},{67,3},{4,68},{6,... | collective-permute-start | bytes 5898248 | tf_op jit(solution)/shard_map/ppermute | solution.py:65
  410.4 30.0 %collective-permute-start.33 = (bf16[2,16,16,512]{3,2,1,0:T(8,128)(2,1)}, bf16[2,16,16,512]{3,2,1,0:T(8,128)(2,1)S(1)}, u32[]{:S(2)}, u32[]{:S(2)}) collective-permute-start(bf16[2,16,16,512]{3,2,1,0:T(8,128)(2,1)} %bitcast.63), channel_id=1, source_target_pairs={{0,64},{2,67},{64,1},{66,2},{1,65},{3,66},{65,0},{67,3},{4,68},{6,... | collective-permute-start | bytes 1572872 | tf_op jit(solution)/shard_map/ppermute | solution.py:65
  439.8 41.7 %collective-permute-start.40 = (bf16[16,16,1920]{2,1,0:T(8,128)(2,1)}, bf16[16,16,1920]{2,1,0:T(8,128)(2,1)}, u32[]{:S(2)}, u32[]{:S(2)}) collective-permute-start(bf16[16,16,1920]{2,1,0:T(8,128)(2,1)} %bitcast.208), channel_id=1, source_target_pairs={{0,64},{2,67},{64,1},{66,2},{1,65},{3,66},{65,0},{67,3},{4,68},{6,... | collective-permute-start | bytes 2949128 | tf_op jit(solution)/shard_map/ppermute | solution.py:65
  440.4 32.5 %collective-permute-start.43 = (bf16[2,16,16,512]{3,2,1,0:T(8,128)(2,1)S(1)}, bf16[2,16,16,512]{3,2,1,0:T(8,128)(2,1)S(1)}, u32[]{:S(2)}, u32[]{:S(2)}) collective-permute-start(bf16[2,16,16,512]{3,2,1,0:T(8,128)(2,1)S(1)} %collective-permute-done.33), channel_id=1, source_target_pairs={{0,2},{2,0},{1,3},{3,1},{4,6},{6,4},{5,7},{7,5},{8,10},{10,8},{9,1... | collective-permute-start | bytes 1572872 | tf_op jit(solution)/shard_map/ppermute | solution.py:52
  472.9 30.0 %collective-permute-start.37 = (bf16[2,16,16,2176]{3,2,1,0:T(8,128)(2,1)}, bf16[2,16,16,2176]{3,2,1,0:T(8,128)(2,1)S(1)}, u32[]{:S(2)}, u32[]{:S(2)}) collective-permute-start(bf16[2,16,16,2176]{3,2,1,0:T(8,128)(2,1)} %collective-permute-done.23), channel_id=1, source_target_pairs={{0,2},{2,0},{1,3},{3,1},{4,6},{6,4},{5,7},{7,5},{8,10},{10,8},{9,1... | collective-permute-start | bytes 6684680 | tf_op jit(solution)/shard_map/ppermute | solution.py:52
  472.9 30.0 %collective-permute-start.30 = (bf16[2,16,16,2176]{3,2,1,0:T(8,128)(2,1)}, bf16[2,16,16,2176]{3,2,1,0:T(8,128)(2,1)S(1)}, u32[]{:S(2)}, u32[]{:S(2)}) collective-permute-start(bf16[2,16,16,2176]{3,2,1,0:T(8,128)(2,1)} %collective-permute-done.22), channel_id=1, source_target_pairs={{0,2},{2,0},{1,3},{3,1},{4,6},{6,4},{5,7},{7,5},{8,10},{10,8},{9,1... | collective-permute-start | bytes 6684680 | tf_op jit(solution)/shard_map/ppermute | solution.py:52
  473.4 29.5 %collective-permute-start.41 = (bf16[2,16,16,1920]{3,2,1,0:T(8,128)(2,1)}, bf16[2,16,16,1920]{3,2,1,0:T(8,128)(2,1)S(1)}, u32[]{:S(2)}, u32[]{:S(2)}) collective-permute-start(bf16[2,16,16,1920]{3,2,1,0:T(8,128)(2,1)} %collective-permute-done.24), channel_id=1, source_target_pairs={{0,2},{2,0},{1,3},{3,1},{4,6},{6,4},{5,7},{7,5},{8,10},{10,8},{9,1... | collective-permute-start | bytes 5898248 | tf_op jit(solution)/shard_map/ppermute | solution.py:52
  518.0 21.0 %collective-permute-start.47 = (bf16[64,2944]{1,0:T(8,128)(2,1)S(1)}, bf16[64,2944]{1,0:T(8,128)(2,1)S(1)}, u32[]{:S(2)}, u32[]{:S(2)}) collective-permute-start(bf16[64,2944]{1,0:T(8,128)(2,1)S(1)} %get-tuple-element.349), channel_id=1, source_target_pairs={{0,64},{64,1},{1,65},{65,0},{2,66},{66,3},{3,67},{67,2},{4,68},{68... | collective-permute-start | bytes 1130504 | tf_op jit(solution)/shard_map/ppermute | solution.py:71
  519.2 33.7 %collective-permute-start.44 = (bf16[96,2944]{1,0:T(8,128)(2,1)}, bf16[96,2944]{1,0:T(8,128)(2,1)S(1)}, u32[]{:S(2)}, u32[]{:S(2)}) collective-permute-start(bf16[96,2944]{1,0:T(8,128)(2,1)} %get-tuple-element.345), channel_id=1, source_target_pairs={{0,4},{4,8},{8,12},{12,0},{1,5},{5,9},{9,13},{13,1},{2,6},{6,10},{... | collective-permute-start | bytes 1695752 | tf_op jit(solution)/shard_map/ppermute | solution.py:72
  525.4 27.5 %collective-permute-start.45 = (bf16[96,2944]{1,0:T(8,128)(2,1)}, bf16[96,2944]{1,0:T(8,128)(2,1)S(1)}, u32[]{:S(2)}, u32[]{:S(2)}) collective-permute-start(bf16[96,2944]{1,0:T(8,128)(2,1)} %get-tuple-element.346), channel_id=1, source_target_pairs={{0,8},{4,12},{8,0},{12,4},{1,9},{5,13},{9,1},{13,5},{2,10},{6,14},... | collective-permute-start | bytes 1695752 | tf_op jit(solution)/shard_map/ppermute | solution.py:72
  532.7 20.3 %collective-permute-start.46 = (bf16[96,2944]{1,0:T(8,128)(2,1)}, bf16[96,2944]{1,0:T(8,128)(2,1)S(1)}, u32[]{:S(2)}, u32[]{:S(2)}) collective-permute-start(bf16[96,2944]{1,0:T(8,128)(2,1)} %get-tuple-element.347), channel_id=1, source_target_pairs={{0,12},{4,0},{8,4},{12,8},{1,13},{5,1},{9,5},{13,9},{2,14},{6,2},{... | collective-permute-start | bytes 1695752 | tf_op jit(solution)/shard_map/ppermute | solution.py:72
  558.8 24.9 %collective-permute-start.53 = (bf16[48,2944]{1,0:T(8,128)(2,1)S(1)}, bf16[48,2944]{1,0:T(8,128)(2,1)S(1)}, u32[]{:S(2)}, u32[]{:S(2)}) collective-permute-start(bf16[48,2944]{1,0:T(8,128)(2,1)S(1)} %get-tuple-element.357), channel_id=1, source_target_pairs={{0,64},{64,1},{1,65},{65,0},{2,66},{66,3},{3,67},{67,2},{4,68},{68... | collective-permute-start | bytes 847880 | tf_op jit(solution)/shard_map/ppermute | solution.py:71
  559.1 24.6 %collective-permute-start.54 = (bf16[48,2944]{1,0:T(8,128)(2,1)S(1)}, bf16[48,2944]{1,0:T(8,128)(2,1)S(1)}, u32[]{:S(2)}, u32[]{:S(2)}) collective-permute-start(bf16[48,2944]{1,0:T(8,128)(2,1)S(1)} %get-tuple-element.358), channel_id=1, source_target_pairs={{0,1},{64,65},{1,0},{65,64},{2,3},{66,67},{3,2},{67,66},{4,5},{68,... | collective-permute-start | bytes 847880 | tf_op jit(solution)/shard_map/ppermute | solution.py:71
  563.5 20.2 %collective-permute-start.55 = (bf16[48,2944]{1,0:T(8,128)(2,1)S(1)}, bf16[48,2944]{1,0:T(8,128)(2,1)S(1)}, u32[]{:S(2)}, u32[]{:S(2)}) collective-permute-start(bf16[48,2944]{1,0:T(8,128)(2,1)S(1)} %get-tuple-element.359), channel_id=1, source_target_pairs={{0,65},{64,0},{1,64},{65,1},{2,67},{66,2},{3,66},{67,3},{4,69},{68... | collective-permute-start | bytes 847880 | tf_op jit(solution)/shard_map/ppermute | solution.py:71
  (179 other events, 1672.6 us)
Sparse Core Ops, SparseCore 0:
  17.6 108.0 all-gather.2
  129.1 82.0 all-gather.4
  269.6 231.1 reduce-scatter.1

commit v3 on v2

--- a/solution.py
+++ b/solution.py
@@ -39,7 +39,7 @@
         kernel,
         out_shape=out_shape,
         compiler_params=pltpu.CompilerParams(vmem_limit_bytes=vmem << 20),
-        cost_estimate=pl.CostEstimate(flops=0, bytes_accessed=0, transcendentals=0),
+        cost_estimate=pl.CostEstimate(flops=flops or 500_000_000, bytes_accessed=moved or 8_000_000, transcendentals=0),
         **kw,
     )
 
@@ -80,11 +80,16 @@
     return lax.optimization_barrier((value, others))[0]
 
 
+def rows_part(t, start, n):
+    v = t[...].reshape(t.shape[-2:])
+    return (v if v.shape[1] == n else v[:, start : start + n]).astype(f32)
+
+
 def add_kernel(plan, *refs):
     at = sum(count for _, count, _, _ in plan)
     outs, place = refs[at:], 0
     for out, count, start, n in plan:
-        value = sum(t[...].reshape(t.shape[-2:]).astype(f32) for t in refs[place : place + count])
+        value = sum(rows_part(t, start, n) for t in refs[place : place + count])
         outs[out][:, start : start + n] = value.astype(bf)
         place += count
 
@@ -96,13 +101,14 @@
         for terms in group:
             for term in terms:
                 a, which = term if isinstance(term, tuple) else (term, None)
-                n = a.shape[-1]
+                wide = a.shape[-1]
                 if which is None:
-                    args.append(a.reshape(256, n))
-                    specs.append(pl.BlockSpec((64, n), lambda i: (i, 0)))
+                    args.append(a.reshape(256, wide))
+                    specs.append(pl.BlockSpec((64, wide), lambda i: (i, 0)))
                 else:
-                    args.append(a.reshape(2, 256, n))
-                    specs.append(pl.BlockSpec((1, 64, n), lambda i, which=which: (which, i, 0)))
+                    args.append(a.reshape(2, 256, wide))
+                    specs.append(pl.BlockSpec((1, 64, wide), lambda i, which=which: (which, i, 0)))
+            n = terms[0].shape[-1]
             plan.append((len(outs), len(terms), start, n))
             start += n
             moved += 512 * n * (len(terms) + 1)
@@ -119,7 +125,7 @@
     outs, place = refs[at:], extra
     added = sum(t[...].astype(f32) for t in refs[:extra]).astype(bf)
     for group, count, start, n in plan:
-        value = sum(t[...].reshape(t.shape[-2:]).astype(f32) for t in refs[place : place + count]).astype(bf)
+        value = sum(rows_part(t, start, n) for t in refs[place : place + count]).astype(bf)
         place += count
         for j in range(4):
 
@@ -140,13 +146,14 @@
         for terms in group:
             for term in terms:
                 a, which = term if isinstance(term, tuple) else (term, None)
-                n = a.shape[-1]
+                wide = a.shape[-1]
                 if which is None:
-                    args.append(a.reshape(-1, n))
-                    specs.append(pl.BlockSpec((rows, n), lambda i, me, g=g: ((me[g] + i) % 4, 0)))
+                    args.append(a.reshape(-1, wide))
+                    specs.append(pl.BlockSpec((rows, wide), lambda i, me, g=g: ((me[g] + i) % 4, 0)))
                 else:
-                    args.append(a.reshape(2, 4 * rows, n))
-                    specs.append(pl.BlockSpec((1, rows, n), lambda i, me, g=g, which=which: (which, (me[g] + i) % 4, 0)))
+                    args.append(a.reshape(2, 4 * rows, wide))
+                    specs.append(pl.BlockSpec((1, rows, wide), lambda i, me, g=g, which=which: (which, (me[g] + i) % 4, 0)))
+            n = terms[0].shape[-1]
             plan.append((g, len(terms), start, n))
             start += n
         dims = (rows + (32 if g == 0 else 0), start)
@@ -160,13 +167,25 @@
     return [out[4 * g : 4 * g + 4] for g in range(len(groups))]
 
 
-def sum_kernel(*refs):
-    for g in range(len(refs) // 5):
-        refs[4 * (len(refs) // 5) + g][...] = sum(t[...].astype(f32) for t in refs[4 * g : 4 * g + 4])
-
-
-def sums_of(groups):
-    return call(sum_kernel, tuple(shape(*g[0].shape) for g in groups))(*(a for g in groups for a in g))
+def final_kernel(x, *refs):
+    z, y, top = refs[:4], refs[4:8], refs[8]
+    outs = refs[9:]
+    groups = [sum(x[i].astype(f32) for i in range(16))]
+    groups += [sum(t[...].astype(f32) for t in g) for g in (z, y)]
+    outs[8][...] = groups[1][16:]
+    for out, g, lo, hi in ((0, 0, 0, 256), (1, 1, 0, 256), (2, 0, 256, 768), (3, 1, 256, 768), (4, 2, 0, 512)):
+        mine = groups[g].shape[1] - (512 if g == 2 else 768)
+        outs[out][0] = groups[g][:16, mine + lo : mine + hi]
+        outs[out][1] = groups[g][:16, lo:hi]
+    for g in range(3):
+        at = 512 if g == 2 else 768
+        outs[5 + g][0] = groups[g][:16, at : at + FF]
+        outs[5 + g][1] = top[:, g * FF : (g + 1) * FF].astype(f32)
+
+
+def final_sums(x, z, y, top):
+    widths = (256, 256, 512, 512, 512, FF, FF, FF)
+    return call(final_kernel, tuple(shape(2, 16, w) for w in widths) + (shape(32, z[0].shape[1]),))(x, *z, *y, top)
 
 
 def passed_on(blocks, axis):
@@ -195,8 +214,9 @@
     return pl.BlockSpec((1, *dims), lambda h: (h,) + (0,) * len(dims))
 
 
-def weight(width, place):
-    return [pl.BlockSpec((1, 512, width), lambda h: (h, 0, place))] * 2
+def weight(width, place, far_place=None):
+    far_place = place if far_place is None else far_place
+    return [pl.BlockSpec((1, 512, width), lambda h, p=p: (h, 0, p)) for p in (place, far_place)]
 
 
 def rms(v, gain):
@@ -244,12 +264,12 @@
         logits_out[...] = dot(latent, low_up[...], NN, highest) + bias[...]
 
 
-def proj(hn, low_down, low_up, bias, w, place):
+def proj(hn, low_down, low_up, bias, w, place, far_place):
     return call(
         proj_kernel,
         (shape(2, ROWS, 1536, dtype=bf), shape(ROWS, 16), shape(ROWS, 512)),
         grid=(2,),
-        in_specs=[whole(ROWS, D), whole(D, 16), whole(16, 512), whole(1, 512)] + weight(1536, place),
+        in_specs=[whole(ROWS, D), whole(D, 16), whole(16, 512), whole(1, 512)] + weight(1536, place, far_place),
         out_specs=[per_half(ROWS, 1536), whole(ROWS, 16), whole(ROWS, 512)],
         flops=4 * ROWS * D * 1536,
         moved=4 * D * 1536,
@@ -445,21 +465,21 @@
     )(d, d_logits, x, gain, g, low_up, low_down, order, *w)
 
 
-def select_kernel(a, sel, out):
-    out[0] = dot(a[...], sel[0], NT).astype(bf)
-
-
-def select(a, sel):
-    n = sel.shape[1]
+def select_kernel(*refs):
+    sel, out = refs[-2:]
+    for i, a in enumerate(refs[:-2]):
+        out[0, i] = dot(a[...], sel[0], NT).astype(bf)
+
+
+def select(arrays, sel):
+    n, count = sel.shape[1], len(arrays)
     both = call(
         select_kernel,
-        shape(2, ROWS, n, dtype=bf),
+        shape(2, count, ROWS, n, dtype=bf),
         grid=(2,),
-        in_specs=[whole(ROWS, D), per_half(n, D)],
-        out_specs=per_half(ROWS, n),
-        flops=4 * ROWS * D * n,
-        moved=4 * D * n,
-    )(a, sel)
+        in_specs=[whole(ROWS, D)] * count + [per_half(n, D)],
+        out_specs=per_half(count, ROWS, n),
+    )(*arrays, sel)
     return both, swap(both)
 
 
@@ -487,7 +507,7 @@
     for i in range(sets):
         a, ar, d, dr = refs[4 * i : 4 * i + 4]
         n = d.shape[-1]
-        r = (dot(a[0], d[0], TN) + dot(ar[0], dr[0], TN)).astype(bf)
+        r = (dot(a[0, 0], d[0], TN) + dot(ar[0, 0], dr[0], TN)).astype(bf)
         to = slice(at, at + n)
         part = lambda i: r[i * 128 : (i + 1) * 128].reshape(lead, 128 // lead, n)
         u[0, :, 0, :, to] = part(0)
@@ -497,15 +517,15 @@
         at += n
 
 
-def x_weight(group, *sets):
+def x_weight(group, selected, base, *sets):
     lead = (4, 1)[group]
     total, args, specs = 0, [], []
-    for (a, ar), d, dr in sets:
+    for i, (d, dr) in enumerate(sets, base):
         n = d.shape[-1] // 2
-        args += [a, ar, d, dr]
+        args += [*selected, d, dr]
         specs += [
-            pl.BlockSpec((1, ROWS, 512), lambda h: (0, 0, group)),
-            pl.BlockSpec((1, ROWS, 512), lambda h: (1, 0, group)),
+            pl.BlockSpec((1, 1, ROWS, 512), lambda h, i=i: (0, i, 0, group)),
+            pl.BlockSpec((1, 1, ROWS, 512), lambda h, i=i: (1, i, 0, group)),
         ]
         specs += [pl.BlockSpec((1, ROWS, n), lambda h: (h, 0, group))] * 2
         total += n
@@ -522,29 +542,30 @@
     )(*args)
 
 
-def y_weight_kernel(sets, where_, *refs):
+def y_weight_kernel(sets, base, where_, *refs):
     u, u1, u0 = refs[-3:]
     h, h2 = where_[0], where_[1]
     at = 0
     for i in range(sets):
-        a, ar, d, dr = refs[4 * i : 4 * i + 4]
+        a, ar = refs[:2]
+        d, dr = refs[2 * i + 2 : 2 * i + 4]
         n = d.shape[-1]
         to = slice(at, at + n)
-        near = lambda place: dot(a[0, :, :256], d[place], TN) + dot(ar[1, :, :256], dr[place], TN)
+        near = lambda place: dot(a[0, base + i, :, :256], d[place], TN) + dot(ar[1, base + i, :, :256], dr[place], TN)
         u0[:, to] = near(h).astype(bf)
         u[0, :, to] = near(1 - h).astype(bf)
-        r = (dot(a[0, :, 256:], d[h2], TN) + dot(ar[1, :, 256:], dr[h2], TN)).astype(bf)
+        r = (dot(a[0, base + i, :, 256:], d[h2], TN) + dot(ar[1, base + i, :, 256:], dr[h2], TN)).astype(bf)
         u1[:, to] = r[:256]
         u[1, :, to] = r[256:]
         at += n
 
 
-def y_weight(where_, *sets):
-    total = sum(d.shape[-1] for _, d, _ in sets)
-    args = [v for (a, ar), d, dr in sets for v in (a, ar, d, dr)]
+def y_weight(where_, selected, base, *sets):
+    total = sum(d.shape[-1] for d, _ in sets)
+    args = [*selected] + [v for pair in sets for v in pair]
     vm = pl.BlockSpec(memory_space=pltpu.VMEM)
     return call(
-        partial(y_weight_kernel, len(sets)),
+        partial(y_weight_kernel, len(sets), base),
         (shape(2, 256, total, dtype=bf), shape(256, total, dtype=bf), shape(256, total, dtype=bf)),
         in_specs=[pl.BlockSpec(memory_space=pltpu.SMEM)] + [vm] * len(args),
         out_specs=(vm,) * 3,
@@ -885,7 +906,7 @@
     along_x, along_z, along_y = (a.reshape(2, -1) for a in (along_x, along_z, along_y))
     sel_xz = one_hot(jnp.concatenate([along_x, along_z], axis=1).reshape(-1)).reshape(2, D, D)
     sel_y = one_hot(along_y.reshape(-1)).reshape(2, 768, D)
-    return base, sel_xz, sel_y, jnp.stack([yh, next_half]).astype(jnp.int32), jnp.stack([z, yh * 2 + yl, x, yh * 2 + yl, x, z]).astype(jnp.int32)
+    return base, sel_xz, sel_y, jnp.stack([yh, next_half]).astype(jnp.int32), jnp.stack([yh * 2 + yl, x, x, z]).astype(jnp.int32)
 
 
 def own_first(a, axis):
@@ -914,10 +935,6 @@
     pad = jnp.zeros((16, 128), bf)
     gathered = chip_gather(jnp.concatenate([*qkvg[0], *qkvg[1], out_w[0], out_w[1], pad, *feeds[0]], axis=1))
     gathered_late = chip_gather(jnp.concatenate(feeds[1], axis=1))
-    gathered = (gathered, swap(gathered))
-    attn_w = [(gathered, 0, 6), (gathered, 1, 7)]
-    feed_w = [(gathered, 1), None]
-
     order, sel_xz, sel_y, where_, me = orders()
     bounds = jnp.cumsum(lengths[0])
     places = jnp.arange(ROWS, dtype=jnp.int32) + yh * ROWS
@@ -927,12 +944,16 @@
     gains_in, gains_mid = own_first(norm_in, 1), own_first(norm_mid, 1)
     downs = own_first(low_down, 1)
 
-    order = after(order, sel_xz, sel_y, segr, segc)
     x, g, hn = entry(hidden_in, cotangent, valid[:, None], order, gains_in[:1])
+    gathered = after(gathered, x, sel_xz, sel_y, gains_in, gains_mid, downs, segr, segc, where_, me)
+    first_far = swap(gathered[:, :, :1536])
+    gathered = (gathered, swap(after(gathered, first_far)))
+    attn_w = [(gathered, 0, 6), (gathered, 1, 7)]
+    feed_w = [(gathered, 1), None]
     saved = []
     for layer in range(LAYERS):
         w, at_qkvg, at_out = attn_w[layer]
-        qkvg, latent, logits = proj(hn, downs[layer], low_up[layer], decay_bias[layer][None], w, at_qkvg)
+        qkvg, latent, logits = proj(hn, downs[layer], low_up[layer], decay_bias[layer][None], (w[0], first_far) if layer == 0 else w, at_qkvg, 0 if layer == 0 else at_qkvg)
         state = lax.ppermute(end_state(qkvg, logits, segr), "yh", [(0, 1)])
         local_mix, state_q = mix(qkvg, logits, segr, segc)
         mixed, rows, x_mid, hm = out_rows(
@@ -940,7 +961,11 @@
         )
         last = layer + 1 == LAYERS
         if last:
-            gathered_late = after(gathered_late, local_mix)
+            sel_a = select((hn, saved[0][10], saved[0][1]), sel_xz)
+            rows_far = [swap(saved[0][8]), swap(rows)]
+            acted_far = swap(saved[0][12])
+            hm = after(hm, sel_a, rows_far, acted_far)
+            gathered_late = after(gathered_late, hm)
             feed_w[1] = ((gathered_late, swap(gathered_late)), 0)
         if last:
             acted, d_pre, output, *back = ffn_both(hm, x_mid, order, g, gains_mid[layer : layer + 1], *feed_w[layer])
@@ -959,11 +984,15 @@
     def second_rings(t):
         return [ring(sixteens(v), a) for v, a in zip(t, "xzy")]
 
-    def last_terms(*parts):
-        return [[(u[i][2], r1[i], (swap(r[i]), 1)) for u, r, r1 in parts] for i in range(3)]
-
-    def weights(sets):
-        return [x_weight(0, *sets[0]), x_weight(1, *sets[1]), y_weight(where_, *sets[2])]
+    def small_grads(grad_in, grad_mid, hn, d_latent, latent, d_logits, d_gain):
+        return (
+            grad_in,
+            grad_mid,
+            dot(hn.astype(f32), d_latent, TN, highest),
+            dot(latent, d_logits, TN, highest),
+            jnp.sum(d_logits, axis=0),
+            jnp.sum(d_gain[:, 0], axis=0),
+        )
 
     def flatten(small):
         stacked = [jnp.stack([part[i] for part in small]) for i in range(6)]
@@ -981,99 +1010,70 @@
         if bottom:
             d_pre, *back = then(ffn_back, g, x_mid, gains_mid[layer : layer + 1], pre, *feed_w[layer])
         gb, g_mid, gm, grad_mid = back
-        d_pre_far, acted_far = swap(d_pre), swap(acted)
+        d_pre_far = swap(d_pre)
         d_g, d_gain, do, d_state = then(out_back, gm, mixed, qkvg, group_gain[layer][None], state_q, w, at_out)
         d_state = lax.ppermute(d_state, "yh", [(1, 0)])
         if bottom:
-            hm_s, gb_s = then(select, hm, sel_xz), then(select, gb, sel_y)
-            sets = (
-                ((hm_s, d_pre, d_pre_far),),
-                ((hm_s, d_pre, d_pre_far),),
-                ((gb_s, acted, acted_far),),
-            )
-            sets = tuple(p + q for p, q in zip(attn_sets, sets))
-            u = then(weights, sets)
-            r = rings(u)
+            sel_b = then(select, (gm_above, gb, gm), sel_y)
         else:
-            t = then(own_weight, hm, swap(hm), d_pre, d_pre_far, gb, swap(gb), acted, acted_far)
+            t = then(own_weight, hm, swap(hm), d_pre, d_pre_far, gb, swap(gb), acted, swap(acted))
             top = lax.psum_scatter(t.reshape(64, 16, 3 * FF), CHIPS, scatter_dimension=0, tiled=False)
         d_q, d_k, d_v, net = then(mix_back, do, qkvg, logits, segr, segc, state, state_q)
         d_k, d_v, d_logits = then(decay_back, d_k, d_v, net, qkvg, logits, segr, segc, d_state)
         d = jnp.concatenate([d_q, d_v, d_k, d_g], axis=2)
         d_far = swap(d)
-        hn_s, gm_s = then(select, hn, sel_xz), then(select, gm, sel_y)
-        attn_sets = (
-            ((hn_s, d, d_far),),
-            ((hn_s, d, d_far),),
-            ((gm_s, rows, swap(rows)),),
-        )
         if bottom:
-            u_last = then(weights, attn_sets)
-            r_last = rings(u_last)
-            t1 = then(second_terms, u, r)
-            r1 = second_rings(t1)
+            sets = (d_above, d_above_far), (d_pre, d_pre_far), (d, d_far)
+            u = [
+                then(lambda v: x_weight(0, sel_a, 0, *v), sets),
+                then(lambda v: x_weight(1, sel_a, 0, *v), sets),
+                then(lambda v: y_weight(where_, sel_b, 0, *v), ((rows_above, rows_far[1]), (acted, acted_far), (rows, rows_far[0]))),
+            ]
+            r = rings(u)
+        else:
+            d_above, d_above_far, gm_above, rows_above = d, d_far, gm, rows
         g, grad_in, d_latent = then(
             attn_back,
             d, d_logits, x, gains_in[layer : layer + 1], g_mid, low_up[layer], downs[layer].astype(f32), order, w, at_qkvg, bottom
         )
-        small[layer] = (
-            grad_in[0],
-            grad_mid[0],
-            dot(hn.astype(f32), d_latent, TN, highest),
-            dot(latent, d_logits, TN, highest),
-            jnp.sum(d_logits, axis=0),
-            jnp.sum(d_gain[:, 0], axis=0),
-        )
+        small[layer] = (grad_in[0], grad_mid[0], hn, d_latent, latent, d_logits, d_gain)
         if bottom:
-            stacked, flat = flatten(small)
+            stacked, flat = flatten([small_grads(*after(v, u)) for v in small])
             flat = flat + swap(flat)
             flat = flat.astype(bf)
-            flat = [flat] + [shift(flat, "x", j) for j in (1, 2, 3)]
-            t1_last = then(second_terms, u_last, after(r_last, flat[0]))
-            r1_last = second_rings(t1_last)
+            moved = [shift(flat, "z", j) for j in (1, 2, 3)]
+            r_far = [swap(v) for v in r]
+            t1 = then(second_terms, u, after(r, flat, r_far))
+            r1 = second_rings(t1)
     input_grad = g
 
-    parts = last_terms((u, r, r1), (u_last, r_last, r1_last))
-    parts = split_sums(me[:3], 64, parts, flat, 0)
-    parts = [passed_on(p, a) for p, a in zip(parts, "zyx")]
-    parts = split_sums(me[3:], 16, [[p] for p in parts], parts[0], 2)
-    parts = [passed_on(p, a) for p, a in zip(parts, "yxz")]
-    sums = dict(zip("xzy", sums_of(parts)))
-    total = sums["x"][16:].reshape(-1)
-    width = {"x": 768, "z": 768, "y": 512}
+    parts = [[(u[i][2], r1[i], (r_far[i], 1))] for i in range(3)]
+    (whole_x,) = add_each([(after(u[0][2], moved), r1[0], (r_far[0], 1))])
+    flat = [flat] + moved
+    got_x = lax.all_to_all(sixteens(whole_x), ("z", "yh", "yl"), 0, 0, tiled=True)
+    parts = split_sums(after(me[:2], whole_x), 64, parts[1:], flat, 0)
+    parts = [passed_on(p, a) for p, a in zip(parts, "yx")]
+    parts = after(parts, got_x)
+    parts = split_sums(me[2:], 16, [[p] for p in parts], parts[0], 2)
+    parts = [passed_on(p, a) for p, a in zip(parts, "xz")]
+    *grads, total = final_sums(got_x, parts[0], parts[1], top)
+    total = total.reshape(-1)
     small_sums, at = [], 0
     for a in stacked:
         small_sums.append(total[at : at + a.size].reshape(a.shape))
         at += a.size
-
-    width = {"x": 768, "z": 768, "y": 512}
-
-    def attn_part(group, lo, hi):
-        at = FF + width[group]
-        return jnp.stack([sums[group][:16, at + lo : at + hi], sums[group][:16, lo:hi]])
-
-    def feed_part(group):
-        at = width[group]
-        place = "xzy".index(group) * FF
-        return jnp.stack([sums[group][:16, at : at + FF], top[:, place : place + FF].astype(f32)])
 
     return (
         output,
         input_grad,
         small_sums[0],
         small_sums[1],
-        attn_part("x", 0, 256),
-        attn_part("z", 0, 256),
-        attn_part("x", 256, 768),
-        attn_part("z", 256, 768),
-        attn_part("y", 0, 512),
+        *grads[:5],
         small_sums[2],
         small_sums[3],
         small_sums[4],
         small_sums[5],
-        feed_part("x"),
-        feed_part("z"),
-        feed_part("y"),
+        *grads[5:],
     )
 
 

time: 611 us -> 578 us (0.946)
  starting transfers between devices: 73.7 us -> 53 us
  other arithmetic: 22.3 us -> 12.5 us
  Pallas kernels: 201 us -> 193 us
    ppermute x25 -> x19, waiting for transfers between devices: 14.1 us -> 41.3 us  [swap(): return lax.ppermute(a, 'c', [(0, 1), (1, 0)])]
    all_gather x2, waiting for transfers between devices: 112 us -> 91.6 us  [chip_gather(): lax.all_gather(s, CHIPS, axis=0, tiled=True).reshape(2, 512, s.shape[1])]
    ppermute x12 -> x6, waiting for transfers between devices: 37.7 us -> 21.9 us  [ring(): return lax.ppermute(a, names, pairs)]
    ppermute x15 -> x12, waiting for transfers between devices: 28.8 us -> 43.6 us  [shift(): return lax.ppermute(a, axis, [(i, (i + step) % 4) for i in range(4)])]
    ppermute x25 -> x19, starting transfers between devices: 16.3 us -> 4.1 us  [swap(): return lax.ppermute(a, 'c', [(0, 1), (1, 0)])]
    unnamed x309 -> x283, local copies, waits for them, and re-layouts: 49.9 us -> 58.5 us
    ppermute x15 -> x12, starting transfers between devices: 22.7 us -> 19.2 us  [shift(): return lax.ppermute(a, axis, [(i, (i + step) % 4) for i in range(4)])]
    pallas_call x4 -> x2, Pallas kernels: 16.9 us -> 14.7 us  [x_weight(): call(partial(x_weight_kernel, len(sets), lead), (shape(2, *dims, dtype=bf...]
  transfers between devices with their start and end apart: 65 -> 48, of which waited for: 31 -> 26; matrix products, arithmetic and copies ran while one was open for 8% -> 4% of each run, Pallas kernels for 30% -> 29%
where the time goes in v3:
time: 578 us; the launch traced here: 568 us
  waiting for transfers between devices  219 us (38%)
  Pallas kernels  193 us (33%)
  local copies, waits for them, and re-layouts  72.7 us (13%)
  starting transfers between devices  53 us (9%)
  between operations  15.9 us (3%)
  other arithmetic  12.5 us (2%)
    all_gather x2, waiting for transfers between devices, chip_gather(): lax.all_gather(s, CHIPS, axis=0, tiled=True).reshape(2, 512, s.shape[1])  91.6 us
    unnamed x283, local copies, waits for them, and re-layouts  58.5 us
    ppermute x12, waiting for transfers between devices, shift(): return lax.ppermute(a, axis, [(i, (i + step) % 4) for i in range(4)])  43.6 us
    ppermute x19, waiting for transfers between devices, swap(): return lax.ppermute(a, 'c', [(0, 1), (1, 0)])  41.3 us
    ppermute x6, waiting for transfers between devices, ring(): return lax.ppermute(a, names, pairs)  21.9 us
    ppermute x12, starting transfers between devices, shift(): return lax.ppermute(a, axis, [(i, (i + step) % 4) for i in range(4)])  19.2 us
    pallas_call x1, Pallas kernels, ffn_both(): call(ffn_both_kernel, (shape(2, ROWS, FF, dtype=bf), shape(2, ROWS, 2 * F...  19.1 us
    pallas_call x2, Pallas kernels, attn_back(): call(partial(attn_back_kernel, first), (shape(ROWS, D), shape(1, D), shap...  17.5 us
  transfers between devices with their start and end apart: 48, of which 26 were waited for; matrix products, arithmetic and copies ran while one was open for 4% of the time, Pallas kernels for 29%

profile of v3, /device:TPU:0, one launch (start us, length us, event | category | flops | bytes accessed | tf_op | source)
XLA Modules:
  0.0 567.9 jit_solution(12546806522934272840)
XLA Ops:
  34.1 91.6 %all-gather.3.cloned.1.call-done = bf16[1024,8448]{1,0:T(8,128)(2,1)} async-done(((bf16[16,8448]{1,0:T(8,128)(2,1)}), bf16[1024,8448]{1,0:T(8,128)(2,1)}) %all-gather.3.cloned.1.call-update) | async-done | bytes 17301520 | tf_op jit(solution)/shard_map/all_gather | solution.py:76
  128.0 5.6 collective-permute-done.wt
  168.0 11.1 %shard_map.311 = (bf16[2,256,2816]{2,1,0:T(8,128)(2,1)}, bf16[2,256,1408]{2,1,0:T(8,128)(2,1)}, f32[256,1024]{1,0:T(8,128)S(1)}, bf16[256,1024]{1,0:T(8,128)(2,1)S(1)}) custom-call(bf16[256,1024]{1,0:T(8,128)(2,1)S(1)} %get-tuple-element.190.hm.refs_1_, f32[256,1024]{1,0:T(8,128)S(1)} %get-tuple-element.191.x, f32[1,1024]{1,0:T(1,128)S(1)} %get-tuple-element.452.gain, ...), custom_call_target="tpu_custom_call" | custom-call | flops 4429185024 | bytes 17301504 | tf_op jit(solution)/shard_map/pallas_call | solution.py:302
  180.1 6.7 %shard_map.316.refs_0_.refs_4_.refs_8_ = bf16[2,3,256,1024]{3,2,1,0:T(8,128)(2,1)} custom-call(bf16[256,1024]{1,0:T(8,128)(2,1)S(1)} %get-tuple-element.295.hn.refs_0_, bf16[256,1024]{1,0:T(8,128)(2,1)S(1)} %get-tuple-element.190.hm.refs_1_, bf16[256,1024]{1,0:T(8,128)(2,1)S(1)} %get-tuple-element.293.hn.refs_2_, bf16[2,1024,1024]{2,1,0:T(8,128)(2,1)} %fusion.refs_3_), custom_call_target="tpu_custom_call" | custom-call | flops 500000000 | bytes 8000000 | tf_op jit(solution)/shard_map/pallas_call | solution.py:476
  209.4 6.4 %collective-permute-done.3.state.state_in = bf16[4,128,256]{2,1,0:T(8,128)(2,1)S(1)} collective-permute-done((bf16[4,128,256]{2,1,0:T(8,128)(2,1)S(1)}, bf16[4,128,256]{2,1,0:T(8,128)(2,1)S(1)}, u32[]{:S(2)}, u32[]{:S(2)}) %collective-permute-start.3) | collective-permute-done | bytes 262176 | tf_op jit(solution)/shard_map/ppermute | solution.py:957
  226.7 13.5 %collective-permute-done.8.wt = bf16[2,512,4224]{2,1,0:T(8,128)(2,1)S(1)} collective-permute-done((bf16[2,512,4224]{2,1,0:T(8,128)(2,1)}, bf16[2,512,4224]{2,1,0:T(8,128)(2,1)S(1)}, u32[]{:S(2)}, u32[]{:S(2)}) %collective-permute-start.8) | collective-permute-done | bytes 8650784 | tf_op jit(solution)/shard_map/ppermute | solution.py:52
  247.1 19.1 %shard_map.317 = (bf16[2,256,1408]{2,1,0:T(8,128)(2,1)S(1)}, bf16[2,256,2816]{2,1,0:T(8,128)(2,1)}, f32[256,1024]{1,0:T(8,128)}, bf16[256,1024]{1,0:T(8,128)(2,1...) custom-call(bf16[256,1024]{1,0:T(8,128)(2,1)S(1)} %copy-done.59, ...), custom_call_target="tpu_custom_call" | custom-call | flops 8858370048 | bytes 17301504 | tf_op jit(solution)/shard_map/pallas_call | solution.py:357
  276.0 8.9 %shard_map.319 = bf16[2,512,4224]{2,1,0:T(8,128)(2,1)} custom-call(bf16[256,1024]{1,0:T(8,128)(2,1)S(1)} %copy-done.60, bf16[256,1024]{1,0:T(8,128)(2,1)S(1)} %collective-permute-done.9.ar, bf16[256,1024]{1,0:T(8,128)(2,1)S(1)} %get-tuple-element.214.b, bf16[256,1024]{1,0:T(8,128)(2,1)S(1)} %collective-permute-done.10.br, ...), custom_call_target="tpu_custom_call" | custom-call | flops 500000000 | bytes 8000000 | tf_op jit(solution)/shard_map/pallas_call | solution.py:495
  288.8 7.5 %shard_map.320 = (bf16[2,256,256]{2,1,0:T(8,128)(2,1)S(1)}, f32[4,256,128]{2,1,0:T(8,128)S(1)}, f32[4,256,256]{2,1,0:T(8,128)S(1)}, f32[4,256,128]{2,1,0:T(8,128)S(1)}) custom-call(bf16[2,256,512]{2,1,0:T(8,128)(2,1)S(1)} %copy-done.64, bf16[2,256,1536]{2,1,0:T(8,128)(2,1)S(1)} %copy-done.3, bf16[2,256,1536]{2,1,0:T(8,128)(2,1)S(1)} %copy-done.3, ...), custom_call_target="tpu_custom_call" | custom-call | flops 1200000000 | bytes 8000000 | tf_op jit(solution)/shard_map/pallas_call | solution.py:807
  297.3 6.4 %shard_map.321 = (bf16[2,256,256]{2,1,0:T(8,128)(2,1)S(1)}, bf16[2,256,512]{2,1,0:T(8,128)(2,1)S(1)}, f32[256,512]{1,0:T(8,128)S(1)}) custom-call(f32[4,256,128]{2,1,0:T(8,128)S(1)} %get-tuple-element.222.dk_in, f32[4,256,256]{2,1,0:T(8,128)S(1)} %get-tuple-element.220.dv_in, f32[4,256,128]{2,1,0:T(8,128)S(1)} %get-tuple-element.221.net, ...), custom_call_target="tpu_custom_call" | custom-call | flops 400000000 | bytes 4000000 | tf_op jit(solution)/shard_map/pallas_call | solution.py:854
  305.2 7.4 %shard_map.322 = (f32[256,1024]{1,0:T(8,128)S(1)}, f32[1,1024]{1,0:T(1,128)S(1)}, f32[256,16]{1,0:T(8,128)S(1)}) custom-call(bf16[2,256,1536]{2,1,0:T(8,128)(2,1)S(1)} %constant_dynamic-update-slice_fusion.20.d.refs_2_, f32[256,512]{1,0:T(8,128)S(1)} %get-tuple-element.300.d_logits, f32[256,1024]{1,0:T(8,128)S(1)} %copy-done.19, ...), custom_call_target="tpu_custom_call" | custom-call | flops 1610612736 | bytes 6291456 | tf_op jit(solution)/shard_map/pallas_call | solution.py:452
  313.2 11.7 %shard_map.323 = (bf16[2,256,2816]{2,1,0:T(8,128)(2,1)}, bf16[256,1024]{1,0:T(8,128)(2,1)S(1)}, f32[256,1024]{1,0:T(8,128)S(1)}, bf16[256,1024]{1,0:T(8,128)(2,1)S(1)}, f32[1,1024]{1,0:T(1,128)S(1)}) custom-call(f32[256,1024]{1,0:T(8,128)S(1)} %get-tuple-element.228.g, f32[256,1024]{1,0:T(8,128)S(1)} %copy-done.16, ...), custom_call_target="tpu_custom_call" | custom-call | flops 4429185024 | bytes 17301504 | tf_op jit(solution)/shard_map/pallas_call | solution.py:414
  341.1 7.5 %shard_map.326 = (bf16[2,256,256]{2,1,0:T(8,128)(2,1)S(1)}, f32[4,256,128]{2,1,0:T(8,128)S(1)}, f32[4,256,256]{2,1,0:T(8,128)S(1)}, f32[4,256,128]{2,1,0:T(8,128)S(1)}) custom-call(bf16[2,256,512]{2,1,0:T(8,128)(2,1)S(1)} %get-tuple-element.244.do_in, bf16[2,256,1536]{2,1,0:T(8,128)(2,1)S(1)} %copy-done.1, bf16[2,256,1536]{2,1,0:T(8,128)(2,1)S(1)} %copy-done.1, ...), custom_call_target="tpu_custom_call" | custom-call | flops 1200000000 | bytes 8000000 | tf_op jit(solution)/shard_map/pallas_call | solution.py:807
  348.6 6.4 %shard_map.327 = (bf16[2,256,256]{2,1,0:T(8,128)(2,1)S(1)}, bf16[2,256,512]{2,1,0:T(8,128)(2,1)S(1)}, f32[256,512]{1,0:T(8,128)S(1)}) custom-call(f32[4,256,128]{2,1,0:T(8,128)S(1)} %get-tuple-element.249.dk_in, f32[4,256,256]{2,1,0:T(8,128)S(1)} %get-tuple-element.247.dv_in, f32[4,256,128]{2,1,0:T(8,128)S(1)} %get-tuple-element.248.net, ...), custom_call_target="tpu_custom_call" | custom-call | flops 400000000 | bytes 4000000 | tf_op jit(solution)/shard_map/pallas_call | solution.py:854
  359.8 7.1 %shard_map.328 = (bf16[2,4,2,32,2944]{4,3,2,1,0:T(8,128)(2,1)}, bf16[4,2,32,2944]{3,2,1,0:T(8,128)(2,1)S(1)}, bf16[4,2,32,2944]{3,2,1,0:T(8,128)(2,1)S(1)}) custom-call(bf16[2,3,256,1024]{3,2,1,0:T(8,128)(2,1)} %shard_map.316.refs_0_.refs_4_.refs_8_, bf16[2,3,256,1024]{3,2,1,0:T(8,128)(2,1)} %collective-permute-done.4.refs_1_.refs_5_.refs_9_, ...), custom_call_target="tpu_custom_call" | custom-call | flops 3087007744 | bytes 6029312 | tf_op jit(solution)/shard_map/pallas_call | solution.py:533
  368.1 7.6 %shard_map.329 = (bf16[2,1,2,128,2944]{4,3,2,1,0:T(8,128)(2,1)}, bf16[1,2,128,2944]{3,2,1,0:T(8,128)(2,1)S(1)}, bf16[1,2,128,2944]{3,2,1,0:T(8,128)(2,1)S(1)}) custom-call(bf16[2,3,256,1024]{3,2,1,0:T(8,128)(2,1)} %shard_map.316.refs_0_.refs_4_.refs_8_, bf16[2,3,256,1024]{3,2,1,0:T(8,128)(2,1)} %collective-permute-done.4.refs_1_.refs_5_.refs_9_, ...), custom_call_target="tpu_custom_call" | custom-call | flops 3087007744 | bytes 6029312 | tf_op jit(solution)/shard_map/pallas_call | solution.py:533
  379.6 7.8 %shard_map.330 = (bf16[2,256,2432]{2,1,0:T(8,128)(2,1)}, bf16[256,2432]{1,0:T(8,128)(2,1)S(1)}, bf16[256,2432]{1,0:T(8,128)(2,1)S(1)}) custom-call(s32[2]{0:T(128)S(1)} %copy-done.105, bf16[2,3,256,768]{3,2,1,0:T(8,128)(2,1)} %copy-done.7, bf16[2,3,256,768]{3,2,1,0:T(8,128)(2,1)} %collective-permute-done.14.refs_1_, bf16[2,256,512]{2,1,0:T(8,128)(2,1)S(1)} %copy-done.55, ...), custom_call_target="tpu_custom_call" | custom-call | flops 2550136832 | bytes 4980736 | tf_op jit(solution)/shard_map/pallas_call | solution.py:567
  390.4 10.2 %shard_map.331 = (f32[256,1024]{1,0:T(8,128)}, f32[1,1024]{1,0:T(1,128)S(1)}, f32[256,16]{1,0:T(8,128)S(1)}) custom-call(bf16[2,256,1536]{2,1,0:T(8,128)(2,1)S(1)} %copy-done.6, f32[256,512]{1,0:T(8,128)S(1)} %get-tuple-element.298.d_logits, f32[256,1024]{1,0:T(8,128)S(1)} %copy-done.14, f32[1,1024]{1,0:T(1,128)S(1)} %copy-done.93, ...), custom_call_target="tpu_custom_call" | custom-call | flops 1610612736 | bytes 6291456 | tf_op jit(solution)/shard_map/pallas_call | solution.py:452
  402.3 19.0 %collective-permute-done.24 = bf16[2,16,16,2944]{3,2,1,0:T(8,128)(2,1)} collective-permute-done((bf16[2,16,16,2944]{3,2,1,0:T(8,128)(2,1)}, bf16[2,16,16,2944]{3,2,1,0:T(8,128)(2,1)}, u32[]{:S(2)}, u32[]{:S(2)}) %collective-permute-start.24) | collective-permute-done | bytes 3014688 | tf_op jit(solution)/shard_map/ppermute | solution.py:65
  447.7 25.5 %collective-permute-done.20.refs_1_ = bf16[32,2944]{1,0:T(8,128)(2,1)S(1)} collective-permute-done((bf16[32,2944]{1,0:T(8,128)(2,1)S(1)}, bf16[32,2944]{1,0:T(8,128)(2,1)S(1)}, u32[]{:S(2)}, u32[]{:S(2)}) %collective-permute-start.20) | collective-permute-done | bytes 188448 | tf_op jit(solution)/shard_map/ppermute | solution.py:72
  482.7 5.8 %all-to-all-start = ((bf16[16,16,2944]{2,1,0:T(8,128)(2,1)}), bf16[16,16,2944]{2,1,0:T(8,128)(2,1)S(1)}, u32[]{:S(2)}, u32[]{:S(2)}) async-start(bf16[16,16,2944]{2,1,0:T(8,128)(2,1)} %bitcast.66), calls=%async_computation | async-start | bytes 3014656 | tf_op jit(solution)/shard_map/all_to_all | solution.py:1053
  507.7 5.7 collective-permute-done.36.refs_10_
  517.3 5.8 %collective-permute-done.32.refs_1_.refs_5_ = bf16[96,2944]{1,0:T(8,128)(2,1)S(1)} collective-permute-done((bf16[96,2944]{1,0:T(8,128)(2,1)S(1)}, bf16[96,2944]{1,0:T(8,128)(2,1)S(1)}, u32[]{:S(2)}, u32[]{:S(2)}) %collective-permute-start.32) | collective-permute-done | bytes 565280 | tf_op jit(solution)/shard_map/ppermute | solution.py:71
  523.1 7.0 %collective-permute-done.33.refs_2_.refs_6_ = bf16[96,2944]{1,0:T(8,128)(2,1)S(1)} collective-permute-done((bf16[96,2944]{1,0:T(8,128)(2,1)S(1)}, bf16[96,2944]{1,0:T(8,128)(2,1)S(1)}, u32[]{:S(2)}, u32[]{:S(2)}) %collective-permute-start.33) | collective-permute-done | bytes 565280 | tf_op jit(solution)/shard_map/ppermute | solution.py:71
  (492 shorter events, 240.8 us)
Async XLA Ops:
  7.2 118.5 %all-gather.3.cloned.1.call-start = ((), (), s32[]{:S(2)}) async-start(), calls=%async_computation.2 | async-start | bytes 17571840 | tf_op jit(solution)/shard_map/all_gather | solution.py:76
  17.5 208.6 %all-gather.5.cloned.1.call-start = ((), (), s32[]{:S(2)}) async-start(), calls=%async_computation.3 | async-start | bytes 8785920 | tf_op jit(solution)/shard_map/all_gather | solution.py:76
  135.2 26.2 %collective-permute-start.2 = (bf16[2,512,8448]{2,1,0:T(8,128)(2,1)}, bf16[2,512,8448]{2,1,0:T(8,128)(2,1)}, u32[]{:S(2)}, u32[]{:S(2)}) collective-permute-start(bf16[2,512,8448]{2,1,0:T(8,128)(2,1)} %bitcast.150), channel_id=1, source_target_pairs={{0,2},{2,0},{1,3},{3,1},{4,6},{6,4},{5,7},{7,5},{8,10},{10,8},{9,1... | collective-permute-start | bytes 51904520 | tf_op jit(solution)/shard_map/ppermute | solution.py:52
  136.1 416.9 %reduce-scatter.2.cloned.1.call-start = ((), (), s32[]{:S(2)}) async-start(), calls=%async_computation.4 | async-start | bytes 8785920 | tf_op jit(solution)/shard_map/reduce_scatter | solution.py:1020
  186.8 39.3 %collective-permute-start.4 = (bf16[2,3,256,1024]{3,2,1,0:T(8,128)(2,1)}, bf16[2,3,256,1024]{3,2,1,0:T(8,128)(2,1)}, u32[]{:S(2)}, u32[]{:S(2)}) collective-permute-start(bf16[2,3,256,1024]{3,2,1,0:T(8,128)(2,1)} %shard_map.316.refs_0_.refs_4_.refs_8_), channel_id=1, source_target_pairs={{0,2},{2,0},{1,3},{3,1},{4,6},{6,4},{5,7},{7,5},{8,10},{10,8},{9,1... | collective-permute-start | bytes 9437192 | tf_op jit(solution)/shard_map/ppermute | solution.py:52
  186.9 39.2 %collective-permute-start.7 = (bf16[2,256,1408]{2,1,0:T(8,128)(2,1)}, bf16[2,256,1408]{2,1,0:T(8,128)(2,1)}, u32[]{:S(2)}, u32[]{:S(2)}) collective-permute-start(bf16[2,256,1408]{2,1,0:T(8,128)(2,1)} %get-tuple-element.273.refs_4_), channel_id=1, source_target_pairs={{0,2},{2,0},{1,3},{3,1},{4,6},{6,4},{5,7},{7,5},{8,10},{10,8},{9,1... | collective-permute-start | bytes 4325384 | tf_op jit(solution)/shard_map/ppermute | solution.py:52
  198.8 17.0 %collective-permute-start.3 = (bf16[4,128,256]{2,1,0:T(8,128)(2,1)S(1)}, bf16[4,128,256]{2,1,0:T(8,128)(2,1)S(1)}, u32[]{:S(2)}, u32[]{:S(2)}) collective-permute-start(bf16[4,128,256]{2,1,0:T(8,128)(2,1)S(1)} %shard_map.314), channel_id=1, source_target_pairs={{0,1},{2,3},{4,5},{6,7},{8,9},{10,11},{12,13},{14,15},{16,17},{18,... | collective-permute-start | bytes 786440 | tf_op jit(solution)/shard_map/ppermute | solution.py:957
  203.9 20.3 %collective-permute-start.5 = (bf16[2,256,512]{2,1,0:T(8,128)(2,1)S(1)}, bf16[2,256,512]{2,1,0:T(8,128)(2,1)S(1)}, u32[]{:S(2)}, u32[]{:S(2)}) collective-permute-start(bf16[2,256,512]{2,1,0:T(8,128)(2,1)S(1)} %copy-done.50), channel_id=1, source_target_pairs={{0,2},{2,0},{1,3},{3,1},{4,6},{6,4},{5,7},{7,5},{8,10},{10,8},{9,1... | collective-permute-start | bytes 1572872 | tf_op jit(solution)/shard_map/ppermute | solution.py:52
  334.0 21.4 %collective-permute-start.17 = (bf16[2,256,2816]{2,1,0:T(8,128)(2,1)}, bf16[2,256,2816]{2,1,0:T(8,128)(2,1)}, u32[]{:S(2)}, u32[]{:S(2)}) collective-permute-start(bf16[2,256,2816]{2,1,0:T(8,128)(2,1)} %get-tuple-element.264.refs_6_), channel_id=1, source_target_pairs={{0,2},{2,0},{1,3},{3,1},{4,6},{6,4},{5,7},{7,5},{8,10},{10,8},{9,1... | collective-permute-start | bytes 8650760 | tf_op jit(solution)/shard_map/ppermute | solution.py:52
  335.8 19.6 %collective-permute-start.16 = (bf16[2,256,1536]{2,1,0:T(8,128)(2,1)S(1)}, bf16[2,256,1536]{2,1,0:T(8,128)(2,1)S(1)}, u32[]{:S(2)}, u32[]{:S(2)}) collective-permute-start(bf16[2,256,1536]{2,1,0:T(8,128)(2,1)S(1)} %constant_dynamic-update-slice_fusion.20.d.refs_2_), channel_id=1, source_target_pairs={{0,2},{2,0},{1,3},{3,1},{4,6},{6,4},{5,7},{7,5},{8,10},{10,8},{9,1... | collective-permute-start | bytes 4718600 | tf_op jit(solution)/shard_map/ppermute | solution.py:52
  378.0 43.2 %collective-permute-start.24 = (bf16[2,16,16,2944]{3,2,1,0:T(8,128)(2,1)}, bf16[2,16,16,2944]{3,2,1,0:T(8,128)(2,1)}, u32[]{:S(2)}, u32[]{:S(2)}) collective-permute-start(bf16[2,16,16,2944]{3,2,1,0:T(8,128)(2,1)} %bitcast.174), channel_id=1, source_target_pairs={{0,4},{2,14},{4,8},{6,2},{8,12},{10,6},{12,0},{14,10},{1,5},{3,15}... | collective-permute-start | bytes 9043976 | tf_op jit(solution)/shard_map/ppermute | solution.py:65
  379.5 43.1 %collective-permute-start.23 = (bf16[2,16,16,2944]{3,2,1,0:T(8,128)(2,1)}, bf16[2,16,16,2944]{3,2,1,0:T(8,128)(2,1)}, u32[]{:S(2)}, u32[]{:S(2)}) collective-permute-start(bf16[2,16,16,2944]{3,2,1,0:T(8,128)(2,1)} %bitcast.173), channel_id=1, source_target_pairs={{0,16},{2,50},{16,32},{18,2},{32,48},{34,18},{48,0},{50,34},{1,17}... | collective-permute-start | bytes 9043976 | tf_op jit(solution)/shard_map/ppermute | solution.py:65
  389.5 36.8 %collective-permute-start.25 = (bf16[2,16,16,2432]{3,2,1,0:T(8,128)(2,1)}, bf16[2,16,16,2432]{3,2,1,0:T(8,128)(2,1)}, u32[]{:S(2)}, u32[]{:S(2)}) collective-permute-start(bf16[2,16,16,2432]{3,2,1,0:T(8,128)(2,1)} %bitcast.175), channel_id=1, source_target_pairs={{0,64},{2,67},{64,1},{66,2},{1,65},{3,66},{65,0},{67,3},{4,68},{6,... | collective-permute-start | bytes 7471112 | tf_op jit(solution)/shard_map/ppermute | solution.py:65
  421.2 14.2 %collective-permute-start.27 = (bf16[2,16,16,2944]{3,2,1,0:T(8,128)(2,1)}, bf16[2,16,16,2944]{3,2,1,0:T(8,128)(2,1)}, u32[]{:S(2)}, u32[]{:S(2)}) collective-permute-start(bf16[2,16,16,2944]{3,2,1,0:T(8,128)(2,1)} %collective-permute-done.24), channel_id=1, source_target_pairs={{0,2},{2,0},{1,3},{3,1},{4,6},{6,4},{5,7},{7,5},{8,10},{10,8},{9,1... | collective-permute-start | bytes 9043976 | tf_op jit(solution)/shard_map/ppermute | solution.py:52
  440.9 37.9 %collective-permute-start.29 = (bf16[16,16,2944]{2,1,0:T(8,128)(2,1)S(1)}, bf16[16,16,2944]{2,1,0:T(8,128)(2,1)S(1)}, u32[]{:S(2)}, u32[]{:S(2)}) collective-permute-start(bf16[16,16,2944]{2,1,0:T(8,128)(2,1)S(1)} %bitcast.148), channel_id=1, source_target_pairs={{0,16},{2,50},{16,32},{18,2},{32,48},{34,18},{48,0},{50,34},{1,17}... | collective-permute-start | bytes 4521992 | tf_op jit(solution)/shard_map/ppermute | solution.py:65
  442.3 46.2 %collective-permute-start.30 = (bf16[16,16,2944]{2,1,0:T(8,128)(2,1)}, bf16[16,16,2944]{2,1,0:T(8,128)(2,1)}, u32[]{:S(2)}, u32[]{:S(2)}) collective-permute-start(bf16[16,16,2944]{2,1,0:T(8,128)(2,1)} %bitcast.69), channel_id=1, source_target_pairs={{0,4},{2,14},{4,8},{6,2},{8,12},{10,6},{12,0},{14,10},{1,5},{3,15}... | collective-permute-start | bytes 4521992 | tf_op jit(solution)/shard_map/ppermute | solution.py:65
  442.3 46.2 %collective-permute-start.31 = (bf16[16,16,2432]{2,1,0:T(8,128)(2,1)}, bf16[16,16,2432]{2,1,0:T(8,128)(2,1)}, u32[]{:S(2)}, u32[]{:S(2)}) collective-permute-start(bf16[16,16,2432]{2,1,0:T(8,128)(2,1)} %bitcast.72), channel_id=1, source_target_pairs={{0,64},{2,67},{64,1},{66,2},{1,65},{3,66},{65,0},{67,3},{4,68},{6,... | collective-permute-start | bytes 3735560 | tf_op jit(solution)/shard_map/ppermute | solution.py:65
  443.0 30.2 %collective-permute-start.20 = (bf16[32,2944]{1,0:T(8,128)(2,1)S(1)}, bf16[32,2944]{1,0:T(8,128)(2,1)S(1)}, u32[]{:S(2)}, u32[]{:S(2)}) collective-permute-start(bf16[32,2944]{1,0:T(8,128)(2,1)S(1)} %add_convert_fusion.refs_0_), channel_id=1, source_target_pairs={{0,4},{4,8},{8,12},{12,0},{1,5},{5,9},{9,13},{13,1},{2,6},{6,10},{... | collective-permute-start | bytes 565256 | tf_op jit(solution)/shard_map/ppermute | solution.py:72
  443.5 29.7 %collective-permute-start.21 = (bf16[32,2944]{1,0:T(8,128)(2,1)S(1)}, bf16[32,2944]{1,0:T(8,128)(2,1)S(1)}, u32[]{:S(2)}, u32[]{:S(2)}) collective-permute-start(bf16[32,2944]{1,0:T(8,128)(2,1)S(1)} %add_convert_fusion.refs_0_), channel_id=1, source_target_pairs={{0,8},{4,12},{8,0},{12,4},{1,9},{5,13},{9,1},{13,5},{2,10},{6,14},... | collective-permute-start | bytes 565256 | tf_op jit(solution)/shard_map/ppermute | solution.py:72
  482.7 48.3 %all-to-all-start = ((bf16[16,16,2944]{2,1,0:T(8,128)(2,1)}), bf16[16,16,2944]{2,1,0:T(8,128)(2,1)S(1)}, u32[]{:S(2)}, u32[]{:S(2)}) async-start(bf16[16,16,2944]{2,1,0:T(8,128)(2,1)} %bitcast.66), calls=%async_computation | async-start | bytes 3014656 | tf_op jit(solution)/shard_map/all_to_all | solution.py:1053
  498.7 24.4 %collective-permute-start.32 = (bf16[96,2944]{1,0:T(8,128)(2,1)S(1)}, bf16[96,2944]{1,0:T(8,128)(2,1)S(1)}, u32[]{:S(2)}, u32[]{:S(2)}) collective-permute-start(bf16[96,2944]{1,0:T(8,128)(2,1)S(1)} %get-tuple-element.315), channel_id=1, source_target_pairs={{0,64},{64,1},{1,65},{65,0},{2,66},{66,3},{3,67},{67,2},{4,68},{68... | collective-permute-start | bytes 1695752 | tf_op jit(solution)/shard_map/ppermute | solution.py:71
  500.8 29.4 %collective-permute-start.33 = (bf16[96,2944]{1,0:T(8,128)(2,1)S(1)}, bf16[96,2944]{1,0:T(8,128)(2,1)S(1)}, u32[]{:S(2)}, u32[]{:S(2)}) collective-permute-start(bf16[96,2944]{1,0:T(8,128)(2,1)S(1)} %get-tuple-element.316), channel_id=1, source_target_pairs={{0,1},{64,65},{1,0},{65,64},{2,3},{66,67},{3,2},{67,66},{4,5},{68,... | collective-permute-start | bytes 1695752 | tf_op jit(solution)/shard_map/ppermute | solution.py:71
  503.4 26.7 %collective-permute-start.34 = (bf16[96,2944]{1,0:T(8,128)(2,1)S(1)}, bf16[96,2944]{1,0:T(8,128)(2,1)S(1)}, u32[]{:S(2)}, u32[]{:S(2)}) collective-permute-start(bf16[96,2944]{1,0:T(8,128)(2,1)S(1)} %get-tuple-element.317), channel_id=1, source_target_pairs={{0,65},{64,0},{1,64},{65,1},{2,67},{66,2},{3,66},{67,3},{4,69},{68... | collective-permute-start | bytes 1695752 | tf_op jit(solution)/shard_map/ppermute | solution.py:71
  538.0 14.9 %collective-permute-start.38 = (bf16[48,2944]{1,0:T(8,128)(2,1)S(1)}, bf16[48,2944]{1,0:T(8,128)(2,1)S(1)}, u32[]{:S(2)}, u32[]{:S(2)}) collective-permute-start(bf16[48,2944]{1,0:T(8,128)(2,1)S(1)} %get-tuple-element.331), channel_id=1, source_target_pairs={{0,16},{16,32},{32,48},{48,0},{1,17},{17,33},{33,49},{49,1},{2,18}... | collective-permute-start | bytes 847880 | tf_op jit(solution)/shard_map/ppermute | solution.py:72
  (149 other events, 1126.8 us)
Sparse Core Ops, SparseCore 0:
  17.6 108.0 all-gather.2
  136.2 85.9 all-gather.4
  285.0 245.9 reduce-scatter.1

commit v4 on v3

--- a/solution.py
+++ b/solution.py
@@ -34,12 +34,12 @@
     return lax.dot_general(a, b, dims, precision=precision, preferred_element_type=f32)
 
 
-def call(kernel, out_shape, *, flops=0, moved=0, vmem=48, **kw):
+def call(kernel, out_shape, *, flops=500_000_000, moved=8_000_000, vmem=48, **kw):
     return pl.pallas_call(
         kernel,
         out_shape=out_shape,
         compiler_params=pltpu.CompilerParams(vmem_limit_bytes=vmem << 20),
-        cost_estimate=pl.CostEstimate(flops=flops or 500_000_000, bytes_accessed=moved or 8_000_000, transcendentals=0),
+        cost_estimate=pl.CostEstimate(flops=flops, bytes_accessed=moved, transcendentals=0),
         **kw,
     )
 
@@ -52,7 +52,7 @@
     return lax.ppermute(a, "c", [(0, 1), (1, 0)])
 
 
-def ring(a, axis):
+def ring(a, axis, cross=0):
     if axis == "y":
         names = ("yl", "c", "yh")
         place = lambda i, c: ((i % 2) * 2 + c) * 2 + i // 2
@@ -60,7 +60,7 @@
         names = (axis, "c")
         place = lambda i, c: i * 2 + c
     pairs = [
-        (place(i, c), place((i + 1 - 2 * c) % 4, c)) for i in range(4) for c in range(2)
+        (place(i, c), place((i + 1 - 2 * c) % 4, c ^ cross)) for i in range(4) for c in range(2)
     ]
     return lax.ppermute(a, names, pairs)
 
@@ -115,7 +115,7 @@
         outs.append(shape(256, start, dtype=bf))
         out_specs.append(pl.BlockSpec((64, start), lambda i: (i, 0)))
     return call(
-        partial(add_kernel, plan), tuple(outs), grid=(4,), in_specs=specs, out_specs=out_specs, flops=moved, moved=moved
+        partial(add_kernel, plan), tuple(outs), grid=(4,), in_specs=specs, out_specs=out_specs, flops=0, moved=0
     )(*args)
 
 
@@ -162,6 +162,8 @@
     out = call(
         partial(split_kernel, plan, rows, len(extra)),
         tuple(outs),
+        flops=0,
+        moved=0,
         grid_spec=pltpu.PrefetchScalarGridSpec(num_scalar_prefetch=1, grid=(4,), in_specs=specs, out_specs=out_specs),
     )(me, *args)
     return [out[4 * g : 4 * g + 4] for g in range(len(groups))]
@@ -460,8 +462,8 @@
         + weight(1536, place),
         out_specs=[whole(ROWS, D), whole(1, D), whole(ROWS, 16)],
         scratch_shapes=[pltpu.VMEM((ROWS, D), f32)],
-        flops=4 * ROWS * D * 1536,
-        moved=4 * D * 1536,
+        flops=0 if first else 4 * ROWS * D * 1536,
+        moved=0 if first else 4 * D * 1536,
     )(d, d_logits, x, gain, g, low_up, low_down, order, *w)
 
 
@@ -502,7 +504,7 @@
 
 
 def x_weight_kernel(sets, lead, *refs):
-    u, u1, u0 = refs[-3:]
+    outs = refs[-4:]
     at = 0
     for i in range(sets):
         a, ar, d, dr = refs[4 * i : 4 * i + 4]
@@ -510,10 +512,8 @@
         r = (dot(a[0, 0], d[0], TN) + dot(ar[0, 0], dr[0], TN)).astype(bf)
         to = slice(at, at + n)
         part = lambda i: r[i * 128 : (i + 1) * 128].reshape(lead, 128 // lead, n)
-        u[0, :, 0, :, to] = part(0)
-        u[1, :, 0, :, to] = part(1)
-        u1[:, 0, :, to] = part(2)
-        u0[:, 0, :, to] = part(3)
+        for k, out in enumerate(outs):
+            out[:, 0, :, to] = part(k)
         at += n
 
 
@@ -532,18 +532,17 @@
     dims = (lead, 2, 128 // lead, total)
     return call(
         partial(x_weight_kernel, len(sets), lead),
-        (shape(2, *dims, dtype=bf), shape(*dims, dtype=bf), shape(*dims, dtype=bf)),
+        (shape(*dims, dtype=bf),) * 4,
         grid=(2,),
         in_specs=specs,
-        out_specs=[pl.BlockSpec((2, lead, 1, 128 // lead, total), lambda h: (0, 0, h, 0, 0))]
-        + [pl.BlockSpec((lead, 1, 128 // lead, total), lambda h: (0, h, 0, 0))] * 2,
-        flops=4 * ROWS * D * total,
-        moved=2 * D * total,
+        out_specs=[pl.BlockSpec((lead, 1, 128 // lead, total), lambda h: (0, h, 0, 0))] * 4,
+        flops=0,
+        moved=0,
     )(*args)
 
 
 def y_weight_kernel(sets, base, where_, *refs):
-    u, u1, u0 = refs[-3:]
+    u2, u1b, u1, u0 = refs[-4:]
     h, h2 = where_[0], where_[1]
     at = 0
     for i in range(sets):
@@ -553,10 +552,10 @@
         to = slice(at, at + n)
         near = lambda place: dot(a[0, base + i, :, :256], d[place], TN) + dot(ar[1, base + i, :, :256], dr[place], TN)
         u0[:, to] = near(h).astype(bf)
-        u[0, :, to] = near(1 - h).astype(bf)
+        u2[:, to] = near(1 - h).astype(bf)
         r = (dot(a[0, base + i, :, 256:], d[h2], TN) + dot(ar[1, base + i, :, 256:], dr[h2], TN)).astype(bf)
         u1[:, to] = r[:256]
-        u[1, :, to] = r[256:]
+        u1b[:, to] = r[256:]
         at += n
 
 
@@ -566,24 +565,35 @@
     vm = pl.BlockSpec(memory_space=pltpu.VMEM)
     return call(
         partial(y_weight_kernel, len(sets), base),
-        (shape(2, 256, total, dtype=bf), shape(256, total, dtype=bf), shape(256, total, dtype=bf)),
+        (shape(256, total, dtype=bf),) * 4,
         in_specs=[pl.BlockSpec(memory_space=pltpu.SMEM)] + [vm] * len(args),
-        out_specs=(vm,) * 3,
-        flops=4 * ROWS * D * total,
-        moved=2 * D * total,
+        out_specs=(vm,) * 4,
+        flops=0,
+        moved=0,
     )(where_, *args)
+
+
+def exact(picks, v):
+    high = v.astype(bf)
+    rest = v - high.astype(f32)
+    mid = rest.astype(bf)
+    low = (rest - mid.astype(f32)).astype(bf)
+    return dot(picks, high) + dot(picks, mid) + dot(picks, low)
 
 
 def log_sigmoid(v):
     return jnp.minimum(v, 0.0) - jnp.log1p(jnp.exp(-jnp.abs(v)))
 
 
-def decays(logits):
+def cumulative(logits):
     ld = log_sigmoid(logits) / decay_norm
     r = lax.broadcasted_iota(jnp.int32, (ROWS, ROWS), 0)
     c = lax.broadcasted_iota(jnp.int32, (ROWS, ROWS), 1)
     lower = ((r >= c) & (r // SPAN == c // SPAN)).astype(f32)
-    cum = dot(lower, ld, NN, highest)
+    return exact(lower.astype(bf), ld)
+
+
+def decays(cum):
     blocks = [cum[i * SPAN : (i + 1) * SPAN] for i in range(4)]
     ends = [b[SPAN - 1 :] for b in blocks]
     return blocks, ends
@@ -618,15 +628,17 @@
     return jnp.concatenate([jnp.exp((ends[i] - blocks[i]) + run_sum(ends, i + 1, 4)) for i in range(4)], axis=0)
 
 
-def state_kernel(k, v, logits, segr, state):
-    blocks, ends = decays(logits[...])
+def state_kernel(k, v, logits, segr, state, cum_out):
+    cum = cumulative(logits[...])
+    cum_out[...] = cum
+    blocks, ends = decays(cum)
     segr = segr[...]
     tail_k = jnp.where(segr == segr[ROWS - 1 :], k[0].astype(f32) * tail_factors(blocks, ends), 0.0).astype(bf)
     state[0] = dot(tail_k, v[0], TN).astype(bf)
 
 
-def mix_kernel(q, k, v, logits, segr, segc, out, state_q):
-    blocks, ends = decays(logits[...])
+def mix_kernel(q, k, v, cum, segr, segc, out, state_q):
+    blocks, ends = decays(cum[...])
     kf = k[0].astype(f32)
     qf = q[0].astype(f32) * scale
     segr, segc = segr[...], segc[...]
@@ -650,10 +662,10 @@
 def end_state(qkvg, logits, segr):
     return call(
         state_kernel,
-        shape(HEADS, KD, VD, dtype=bf),
+        (shape(HEADS, KD, VD, dtype=bf), shape(ROWS, HEADS * KD)),
         grid=(HEADS,),
         in_specs=[head_cols(KD, 6), head_cols(VD, 1), pl.BlockSpec((ROWS, KD), lambda t: (0, t)), whole(ROWS, 1)],
-        out_specs=by_head(KD, VD),
+        out_specs=[by_head(KD, VD), pl.BlockSpec((ROWS, KD), lambda t: (0, t))],
         flops=HEADS * 20_000_000,
         moved=2_000_000,
     )(qkvg, qkvg, logits, segr)
@@ -762,10 +774,10 @@
 
 
 def mix_back_kernel(
-    do_in, q, k, v, logits, segr, segc, state_in, state_q_in, dq_out, dk_out, dv_out, net_out
+    do_in, q, k, v, cum, segr, segc, state_in, state_q_in, dq_out, dk_out, dv_out, net_out
 ):
     do = do_in[0]
-    blocks, ends = decays(logits[...])
+    blocks, ends = decays(cum[...])
     kf = k[0].astype(f32)
     qf = q[0].astype(f32) * scale
     segr, segc = segr[...], segc[...]
@@ -830,9 +842,9 @@
     )(do, qkvg, qkvg, qkvg, logits, segr, segc, state, state_q)
 
 
-def decay_back_kernel(dk_in, dv_in, net, k, v, logits_in, segr, segc, d_state, dk_out, dv_out, d_logits):
+def decay_back_kernel(dk_in, dv_in, net, k, v, logits_in, cum, segr, segc, d_state, dk_out, dv_out, d_logits):
     logits = logits_in[...]
-    blocks, ends = decays(logits)
+    blocks, ends = decays(cum[...])
     segr, segc = segr[...], segc[...]
     kf = k[0].astype(f32)
     tail = jnp.where(segr == segr[ROWS - 1 :], tail_factors(blocks, ends), 0.0)
@@ -844,13 +856,13 @@
     r = lax.broadcasted_iota(jnp.int32, (ROWS, ROWS), 0)
     c = lax.broadcasted_iota(jnp.int32, (ROWS, ROWS), 1)
     same = segr == segc
-    after = jnp.where(same & (c >= r), 1.0, 0.0)
-    before = jnp.where(same & (c < r), 1.0, 0.0)
-    d_ld = dot(after, net[0], NN, highest) + dot(before, back * tail_k.astype(f32), NN, highest)
+    after = jnp.where(same & (c >= r), 1.0, 0.0).astype(bf)
+    before = jnp.where(same & (c < r), 1.0, 0.0).astype(bf)
+    d_ld = exact(after, net[0]) + exact(before, back * tail_k.astype(f32))
     d_logits[...] = d_ld * jax.nn.sigmoid(-logits) / decay_norm
 
 
-def decay_back(dk, dv, net, qkvg, logits, segr, segc, d_state):
+def decay_back(dk, dv, net, qkvg, logits, cum, segr, segc, d_state):
     return call(
         decay_back_kernel,
         (
@@ -866,6 +878,7 @@
             head_cols(KD, 6),
             head_cols(VD, 1),
             pl.BlockSpec((ROWS, KD), lambda t: (0, t)),
+            pl.BlockSpec((ROWS, KD), lambda t: (0, t)),
             whole(ROWS, 1),
             whole(1, ROWS),
             by_head(KD, VD),
@@ -873,7 +886,7 @@
         out_specs=[head_cols(KD), head_cols(VD), pl.BlockSpec((ROWS, KD), lambda t: (0, t))],
         flops=HEADS * 100_000_000,
         moved=4_000_000,
-    )(dk, dv, net, qkvg, qkvg, logits, segr, segc, d_state)
+    )(dk, dv, net, qkvg, qkvg, logits, cum, segr, segc, d_state)
 
 
 def one_hot(places):
@@ -954,8 +967,9 @@
     for layer in range(LAYERS):
         w, at_qkvg, at_out = attn_w[layer]
         qkvg, latent, logits = proj(hn, downs[layer], low_up[layer], decay_bias[layer][None], (w[0], first_far) if layer == 0 else w, at_qkvg, 0 if layer == 0 else at_qkvg)
-        state = lax.ppermute(end_state(qkvg, logits, segr), "yh", [(0, 1)])
-        local_mix, state_q = mix(qkvg, logits, segr, segc)
+        state, cum = end_state(qkvg, logits, segr)
+        state = lax.ppermute(state, "yh", [(0, 1)])
+        local_mix, state_q = mix(qkvg, cum, segr, segc)
         mixed, rows, x_mid, hm = out_rows(
             local_mix, state_q, state, qkvg, group_gain[layer][None], x, gains_mid[layer : layer + 1], w, at_out
         )
@@ -969,19 +983,20 @@
             feed_w[1] = ((gathered_late, swap(gathered_late)), 0)
         if last:
             acted, d_pre, output, *back = ffn_both(hm, x_mid, order, g, gains_mid[layer : layer + 1], *feed_w[layer])
-            saved.append((x, hn, qkvg, latent, logits, state, state_q, mixed, rows, x_mid, hm, None, acted))
+            saved.append((x, hn, qkvg, latent, (logits, cum), state, state_q, mixed, rows, x_mid, hm, None, acted))
         else:
             pre, acted, x_next, hn_next = ffn(hm, x_mid, gains_in[layer + 1 : layer + 2], *feed_w[layer])
-            saved.append((x, hn, qkvg, latent, logits, state, state_q, mixed, rows, x_mid, hm, pre, acted))
+            saved.append((x, hn, qkvg, latent, (logits, cum), state, state_q, mixed, rows, x_mid, hm, pre, acted))
             x, hn = x_next, hn_next
 
     def rings(u):
-        return [ring(v[0].reshape(2, 16, 16, -1), a) for v, a in zip(u, "xzy")]
+        return [ring(sixteens(v[0]), a) for v, a in zip(u, "xzy")]
 
     def second_terms(u, r):
-        return add_each(*([(v[1], (w, 0))] for v, w in zip(u, r)))
-
-    def second_rings(t):
+        return add_each(*([(v[2], w)] for v, w in zip(u, r)))
+
+    def second_rings(t, moved):
+        t = t[0], after(t[1], moved), t[2]
         return [ring(sixteens(v), a) for v, a in zip(t, "xzy")]
 
     def small_grads(grad_in, grad_mid, hn, d_latent, latent, d_logits, d_gain):
@@ -1004,7 +1019,7 @@
     then = Order()
     small = [None] * LAYERS
     for layer in reversed(range(LAYERS)):
-        x, hn, qkvg, latent, logits, state, state_q, mixed, rows, x_mid, hm, pre, acted = saved[layer]
+        x, hn, qkvg, latent, (logits, cum), state, state_q, mixed, rows, x_mid, hm, pre, acted = saved[layer]
         bottom = layer == 0
         w, at_qkvg, at_out = attn_w[layer]
         if bottom:
@@ -1018,8 +1033,8 @@
         else:
             t = then(own_weight, hm, swap(hm), d_pre, d_pre_far, gb, swap(gb), acted, swap(acted))
             top = lax.psum_scatter(t.reshape(64, 16, 3 * FF), CHIPS, scatter_dimension=0, tiled=False)
-        d_q, d_k, d_v, net = then(mix_back, do, qkvg, logits, segr, segc, state, state_q)
-        d_k, d_v, d_logits = then(decay_back, d_k, d_v, net, qkvg, logits, segr, segc, d_state)
+        d_q, d_k, d_v, net = then(mix_back, do, qkvg, cum, segr, segc, state, state_q)
+        d_k, d_v, d_logits = then(decay_back, d_k, d_v, net, qkvg, logits, cum, segr, segc, d_state)
         d = jnp.concatenate([d_q, d_v, d_k, d_g], axis=2)
         d_far = swap(d)
         if bottom:
@@ -1030,6 +1045,7 @@
                 then(lambda v: y_weight(where_, sel_b, 0, *v), ((rows_above, rows_far[1]), (acted, acted_far), (rows, rows_far[0]))),
             ]
             r = rings(u)
+            r_far = [ring(sixteens(v[1]), a, 1) for v, a in zip(u, "xzy")]
         else:
             d_above, d_above_far, gm_above, rows_above = d, d_far, gm, rows
         g, grad_in, d_latent = then(
@@ -1038,17 +1054,16 @@
         )
         small[layer] = (grad_in[0], grad_mid[0], hn, d_latent, latent, d_logits, d_gain)
         if bottom:
-            stacked, flat = flatten([small_grads(*after(v, u)) for v in small])
+            stacked, flat = flatten([small_grads(*after(v, r)) for v in small])
             flat = flat + swap(flat)
             flat = flat.astype(bf)
             moved = [shift(flat, "z", j) for j in (1, 2, 3)]
-            r_far = [swap(v) for v in r]
-            t1 = then(second_terms, u, after(r, flat, r_far))
-            r1 = second_rings(t1)
+            t1 = then(second_terms, u, after(r, flat))
+            r1 = second_rings(t1, moved)
     input_grad = g
 
-    parts = [[(u[i][2], r1[i], (r_far[i], 1))] for i in range(3)]
-    (whole_x,) = add_each([(after(u[0][2], moved), r1[0], (r_far[0], 1))])
+    parts = [[(u[i][3], r1[i], r_far[i])] for i in range(3)]
+    (whole_x,) = add_each(parts[0])
     flat = [flat] + moved
     got_x = lax.all_to_all(sixteens(whole_x), ("z", "yh", "yl"), 0, 0, tiled=True)
     parts = split_sums(after(me[:2], whole_x), 64, parts[1:], flat, 0)

time: 578 us -> 571 us (0.988)
  Pallas kernels: 193 us -> 176 us
  local copies, waits for them, and re-layouts: 72.7 us -> 80.5 us
    ppermute x6 -> x9, waiting for transfers between devices: 21.9 us -> 47.4 us  [ring(): return lax.ppermute(a, names, pairs)]
    ppermute x12, waiting for transfers between devices: 43.6 us -> 27.5 us  [shift(): return lax.ppermute(a, axis, [(i, (i + step) % 4) for i in range(4)])]
    unnamed x283 -> x305, local copies, waits for them, and re-layouts: 58.5 us -> 65.7 us
    ppermute x19 -> x16, waiting for transfers between devices: 41.3 us -> 34.2 us  [swap(): return lax.ppermute(a, 'c', [(0, 1), (1, 0)])]
  transfers between devices with their start and end apart: 48 -> 48, of which waited for: 26 -> 27; matrix products, arithmetic and copies ran while one was open for 4% -> 5% of each run, Pallas kernels for 29% -> 26%
where the time goes in v4:
time: 571 us; the launch traced here: 560 us
  waiting for transfers between devices  223 us (39%)
  Pallas kernels  176 us (31%)
  local copies, waits for them, and re-layouts  80.5 us (14%)
  starting transfers between devices  49.7 us (9%)
  between operations  15.9 us (3%)
  other arithmetic  13.4 us (2%)
    all_gather x2, waiting for transfers between devices, chip_gather(): lax.all_gather(s, CHIPS, axis=0, tiled=True).reshape(2, 512, s.shape[1])  91.7 us
    unnamed x305, local copies, waits for them, and re-layouts  65.7 us
    ppermute x9, waiting for transfers between devices, ring(): return lax.ppermute(a, names, pairs)  47.4 us
    ppermute x16, waiting for transfers between devices, swap(): return lax.ppermute(a, 'c', [(0, 1), (1, 0)])  34.2 us
    ppermute x12, waiting for transfers between devices, shift(): return lax.ppermute(a, axis, [(i, (i + step) % 4) for i in range(4)])  27.5 us
    pallas_call x1, Pallas kernels, ffn_both(): call(ffn_both_kernel, (shape(2, ROWS, FF, dtype=bf), shape(2, ROWS, 2 * F...  19.1 us
    pallas_call x2, Pallas kernels, attn_back(): call(partial(attn_back_kernel, first), (shape(ROWS, D), shape(1, D), shap...  17.5 us
    pallas_call x2, Pallas kernels, x_weight(): call(partial(x_weight_kernel, len(sets), lead), (shape(*dims, dtype=bf),)...  15.1 us
  transfers between devices with their start and end apart: 48, of which 27 were waited for; matrix products, arithmetic and copies ran while one was open for 5% of the time, Pallas kernels for 26%

profile of v4, /device:TPU:0, one launch (start us, length us, event | category | flops | bytes accessed | tf_op | source)
XLA Modules:
  0.0 560.1 jit_solution(8936255022794894855)
XLA Ops:
  34.0 91.7 %all-gather.3.cloned.1.call-done = bf16[1024,8448]{1,0:T(8,128)(2,1)} async-done(((bf16[16,8448]{1,0:T(8,128)(2,1)}), bf16[1024,8448]{1,0:T(8,128)(2,1)}) %all-gather.3.cloned.1.call-update) | async-done | bytes 17301520 | tf_op jit(solution)/shard_map/all_gather | solution.py:76
  128.0 5.6 %collective-permute-done.wt = bf16[2,512,1536]{2,1,0:T(8,128)(2,1)S(1)} collective-permute-done((bf16[2,512,1536]{2,1,0:T(8,128)(2,1)S(1)}, bf16[2,512,1536]{2,1,0:T(8,128)(2,1)S(1)}, u32[]{:S(2)}, u32[]{:S(2)}) %collective-permute-start) | collective-permute-done | bytes 3145760 | tf_op jit(solution)/shard_map/ppermute | solution.py:52
  147.0 5.1 collective-permute-start.1
  168.1 11.0 %shard_map.311 = (bf16[2,256,2816]{2,1,0:T(8,128)(2,1)}, bf16[2,256,1408]{2,1,0:T(8,128)(2,1)}, f32[256,1024]{1,0:T(8,128)S(1)}, bf16[256,1024]{1,0:T(8,128)(2,1)S(1)}) custom-call(bf16[256,1024]{1,0:T(8,128)(2,1)S(1)} %get-tuple-element.199.hm.refs_1_, f32[256,1024]{1,0:T(8,128)S(1)} %get-tuple-element.200.x, f32[1,1024]{1,0:T(1,128)S(1)} %get-tuple-element.466.gain, ...), custom_call_target="tpu_custom_call" | custom-call | flops 4429185024 | bytes 17301504 | tf_op jit(solution)/shard_map/pallas_call | solution.py:304
  180.0 6.7 %shard_map.316.refs_0_.refs_4_.refs_8_ = bf16[2,3,256,1024]{3,2,1,0:T(8,128)(2,1)} custom-call(bf16[256,1024]{1,0:T(8,128)(2,1)S(1)} %get-tuple-element.310.hn.refs_0_, bf16[256,1024]{1,0:T(8,128)(2,1)S(1)} %get-tuple-element.199.hm.refs_1_, bf16[256,1024]{1,0:T(8,128)(2,1)S(1)} %get-tuple-element.308.hn.refs_2_, bf16[2,1024,1024]{2,1,0:T(8,128)(2,1)} %fusion.refs_3_), custom_call_target="tpu_custom_call" | custom-call | flops 500000000 | bytes 8000000 | tf_op jit(solution)/shard_map/pallas_call | solution.py:478
  206.5 8.2 %collective-permute-done.3.state.state_in = bf16[4,128,256]{2,1,0:T(8,128)(2,1)S(1)} collective-permute-done((bf16[4,128,256]{2,1,0:T(8,128)(2,1)S(1)}, bf16[4,128,256]{2,1,0:T(8,128)(2,1)S(1)}, u32[]{:S(2)}, u32[]{:S(2)}) %collective-permute-start.3) | collective-permute-done | bytes 262176 | tf_op jit(solution)/shard_map/ppermute | solution.py:971
  225.6 13.5 %collective-permute-done.8.wt = bf16[2,512,4224]{2,1,0:T(8,128)(2,1)S(1)} collective-permute-done((bf16[2,512,4224]{2,1,0:T(8,128)(2,1)}, bf16[2,512,4224]{2,1,0:T(8,128)(2,1)S(1)}, u32[]{:S(2)}, u32[]{:S(2)}) %collective-permute-start.8) | collective-permute-done | bytes 8650784 | tf_op jit(solution)/shard_map/ppermute | solution.py:52
  246.0 19.1 %shard_map.317 = (bf16[2,256,1408]{2,1,0:T(8,128)(2,1)S(1)}, bf16[2,256,2816]{2,1,0:T(8,128)(2,1)}, f32[256,1024]{1,0:T(8,128)}, bf16[256,1024]{1,0:T(8,128)(2,1...) custom-call(bf16[256,1024]{1,0:T(8,128)(2,1)S(1)} %copy-done.67, ...), custom_call_target="tpu_custom_call" | custom-call | flops 8858370048 | bytes 17301504 | tf_op jit(solution)/shard_map/pallas_call | solution.py:359
  275.0 8.9 %shard_map.319 = bf16[2,512,4224]{2,1,0:T(8,128)(2,1)} custom-call(bf16[256,1024]{1,0:T(8,128)(2,1)S(1)} %copy-done.68, bf16[256,1024]{1,0:T(8,128)(2,1)S(1)} %collective-permute-done.9.ar, bf16[256,1024]{1,0:T(8,128)(2,1)S(1)} %get-tuple-element.225.b, bf16[256,1024]{1,0:T(8,128)(2,1)S(1)} %collective-permute-done.10.br, ...), custom_call_target="tpu_custom_call" | custom-call | flops 500000000 | bytes 8000000 | tf_op jit(solution)/shard_map/pallas_call | solution.py:497
  302.0 7.4 %shard_map.322 = (f32[256,1024]{1,0:T(8,128)S(1)}, f32[1,1024]{1,0:T(1,128)S(1)}, f32[256,16]{1,0:T(8,128)S(1)}) custom-call(bf16[2,256,1536]{2,1,0:T(8,128)(2,1)S(1)} %constant_dynamic-update-slice_fusion.20.d.refs_2_, f32[256,512]{1,0:T(8,128)S(1)} %get-tuple-element.315.d_logits, f32[256,1024]{1,0:T(8,128)S(1)} %copy-done.18, ...), custom_call_target="tpu_custom_call" | custom-call | flops 1610612736 | bytes 6291456 | tf_op jit(solution)/shard_map/pallas_call | solution.py:454
  310.0 11.7 %shard_map.323 = (bf16[2,256,2816]{2,1,0:T(8,128)(2,1)}, bf16[256,1024]{1,0:T(8,128)(2,1)S(1)}, f32[256,1024]{1,0:T(8,128)S(1)}, bf16[256,1024]{1,0:T(8,128)(2,1)S(1)}, f32[1,1024]{1,0:T(1,128)S(1)}) custom-call(f32[256,1024]{1,0:T(8,128)S(1)} %get-tuple-element.239.g, f32[256,1024]{1,0:T(8,128)S(1)} %copy-done.15, ...), custom_call_target="tpu_custom_call" | custom-call | flops 4429185024 | bytes 17301504 | tf_op jit(solution)/shard_map/pallas_call | solution.py:416
  333.7 5.1 collective-permute-done.14.refs_1_
  353.6 7.4 %shard_map.328 = (bf16[4,2,32,2944]{3,2,1,0:T(8,128)(2,1)}, bf16[4,2,32,2944]{3,2,1,0:T(8,128)(2,1)S(1)}, bf16[4,2,32,2944]{3,2,1,0:T(8,128)(2,1)S(1)}, bf16[4,2,32,2944]{3,2,1,0:T(8,128)(2,1)S(1)}) custom-call(bf16[2,3,256,1024]{3,2,1,0:T(8,128)(2,1)} %shard_map.316.refs_0_.refs_4_.refs_8_, ...), custom_call_target="tpu_custom_call" | custom-call | tf_op jit(solution)/shard_map/pallas_call | solution.py:533
  363.5 7.6 %shard_map.329 = (bf16[1,2,128,2944]{3,2,1,0:T(8,128)(2,1)}, bf16[1,2,128,2944]{3,2,1,0:T(8,128)(2,1)}, bf16[1,2,128,2944]{3,2,1,0:T(8,128)(2,1)S(1)}, bf16[1,2,128,2944]{3,2,1,0:T(8,128)(2,1)S(1)}) custom-call(bf16[2,3,256,1024]{3,2,1,0:T(8,128)(2,1)} %shard_map.316.refs_0_.refs_4_.refs_8_, ...), custom_call_target="tpu_custom_call" | custom-call | tf_op jit(solution)/shard_map/pallas_call | solution.py:533
  377.0 7.4 %shard_map.330 = (bf16[256,2432]{1,0:T(8,128)(2,1)S(1)}, bf16[256,2432]{1,0:T(8,128)(2,1)}, bf16[256,2432]{1,0:T(8,128)(2,1)S(1)}, bf16[256,2432]{1,0:T(8,128)(2,1)}) custom-call(s32[2]{0:T(128)S(1)} %copy-done.114, bf16[2,3,256,768]{3,2,1,0:T(8,128)(2,1)} %copy-done.8, bf16[2,3,256,768]{3,2,1,0:T(8,128)(2,1)} %collective-permute-done.14.refs_1_, ...), custom_call_target="tpu_custom_call" | custom-call | tf_op jit(solution)/shard_map/pallas_call | solution.py:566
  385.3 10.2 %shard_map.331 = (f32[256,1024]{1,0:T(8,128)}, f32[1,1024]{1,0:T(1,128)S(1)}, f32[256,16]{1,0:T(8,128)S(1)}) custom-call(bf16[2,256,1536]{2,1,0:T(8,128)(2,1)S(1)} %copy-done.7, f32[256,512]{1,0:T(8,128)S(1)} %get-tuple-element.313.d_logits, f32[256,1024]{1,0:T(8,128)S(1)} %copy-done.13, f32[1,1024]{1,0:T(1,128)S(1)} %copy-done.102, ...), custom_call_target="tpu_custom_call" | custom-call | tf_op jit(solution)/shard_map/pallas_call | solution.py:454
  396.1 9.0 %collective-permute-done.21 = bf16[16,16,2432]{2,1,0:T(8,128)(2,1)S(1)} collective-permute-done((bf16[16,16,2432]{2,1,0:T(8,128)(2,1)S(1)}, bf16[16,16,2432]{2,1,0:T(8,128)(2,1)S(1)}, u32[]{:S(2)}, u32[]{:S(2)}) %collective-permute-start.21) | collective-permute-done | bytes 1245216 | tf_op jit(solution)/shard_map/ppermute | solution.py:65
  414.7 5.2 shard_map.332
  426.1 5.3 collective-permute-done.25.refs_1_
  438.6 16.0 %collective-permute-done.23 = bf16[16,16,2944]{2,1,0:T(8,128)(2,1)S(1)} collective-permute-done((bf16[16,16,2944]{2,1,0:T(8,128)(2,1)S(1)}, bf16[16,16,2944]{2,1,0:T(8,128)(2,1)S(1)}, u32[]{:S(2)}, u32[]{:S(2)}) %collective-permute-start.23) | collective-permute-done | bytes 1507360 | tf_op jit(solution)/shard_map/ppermute | solution.py:65
  461.0 22.4 %collective-permute-done.30 = bf16[16,16,2432]{2,1,0:T(8,128)(2,1)} collective-permute-done((bf16[16,16,2432]{2,1,0:T(8,128)(2,1)}, bf16[16,16,2432]{2,1,0:T(8,128)(2,1)}, u32[]{:S(2)}, u32[]{:S(2)}) %collective-permute-start.30) | collective-permute-done | bytes 1245216 | tf_op jit(solution)/shard_map/ppermute | solution.py:65
  486.3 5.6 shard_map.334
  499.4 5.4 collective-permute-done.35.refs_9_
  513.0 8.6 %collective-permute-done.33.refs_2_.refs_6_ = bf16[96,2944]{1,0:T(8,128)(2,1)S(1)} collective-permute-done((bf16[96,2944]{1,0:T(8,128)(2,1)S(1)}, bf16[96,2944]{1,0:T(8,128)(2,1)S(1)}, u32[]{:S(2)}, u32[]{:S(2)}) %collective-permute-start.33) | collective-permute-done | bytes 565280 | tf_op jit(solution)/shard_map/ppermute | solution.py:71
  (514 shorter events, 240.2 us)
Async XLA Ops:
  7.2 118.5 %all-gather.3.cloned.1.call-start = ((), (), s32[]{:S(2)}) async-start(), calls=%async_computation.2 | async-start | bytes 17571840 | tf_op jit(solution)/shard_map/all_gather | solution.py:76
  17.5 207.6 %all-gather.5.cloned.1.call-start = ((), (), s32[]{:S(2)}) async-start(), calls=%async_computation.3 | async-start | bytes 8785920 | tf_op jit(solution)/shard_map/all_gather | solution.py:76
  135.2 26.2 %collective-permute-start.2 = (bf16[2,512,8448]{2,1,0:T(8,128)(2,1)}, bf16[2,512,8448]{2,1,0:T(8,128)(2,1)}, u32[]{:S(2)}, u32[]{:S(2)}) collective-permute-start(bf16[2,512,8448]{2,1,0:T(8,128)(2,1)} %bitcast.157), channel_id=1, source_target_pairs={{0,2},{2,0},{1,3},{3,1},{4,6},{6,4},{5,7},{7,5},{8,10},{10,8},{9,1... | collective-permute-start | bytes 51904520 | tf_op jit(solution)/shard_map/ppermute | solution.py:52
  136.1 409.2 %reduce-scatter.2.cloned.1.call-start = ((), (), s32[]{:S(2)}) async-start(), calls=%async_computation.4 | async-start | bytes 8785920 | tf_op jit(solution)/shard_map/reduce_scatter | solution.py:1035
  186.7 38.3 %collective-permute-start.4 = (bf16[2,3,256,1024]{3,2,1,0:T(8,128)(2,1)}, bf16[2,3,256,1024]{3,2,1,0:T(8,128)(2,1)}, u32[]{:S(2)}, u32[]{:S(2)}) collective-permute-start(bf16[2,3,256,1024]{3,2,1,0:T(8,128)(2,1)} %shard_map.316.refs_0_.refs_4_.refs_8_), channel_id=1, source_target_pairs={{0,2},{2,0},{1,3},{3,1},{4,6},{6,4},{5,7},{7,5},{8,10},{10,8},{9,1... | collective-permute-start | bytes 9437192 | tf_op jit(solution)/shard_map/ppermute | solution.py:52
  186.8 38.2 %collective-permute-start.7 = (bf16[2,256,1408]{2,1,0:T(8,128)(2,1)}, bf16[2,256,1408]{2,1,0:T(8,128)(2,1)}, u32[]{:S(2)}, u32[]{:S(2)}) collective-permute-start(bf16[2,256,1408]{2,1,0:T(8,128)(2,1)} %get-tuple-element.286.refs_4_), channel_id=1, source_target_pairs={{0,2},{2,0},{1,3},{3,1},{4,6},{6,4},{5,7},{7,5},{8,10},{10,8},{9,1... | collective-permute-start | bytes 4325384 | tf_op jit(solution)/shard_map/ppermute | solution.py:52
  197.8 16.9 %collective-permute-start.3 = (bf16[4,128,256]{2,1,0:T(8,128)(2,1)S(1)}, bf16[4,128,256]{2,1,0:T(8,128)(2,1)S(1)}, u32[]{:S(2)}, u32[]{:S(2)}) collective-permute-start(bf16[4,128,256]{2,1,0:T(8,128)(2,1)S(1)} %get-tuple-element.207), channel_id=1, source_target_pairs={{0,1},{2,3},{4,5},{6,7},{8,9},{10,11},{12,13},{14,15},{16,17},{18,... | collective-permute-start | bytes 786440 | tf_op jit(solution)/shard_map/ppermute | solution.py:971
  202.8 20.3 %collective-permute-start.5 = (bf16[2,256,512]{2,1,0:T(8,128)(2,1)S(1)}, bf16[2,256,512]{2,1,0:T(8,128)(2,1)S(1)}, u32[]{:S(2)}, u32[]{:S(2)}) collective-permute-start(bf16[2,256,512]{2,1,0:T(8,128)(2,1)S(1)} %copy-done.58), channel_id=1, source_target_pairs={{0,2},{2,0},{1,3},{3,1},{4,6},{6,4},{5,7},{7,5},{8,10},{10,8},{9,1... | collective-permute-start | bytes 1572872 | tf_op jit(solution)/shard_map/ppermute | solution.py:52
  331.7 17.4 %collective-permute-start.17 = (bf16[2,256,2816]{2,1,0:T(8,128)(2,1)}, bf16[2,256,2816]{2,1,0:T(8,128)(2,1)}, u32[]{:S(2)}, u32[]{:S(2)}) collective-permute-start(bf16[2,256,2816]{2,1,0:T(8,128)(2,1)} %get-tuple-element.276.refs_6_), channel_id=1, source_target_pairs={{0,2},{2,0},{1,3},{3,1},{4,6},{6,4},{5,7},{7,5},{8,10},{10,8},{9,1... | collective-permute-start | bytes 8650760 | tf_op jit(solution)/shard_map/ppermute | solution.py:52
  333.5 15.5 %collective-permute-start.16 = (bf16[2,256,1536]{2,1,0:T(8,128)(2,1)S(1)}, bf16[2,256,1536]{2,1,0:T(8,128)(2,1)S(1)}, u32[]{:S(2)}, u32[]{:S(2)}) collective-permute-start(bf16[2,256,1536]{2,1,0:T(8,128)(2,1)S(1)} %constant_dynamic-update-slice_fusion.20.d.refs_2_), channel_id=1, source_target_pairs={{0,2},{2,0},{1,3},{3,1},{4,6},{6,4},{5,7},{7,5},{8,10},{10,8},{9,1... | collective-permute-start | bytes 4718600 | tf_op jit(solution)/shard_map/ppermute | solution.py:52
  373.4 32.7 %collective-permute-start.20 = (bf16[16,16,2944]{2,1,0:T(8,128)(2,1)}, bf16[16,16,2944]{2,1,0:T(8,128)(2,1)}, u32[]{:S(2)}, u32[]{:S(2)}) collective-permute-start(bf16[16,16,2944]{2,1,0:T(8,128)(2,1)} %bitcast.41), channel_id=1, source_target_pairs={{0,4},{2,14},{4,8},{6,2},{8,12},{10,6},{12,0},{14,10},{1,5},{3,15}... | collective-permute-start | bytes 4521992 | tf_op jit(solution)/shard_map/ppermute | solution.py:65
  374.9 31.2 %collective-permute-start.19 = (bf16[16,16,2944]{2,1,0:T(8,128)(2,1)}, bf16[16,16,2944]{2,1,0:T(8,128)(2,1)}, u32[]{:S(2)}, u32[]{:S(2)}) collective-permute-start(bf16[16,16,2944]{2,1,0:T(8,128)(2,1)} %bitcast.40), channel_id=1, source_target_pairs={{0,16},{2,50},{16,32},{18,2},{32,48},{34,18},{48,0},{50,34},{1,17}... | collective-permute-start | bytes 4521992 | tf_op jit(solution)/shard_map/ppermute | solution.py:65
  384.4 20.7 %collective-permute-start.21 = (bf16[16,16,2432]{2,1,0:T(8,128)(2,1)S(1)}, bf16[16,16,2432]{2,1,0:T(8,128)(2,1)S(1)}, u32[]{:S(2)}, u32[]{:S(2)}) collective-permute-start(bf16[16,16,2432]{2,1,0:T(8,128)(2,1)S(1)} %bitcast.155), channel_id=1, source_target_pairs={{0,64},{2,67},{64,1},{66,2},{1,65},{3,66},{65,0},{67,3},{4,68},{6,... | collective-permute-start | bytes 3735560 | tf_op jit(solution)/shard_map/ppermute | solution.py:65
  413.0 25.4 %collective-permute-start.24 = (bf16[16,16,2944]{2,1,0:T(8,128)(2,1)}, bf16[16,16,2944]{2,1,0:T(8,128)(2,1)S(1)}, u32[]{:S(2)}, u32[]{:S(2)}) collective-permute-start(bf16[16,16,2944]{2,1,0:T(8,128)(2,1)} %bitcast.153), channel_id=1, source_target_pairs={{0,18},{2,48},{16,34},{18,0},{32,50},{34,16},{48,2},{50,32},{1,19}... | collective-permute-start | bytes 4521992 | tf_op jit(solution)/shard_map/ppermute | solution.py:65
  419.9 34.7 %collective-permute-start.23 = (bf16[16,16,2944]{2,1,0:T(8,128)(2,1)S(1)}, bf16[16,16,2944]{2,1,0:T(8,128)(2,1)S(1)}, u32[]{:S(2)}, u32[]{:S(2)}) collective-permute-start(bf16[16,16,2944]{2,1,0:T(8,128)(2,1)S(1)} %bitcast.154), channel_id=1, source_target_pairs={{0,16},{2,50},{16,32},{18,2},{32,48},{34,18},{48,0},{50,34},{1,17}... | collective-permute-start | bytes 4521992 | tf_op jit(solution)/shard_map/ppermute | solution.py:65
  432.1 29.0 %collective-permute-start.29 = (bf16[16,16,2944]{2,1,0:T(8,128)(2,1)}, bf16[16,16,2944]{2,1,0:T(8,128)(2,1)}, u32[]{:S(2)}, u32[]{:S(2)}) collective-permute-start(bf16[16,16,2944]{2,1,0:T(8,128)(2,1)} %bitcast.72), channel_id=1, source_target_pairs={{0,6},{2,12},{4,10},{6,0},{8,14},{10,4},{12,2},{14,8},{1,7},{3,13}... | collective-permute-start | bytes 4521992 | tf_op jit(solution)/shard_map/ppermute | solution.py:65
  436.6 46.9 %collective-permute-start.28 = (bf16[16,16,2944]{2,1,0:T(8,128)(2,1)}, bf16[16,16,2944]{2,1,0:T(8,128)(2,1)}, u32[]{:S(2)}, u32[]{:S(2)}) collective-permute-start(bf16[16,16,2944]{2,1,0:T(8,128)(2,1)} %bitcast.180), channel_id=1, source_target_pairs={{0,4},{2,14},{4,8},{6,2},{8,12},{10,6},{12,0},{14,10},{1,5},{3,15}... | collective-permute-start | bytes 4521992 | tf_op jit(solution)/shard_map/ppermute | solution.py:65
  438.4 22.7 %collective-permute-start.31 = (bf16[16,16,2432]{2,1,0:T(8,128)(2,1)}, bf16[16,16,2432]{2,1,0:T(8,128)(2,1)}, u32[]{:S(2)}, u32[]{:S(2)}) collective-permute-start(bf16[16,16,2432]{2,1,0:T(8,128)(2,1)} %bitcast.76), channel_id=1, source_target_pairs={{0,66},{2,65},{64,3},{66,0},{1,67},{3,64},{65,2},{67,1},{4,70},{6,... | collective-permute-start | bytes 3735560 | tf_op jit(solution)/shard_map/ppermute | solution.py:65
  438.4 45.1 %collective-permute-start.30 = (bf16[16,16,2432]{2,1,0:T(8,128)(2,1)}, bf16[16,16,2432]{2,1,0:T(8,128)(2,1)}, u32[]{:S(2)}, u32[]{:S(2)}) collective-permute-start(bf16[16,16,2432]{2,1,0:T(8,128)(2,1)} %bitcast.74), channel_id=1, source_target_pairs={{0,64},{2,67},{64,1},{66,2},{1,65},{3,66},{65,0},{67,3},{4,68},{6,... | collective-permute-start | bytes 3735560 | tf_op jit(solution)/shard_map/ppermute | solution.py:65
  456.5 65.9 %all-to-all-start = ((bf16[16,16,2944]{2,1,0:T(8,128)(2,1)}), bf16[16,16,2944]{2,1,0:T(8,128)(2,1)S(1)}, u32[]{:S(2)}, u32[]{:S(2)}) async-start(bf16[16,16,2944]{2,1,0:T(8,128)(2,1)} %bitcast.67), calls=%async_computation | async-start | bytes 3014656 | tf_op jit(solution)/shard_map/all_to_all | solution.py:1068
  493.1 19.9 %collective-permute-start.32 = (bf16[96,2944]{1,0:T(8,128)(2,1)S(1)}, bf16[96,2944]{1,0:T(8,128)(2,1)S(1)}, u32[]{:S(2)}, u32[]{:S(2)}) collective-permute-start(bf16[96,2944]{1,0:T(8,128)(2,1)S(1)} %get-tuple-element.329), channel_id=1, source_target_pairs={{0,64},{64,1},{1,65},{65,0},{2,66},{66,3},{3,67},{67,2},{4,68},{68... | collective-permute-start | bytes 1695752 | tf_op jit(solution)/shard_map/ppermute | solution.py:71
  493.1 28.5 %collective-permute-start.33 = (bf16[96,2944]{1,0:T(8,128)(2,1)S(1)}, bf16[96,2944]{1,0:T(8,128)(2,1)S(1)}, u32[]{:S(2)}, u32[]{:S(2)}) collective-permute-start(bf16[96,2944]{1,0:T(8,128)(2,1)S(1)} %get-tuple-element.330), channel_id=1, source_target_pairs={{0,1},{64,65},{1,0},{65,64},{2,3},{66,67},{3,2},{67,66},{4,5},{68,... | collective-permute-start | bytes 1695752 | tf_op jit(solution)/shard_map/ppermute | solution.py:71
  496.7 24.9 %collective-permute-start.34 = (bf16[96,2944]{1,0:T(8,128)(2,1)S(1)}, bf16[96,2944]{1,0:T(8,128)(2,1)S(1)}, u32[]{:S(2)}, u32[]{:S(2)}) collective-permute-start(bf16[96,2944]{1,0:T(8,128)(2,1)S(1)} %get-tuple-element.331), channel_id=1, source_target_pairs={{0,65},{64,0},{1,64},{65,1},{2,67},{66,2},{3,66},{67,3},{4,69},{68... | collective-permute-start | bytes 1695752 | tf_op jit(solution)/shard_map/ppermute | solution.py:71
  529.9 15.3 %collective-permute-start.39 = (bf16[48,2944]{1,0:T(8,128)(2,1)S(1)}, bf16[48,2944]{1,0:T(8,128)(2,1)S(1)}, u32[]{:S(2)}, u32[]{:S(2)}) collective-permute-start(bf16[48,2944]{1,0:T(8,128)(2,1)S(1)} %get-tuple-element.346), channel_id=1, source_target_pairs={{0,32},{16,48},{32,0},{48,16},{1,33},{17,49},{33,1},{49,17},{2,34}... | collective-permute-start | bytes 847880 | tf_op jit(solution)/shard_map/ppermute | solution.py:72
  (160 other events, 1071.0 us)
Sparse Core Ops, SparseCore 0:
  17.6 108.0 all-gather.2
  136.2 85.0 all-gather.4
  284.0 250.0 reduce-scatter.1
